TPU v7x, 32 devices: a whole 2x2x4 slice. The times are simulated.
32 devices in a mesh: groups: 2 (over y), ep: 4 (over z), tp: 4 (over x, core).
Axes of the slice: x: 2, y: 2, z: 4, core: 2. Of those that a mesh axis runs over, the one named last changes fastest.
Arguments:
- resid: bfloat16 [256, 4096], P(('groups', 'ep'), 'tp'), parts along dimension 0, may hold values from -36 to 36
- query: bfloat16 [256, 4096], P(('groups', 'ep'), 'tp'), parts along dimension 0, may hold values from -4.5 to 4.5
- new_key: bfloat16 [256, 4096], P(('groups', 'ep'), 'tp'), parts along dimension 0, may hold values from -4.5 to 4.5
- new_value: bfloat16 [256, 4096], P(('groups', 'ep'), 'tp'), parts along dimension 0, may hold values from -4.5 to 4.5
- cache_keys: bfloat16 [256, 8, 4096], P(('groups', 'ep'), None, 'tp'), parts along dimension 0, may hold values from -4.5 to 4.5
- cache_values: bfloat16 [256, 8, 4096], P(('groups', 'ep'), None, 'tp'), parts along dimension 0, may hold values from -4.5 to 4.5
- cache_lengths: int32 [256], P(('groups', 'ep')), parts along dimension 0, may hold values from 2 to 8, as said below
- shallow_expert: int32 [256, 1], P(('groups', 'ep')), parts along dimension 0, may hold values from 0 to 3; in each aligned block of 32 rows (0 to 31, 32 to 63, ...) at most 12 rows name the same one
- shallow_gate: float32 [256], P(('groups', 'ep')), parts along dimension 0, may hold values from 0.2 to 1
- shallow_up: bfloat16 [4096, 32768], P('tp', 'ep'), may hold values from -0.09375 to 0.09375
- shallow_down: bfloat16 [32768, 4096], P('ep', 'tp'), may hold values from -0.0625 to 0.0625
- deep_expert: int32 [256, 1], P(('groups', 'ep')), parts along dimension 0, may hold values from 0 to 3; in each aligned block of 32 rows (0 to 31, 32 to 63, ...) at most 12 rows name the same one
- deep_gate: float32 [256], P(('groups', 'ep')), parts along dimension 0, may hold values from 0.2 to 1
- deep_up: bfloat16 [4096, 32768], P('tp', 'ep'), may hold values from -0.09375 to 0.09375
- deep_down: bfloat16 [32768, 4096], P('ep', 'tp'), may hold values from -0.0625 to 0.0625
Outputs:
- decoded: bfloat16 [256, 4096], P(('groups', 'ep'), 'tp'), parts along dimension 0
There are 2 independent parts, one for each index of `groups`. A program takes and returns all parts, laid end to end along the dimension named above; an argument that names none is the same for every part. Nothing has to cross between parts.
Inputs may be any that keep to these rules, and one draw needn't show every extreme that they name: `cache_lengths`: some row holds exactly 8 positions. `shallow_expert`: of the rows of one ep index at most 12 name one expert, and exactly 12 do for some expert on some ep index. `deep_expert`: of the rows of one ep index at most 12 name one expert, and exactly 12 do for some expert on some ep index.
All inputs are finite; a program needn't handle non-finite values.
Results may differ from a plain program's by a relative error of at most 0.006.
Values may be sent and summed in bfloat16 or wider, within the bound.
No kernel may reach another device: no remote copies, remote signals or barrier semaphores. Data moves between devices by JAX's collectives and lax.ppermute only.
A program may use at most 192 MiB of HBM per device.

v0:
```python
import math

import jax
import jax.numpy as jnp
from jax import lax
from jax.sharding import PartitionSpec as P

D = 4096
HD = 128
EXPERTS = 4
CAP = 12


epsilon = 1e-05


def attention(resid, query, new_key, new_value, cache_keys, cache_values, cache_lengths):
    row_count, feature_count = resid.shape
    heads_here = feature_count // HD
    depth = cache_keys.shape[1]
    queries = query.reshape(row_count, heads_here, HD)
    own_keys = new_key.reshape(row_count, heads_here, HD)
    own_values = new_value.reshape(row_count, heads_here, HD)
    past_keys = cache_keys.reshape(row_count, depth, heads_here, HD)
    past_values = cache_values.reshape(row_count, depth, heads_here, HD)
    factor = 1.0 / math.sqrt(HD)
    cached = (
        jnp.einsum("rhd,rjhd->rhj", queries, past_keys, preferred_element_type=jnp.float32) * factor
    )
    own_score = (
        jnp.einsum("rhd,rhd->rh", queries, own_keys, preferred_element_type=jnp.float32) * factor
    )
    valid = jnp.arange(depth)[None, None, :] < cache_lengths[:, None, None]
    masked = jnp.where(valid, cached, -1e30)
    highest = jnp.maximum(jnp.max(masked, axis=-1), own_score)
    cached_exp = jnp.where(valid, jnp.exp(masked - highest[..., None]), 0.0)
    own_exp = jnp.exp(own_score - highest)
    total = jnp.sum(cached_exp, axis=-1) + own_exp
    past_weights = (cached_exp / total[..., None]).astype(jnp.bfloat16)
    own_weight = (own_exp / total).astype(jnp.bfloat16)
    attended = jnp.einsum(
        "rhj,rjhd->rhd", past_weights, past_values, preferred_element_type=jnp.float32
    )
    attended = attended + own_weight.astype(jnp.float32)[..., None] * own_values.astype(jnp.float32)
    return (resid.astype(jnp.float32) + attended.reshape(row_count, feature_count)).astype(
        jnp.bfloat16
    )


def expert_layer(states, expert_ids, gates, up_weight, down_weight):
    row_count, feature_count = states.shape
    ep_count = lax.axis_size("ep")
    sharing = ep_count // EXPERTS
    mine = lax.axis_index("ep") // sharing
    wide = states.astype(jnp.float32)
    row_sum, row_square = lax.psum((jnp.sum(wide, axis=1), jnp.sum(wide * wide, axis=1)), "tp")
    center = row_sum / D
    spread = row_square / D - center * center
    normalized = ((wide - center[:, None]) * lax.rsqrt(spread + epsilon)[:, None]).astype(
        jnp.bfloat16
    )
    slots = CAP
    routed = expert_ids[:, 0]
    onehot = (routed[:, None] == jnp.arange(EXPERTS)[None, :]).astype(jnp.int32)
    earlier = jnp.cumsum(onehot, axis=0) - onehot
    rank_in = jnp.sum(earlier * onehot, axis=1)
    position = routed * slots + rank_in
    placing = (position[None, :] == jnp.arange(EXPERTS * slots)[:, None]).astype(jnp.bfloat16)
    compact = jnp.dot(placing, normalized, preferred_element_type=jnp.float32).astype(jnp.bfloat16)
    compact = compact.reshape(EXPERTS, slots, feature_count)
    chosen = lax.dynamic_index_in_dim(
        lax.all_gather(compact[None], "ep", axis=0, tiled=True), mine, axis=1, keepdims=False
    )
    pre = jnp.einsum("scd,df->scf", chosen, up_weight, preferred_element_type=jnp.float32)
    hidden_width = pre.shape[2]
    flat_pre = pre.reshape(ep_count * slots, hidden_width)
    summed = lax.psum(flat_pre, "tp")
    activated = jax.nn.gelu(summed, approximate=True).astype(jnp.bfloat16)
    partial_value = jnp.dot(activated, down_weight, preferred_element_type=jnp.float32)
    returned = lax.all_to_all(
        partial_value.reshape(ep_count, slots, feature_count),
        "ep",
        split_axis=0,
        concat_axis=0,
        tiled=True,
    )
    combined = jnp.sum(returned.reshape(EXPERTS, sharing, slots, feature_count), axis=1)
    combined = combined.reshape(EXPERTS * slots, feature_count)
    produced = jnp.take(combined, position, axis=0)
    return (wide + gates[:, None] * produced).astype(jnp.bfloat16)


def body(
    resid,
    query,
    new_key,
    new_value,
    cache_keys,
    cache_values,
    cache_lengths,
    shallow_expert,
    shallow_gate,
    shallow_up,
    shallow_down,
    deep_expert,
    deep_gate,
    deep_up,
    deep_down,
):
    shallow_in = attention(
        resid, query, new_key, new_value, cache_keys, cache_values, cache_lengths
    )
    shallow_out = expert_layer(shallow_in, shallow_expert, shallow_gate, shallow_up, shallow_down)
    return expert_layer(shallow_out, deep_expert, deep_gate, deep_up, deep_down)


def solution(mesh):
    return jax.shard_map(
        body,
        mesh=mesh,
        in_specs=(
            P(("groups", "ep"), "tp"),
            P(("groups", "ep"), "tp"),
            P(("groups", "ep"), "tp"),
            P(("groups", "ep"), "tp"),
            P(("groups", "ep"), None, "tp"),
            P(("groups", "ep"), None, "tp"),
            P(("groups", "ep")),
            P(("groups", "ep"), None),
            P(("groups", "ep")),
            P("tp", "ep"),
            P("ep", "tp"),
            P(("groups", "ep"), None),
            P(("groups", "ep")),
            P("tp", "ep"),
            P("ep", "tp"),
        ),
        out_specs=P(("groups", "ep"), "tp"),
        check_vma=False,
    )
```

profile of v0, /device:TPU:0, one launch (start us, length us, event | category | flops | bytes accessed | tf_op | source)
XLA Modules:
  0.0 219.5 jit_solution(9551205511076606880)
XLA Ops:
  6.6 1.0 reshape.134
  7.5 1.4 fusion.30
  9.1 0.7 iota_compare_fusion.6
  9.7 0.8 copy.33
  10.6 0.9 copy.32
  12.2 0.2 select_reduce_fusion.1
  12.4 0.4 fusion.28
  13.1 8.3 %all-reduce.1 = (f32[32]{0:T(128)S(1)}, f32[32]{0:T(128)S(1)}) all-reduce(f32[32]{0:T(128)S(1)} %get-tuple-element.9, f32[32]{0:T(128)S(1)} %get-tuple-element.8), channel_id=1, replica_groups=mesh['groups'=2,'ep'=4,'tp'=4] {'tp'}, use_global_device_ids=true, to_apply=%region_7.8 | all-reduce | flops 64 | bytes 512 | tf_op jit(solution)/shard_map/psum | solution.py:56
  21.4 0.2 convolution_convert_fusion.1
  21.8 14.6 %all_gather.6 = bf16[4,4,12,1024]{3,1,2,0:T(4,128)(2,1)S(1)} all-gather(bf16[1,4,12,1024]{3,1,2,0:T(4,128)(2,1)S(1)} %copy.19), channel_id=1, replica_groups=mesh['groups'=2,'ep'=4,'tp'=4] {'ep'}, dimensions={0}, use_global_device_ids=true | all-gather | bytes 491520 | tf_op jit(solution)/shard_map/all_gather | solution.py:72
  36.4 0.6 dynamic-slice_reduce_fusion.1
  37.0 9.9 %fusion.69 = f32[48,8192]{1,0:T(8,128)} fusion(bf16[48,1024]{1,0:T(8,128)(2,1)S(1)} %dot_general.35, bf16[1024,8192]{1,0:T(8,128)(2,1)} %param.26), kind=kOutput, calls=%fused_computation.110 | convolution fusion | flops 805306368 | bytes 18448384 | tf_op jit(solution)/shard_map/scd,df->scf/dot_general | solution.py:74
  47.0 0.6 copy-done.5
  47.9 43.1 %all-reduce.5.cloned.1.call-done = f32[48,8192]{1,0:T(8,128)} async-done(((f32[48,8192]{1,0:T(8,128)}), f32[48,8192]{1,0:T(8,128)}) %all-reduce.5.cloned.1.call-update) | async-done | bytes 1572880 | tf_op jit(solution)/shard_map/psum | solution.py:77
  91.0 9.2 %fusion.18 = f32[48,1024]{1,0:T(8,128)S(1)} fusion(bf16[8192,1024]{1,0:T(8,128)(2,1)} %param.27, f32[48,8192]{1,0:T(8,128)} %all-reduce.5.cloned.1.call-done), kind=kOutput, calls=%fused_computation.23 | convolution fusion | flops 808845312 | bytes 18546688 | tf_op jit(solution)/shard_map/dot_general | solution.py:79
  100.2 0.7 reshape.100
  100.9 4.6 %all-to-all-start = ((f32[4,12,1024]{2,1,0:T(8,128)}), f32[4,12,1024]{2,1,0:T(8,128)S(1)}, u32[]{:S(2)}, u32[]{:S(2)}) async-start(f32[4,12,1024]{2,1,0:T(8,128)} %reshape.100), calls=%async_computation | async-start | bytes 524288 | tf_op jit(solution)/shard_map/all_to_all | solution.py:80
  105.6 8.8 %all-to-all-done = f32[4,12,1024]{2,1,0:T(8,128)S(1)} async-done(((f32[4,12,1024]{2,1,0:T(8,128)}), f32[4,12,1024]{2,1,0:T(8,128)S(1)}, u32[]{:S(2)}, u32[]{:S(2)}) %all-to-all-start) | async-done | bytes 196640 | tf_op jit(solution)/shard_map/all_to_all | solution.py:80
  114.4 0.6 gather_fusion
  115.0 0.2 convert_reduce_fusion
  115.2 5.7 %all-reduce = (f32[32]{0:T(128)S(1)}, f32[32]{0:T(128)S(1)}) all-reduce(f32[32]{0:T(128)S(1)} %get-tuple-element.7, f32[32]{0:T(128)S(1)} %get-tuple-element.6), channel_id=1, replica_groups=mesh['groups'=2,'ep'=4,'tp'=4] {'tp'}, use_global_device_ids=true, to_apply=%region_14.16 | all-reduce | flops 64 | bytes 512 | tf_op jit(solution)/shard_map/psum | solution.py:56
  120.9 0.2 convolution_convert_fusion
  121.2 15.2 %all_gather.7 = bf16[4,4,12,1024]{3,1,2,0:T(4,128)(2,1)S(1)} all-gather(bf16[1,4,12,1024]{3,1,2,0:T(4,128)(2,1)S(1)} %copy.20), channel_id=1, replica_groups=mesh['groups'=2,'ep'=4,'tp'=4] {'ep'}, dimensions={0}, use_global_device_ids=true | all-gather | bytes 491520 | tf_op jit(solution)/shard_map/all_gather | solution.py:72
  136.4 0.6 dynamic-slice_reduce_fusion
  137.0 9.9 %fusion.70 = f32[48,8192]{1,0:T(8,128)} fusion(bf16[48,1024]{1,0:T(8,128)(2,1)S(1)} %dot_general.39, bf16[1024,8192]{1,0:T(8,128)(2,1)} %param.30), kind=kOutput, calls=%fused_computation.111 | convolution fusion | flops 805306368 | bytes 18448384 | tf_op jit(solution)/shard_map/scd,df->scf/dot_general | solution.py:74
  147.0 40.9 %all-reduce.7.cloned.1.call-done = f32[48,8192]{1,0:T(8,128)} async-done(((f32[48,8192]{1,0:T(8,128)}), f32[48,8192]{1,0:T(8,128)}) %all-reduce.7.cloned.1.call-update) | async-done | bytes 1572880 | tf_op jit(solution)/shard_map/psum | solution.py:77
  187.9 9.3 %fusion.16 = f32[48,1024]{1,0:T(8,128)S(1)} fusion(bf16[8192,1024]{1,0:T(8,128)(2,1)} %param.31, f32[48,8192]{1,0:T(8,128)} %all-reduce.7.cloned.1.call-done), kind=kOutput, calls=%fused_computation.22 | convolution fusion | flops 808845312 | bytes 18546688 | tf_op jit(solution)/shard_map/dot_general | solution.py:79
  197.2 0.7 reshape.102
  197.9 4.6 %all-to-all-start.1 = ((f32[4,12,1024]{2,1,0:T(8,128)}), f32[4,12,1024]{2,1,0:T(8,128)S(1)}, u32[]{:S(2)}, u32[]{:S(2)}) async-start(f32[4,12,1024]{2,1,0:T(8,128)} %reshape.102), calls=%async_computation.1 | async-start | bytes 524288 | tf_op jit(solution)/shard_map/all_to_all | solution.py:80
  202.5 8.8 %all-to-all-done.1 = f32[4,12,1024]{2,1,0:T(8,128)S(1)} async-done(((f32[4,12,1024]{2,1,0:T(8,128)}), f32[4,12,1024]{2,1,0:T(8,128)S(1)}, u32[]{:S(2)}, u32[]{:S(2)}) %all-to-all-start.1) | async-done | bytes 196640 | tf_op jit(solution)/shard_map/all_to_all | solution.py:80
  211.3 0.6 gather_fusion.1
  211.9 0.7 fusion.39
  (54 shorter events, 1.8 us)
Async XLA Ops:
  6.5 5.8 %copy-start = (bf16[32,8,1024]{2,1,0:T(8,128)(2,1)S(1)}, bf16[32,8,1024]{2,1,0:T(8,128)(2,1)}, u32[]{:S(2)}) copy-start(bf16[32,8,1024]{2,1,0:T(8,128)(2,1)} %param.22) | copy-start | bytes 1572868
  6.5 5.5 %copy-start.2 = (bf16[32,1024]{1,0:T(8,128)(2,1)S(1)}, bf16[32,1024]{1,0:T(8,128)(2,1)}, u32[]{:S(2)}) copy-start(bf16[32,1024]{1,0:T(8,128)(2,1)} %param.20) | copy-start | bytes 196612
  6.5 5.5 %copy-start.4 = (s32[32,1]{0,1:T(1,128)S(1)}, s32[32,1]{0,1:T(1,128)}, u32[]{:S(2)}) copy-start(s32[32,1]{0,1:T(1,128)} %param.24) | copy-start | bytes 388
  6.5 84.4 %all-reduce.5.cloned.1.call-start = ((), (), s32[]{:S(2)}) async-start(), calls=%async_computation.2 | async-start | bytes 3145728 | tf_op jit(solution)/shard_map/psum | solution.py:77
  9.0 4.0 %copy-start.3 = (bf16[32,1024]{1,0:T(8,128)(2,1)S(1)}, bf16[32,1024]{1,0:T(8,128)(2,1)}, u32[]{:S(2)}) copy-start(bf16[32,1024]{1,0:T(8,128)(2,1)} %param.17) | copy-start | bytes 196612
  46.9 0.7 copy-start.5
  100.2 14.8 %copy-start.6 = (f32[32]{0:T(128)S(1)}, f32[32]{0:T(128)}, u32[]{:S(2)}) copy-start(f32[32]{0:T(128)} %param.25) | copy-start | bytes 388
  100.9 13.4 %all-to-all-start = ((f32[4,12,1024]{2,1,0:T(8,128)}), f32[4,12,1024]{2,1,0:T(8,128)S(1)}, u32[]{:S(2)}, u32[]{:S(2)}) async-start(f32[4,12,1024]{2,1,0:T(8,128)} %reshape.100), calls=%async_computation | async-start | bytes 524288 | tf_op jit(solution)/shard_map/all_to_all | solution.py:80
  105.5 82.3 %all-reduce.7.cloned.1.call-start = ((), (), s32[]{:S(2)}) async-start(), calls=%async_computation.3 | async-start | bytes 3145728 | tf_op jit(solution)/shard_map/psum | solution.py:77
  187.9 24.8 %copy-start.1 = (bf16[32,8,1024]{2,1,0:T(8,128)(2,1)S(1)}, bf16[32,8,1024]{2,1,0:T(8,128)(2,1)}, u32[]{:S(2)}) copy-start(bf16[32,8,1024]{2,1,0:T(8,128)(2,1)} %param.22) | copy-start | bytes 1572868
  197.2 14.8 %copy-start.7 = (f32[32]{0:T(128)S(1)}, f32[32]{0:T(128)}, u32[]{:S(2)}) copy-start(f32[32]{0:T(128)} %param.29) | copy-start | bytes 388
  197.9 13.4 %all-to-all-start.1 = ((f32[4,12,1024]{2,1,0:T(8,128)}), f32[4,12,1024]{2,1,0:T(8,128)S(1)}, u32[]{:S(2)}, u32[]{:S(2)}) async-start(f32[4,12,1024]{2,1,0:T(8,128)} %reshape.102), calls=%async_computation.1 | async-start | bytes 524288 | tf_op jit(solution)/shard_map/all_to_all | solution.py:80
Sparse Core Ops, SparseCore 0:
  47.1 43.8 all-reduce.4
  147.1 40.7 all-reduce.6
where the time goes:
time: 220 us; the launch traced here: 219 us
  waiting for transfers between devices  102 us (46%)
  blocking collectives  43.8 us (20%)
  matrix products  40.7 us (19%)
  between operations  13.7 us (6%)
  starting transfers between devices  9.2 us (4%)
  local copies, waits for them, and re-layouts  7.89 us (4%)
  other arithmetic  2.72 us (1%)
    psum x2, waiting for transfers between devices, expert_layer(): summed = lax.psum(flat_pre, 'tp')  84 us
    all_gather x2, blocking collectives, expert_layer(): lax.all_gather(compact[None], 'ep', axis=0, tiled=True)  29.8 us
    dot_general x2, matrix products, expert_layer(): jnp.einsum('scd,df->scf', chosen, up_weight, preferred_element_type=jnp.f...  19.9 us
    dot_general x2, matrix products, expert_layer(): jnp.dot(activated, down_weight, preferred_element_type=jnp.float32)  18.5 us
    all_to_all x2, waiting for transfers between devices, expert_layer(): lax.all_to_all(partial_value.reshape(ep_count, slots, feature_count), 'ep...  17.5 us
    psum x2, blocking collectives, expert_layer(): lax.psum((jnp.sum(wide, axis=1), jnp.sum(wide * wide, axis=1)), 'tp')  14 us
    all_to_all x2, starting transfers between devices, expert_layer(): lax.all_to_all(partial_value.reshape(ep_count, slots, feature_count), 'ep...  9.2 us
  transfers between devices with their start and end apart: 4, of which 4 were waited for; matrix products, arithmetic and copies ran while one was open for 0% of the time, Pallas kernels for 0%

commit v1 on v0

--- a/solution.py
+++ b/solution.py
@@ -1,8 +1,11 @@
+import functools
 import math
 
 import jax
 import jax.numpy as jnp
 from jax import lax
+from jax.experimental import pallas as pl
+from jax.experimental.pallas import tpu as pltpu
 from jax.sharding import PartitionSpec as P
 
 D = 4096
@@ -90,7 +93,7 @@
     return (wide + gates[:, None] * produced).astype(jnp.bfloat16)
 
 
-def body(
+def general_body(
     resid,
     query,
     new_key,
@@ -114,9 +117,482 @@
     return expert_layer(shallow_out, deep_expert, deep_gate, deep_up, deep_down)
 
 
+SLOTS = EXPERTS * CAP
+PAD = 16
+TALL = 56
+META = 128
+MIB = 1 << 20
+F32 = jnp.float32
+BF16 = jnp.bfloat16
+
+
+def iota(shape, dim):
+    return lax.broadcasted_iota(jnp.int32, shape, dim)
+
+
+def to_column(row, count):
+    same = iota((count, count), 0) == iota((count, count), 1)
+    return jnp.sum(jnp.where(same, row, jnp.zeros_like(row)), axis=1, keepdims=True)
+
+
+def to_row(column, count):
+    same = iota((count, count), 0) == iota((count, count), 1)
+    return jnp.sum(jnp.where(same, column, jnp.zeros_like(column)), axis=0, keepdims=True)
+
+
+def ranks(id_row, id_column, count):
+    earlier = iota((count, count), 1) < iota((count, count), 0)
+    same = (id_row == id_column) & earlier
+    return jnp.sum(same.astype(jnp.int32), axis=1, keepdims=True)
+
+
+def split3(value):
+    high = value.astype(BF16).astype(F32)
+    middle = (value - high).astype(BF16).astype(F32)
+    low = (value - high - middle).astype(BF16).astype(F32)
+    return high, middle, low
+
+
+def dot(left, right):
+    return jnp.dot(left, right, preferred_element_type=F32)
+
+
+def params(mib):
+    return pltpu.CompilerParams(vmem_limit_bytes=mib * MIB)
+
+
+def cost(flops, moved):
+    return pl.CostEstimate(flops=flops, bytes_accessed=moved, transcendentals=0)
+
+
+VM = pl.BlockSpec(memory_space=pltpu.VMEM)
+SM = pl.BlockSpec(memory_space=pltpu.SMEM)
+
+
+def attend_kernel(
+    place_ref, resid_ref, query_ref, key_ref, value_ref, keys_ref, values_ref, length_ref,
+    shallow_ref, sgate_ref, deep_ref, dgate_ref, out0, out1, out2, out3,
+):
+    rows, features = resid_ref.shape
+    depth = keys_ref.shape[1]
+    flat = rows * depth
+    factor = 1.0 / math.sqrt(HD)
+    spread = (iota((features, META), 0) // HD == iota((features, META), 1)).astype(BF16)
+    gather = (iota((META, features), 1) // HD == iota((META, features), 0)).astype(BF16)
+
+    def head_sums(products):
+        high = products.astype(BF16)
+        low = (products - high.astype(F32)).astype(BF16)
+        return dot(high, spread) + dot(low, spread)
+
+    query = query_ref[...].astype(F32)
+    own = head_sums(query * key_ref[...].astype(F32)) * factor
+    products = query[:, None, :] * keys_ref[...].astype(F32)
+    cached = head_sums(products.reshape(flat, features)) * factor
+    repeated = iota((flat, rows), 0) // depth == iota((flat, rows), 1)
+    length = jnp.sum(jnp.where(repeated, length_ref[...], 0), axis=1, keepdims=True)
+    valid = (iota((flat, META), 0) % depth) < length
+    masked = jnp.where(valid, cached, -1e30).reshape(rows, depth, META)
+    highest = jnp.maximum(jnp.max(masked, axis=1), own)
+    past = jnp.exp(masked - highest[:, None, :])
+    past = jnp.where(valid, past.reshape(flat, META), 0.0).reshape(rows, depth, META)
+    own_exp = jnp.exp(own - highest)
+    total = jnp.sum(past, axis=1) + own_exp
+    weights = (past / total[:, None, :]).reshape(flat, META).astype(BF16)
+    own_weight = (own_exp / total).astype(BF16)
+    wide = dot(weights, gather).reshape(rows, depth, features)
+    attended = jnp.sum(wide * values_ref[...].astype(F32), axis=1)
+    attended = attended + dot(own_weight, gather) * value_ref[...].astype(F32)
+    states = (resid_ref[...].astype(F32) + attended).astype(BF16)
+
+    here = place_ref[1]
+    shallow = shallow_ref[...]
+    deep = deep_ref[...]
+    shallow_column = to_column(shallow, rows)
+    deep_column = to_column(deep, rows)
+    place = (shallow_column ^ here) * PAD + ranks(shallow, shallow_column, rows)
+    lane = iota((rows, META), 1)
+    notes = jnp.where(lane == 0, deep_column.astype(F32), 0.0)
+    notes = jnp.where(lane == 1, ranks(deep, deep_column, rows).astype(F32), notes)
+    for start, gate_ref in ((2, sgate_ref), (5, dgate_ref)):
+        for at, piece in enumerate(split3(to_column(gate_ref[...], rows))):
+            notes = jnp.where(lane == start + at, piece, notes)
+    notes = jnp.where(lane == 8, 1.0, notes)
+    full = jnp.concatenate([states, notes.astype(BF16)], axis=1)
+    choose = (iota((EXPERTS * PAD, rows), 0) == to_row(place, rows)).astype(BF16)
+    sent = dot(choose, full)
+    for at, out in enumerate((out0, out1, out2, out3)):
+        out[...] = sent[at * PAD : (at + 1) * PAD].astype(BF16)
+
+
+def attend(place, arrays):
+    rows, features = arrays[0].shape
+    shape = jax.ShapeDtypeStruct((PAD, features + META), BF16)
+    return pl.pallas_call(
+        attend_kernel,
+        in_specs=[SM] + [VM] * len(arrays),
+        out_specs=[VM] * 4,
+        out_shape=[shape] * 4,
+        compiler_params=params(24),
+        name="attend",
+    )(place, *arrays)
+
+
+def choose_shallow():
+    source = iota((TALL, EXPERTS * PAD), 1)
+    kept = jnp.where(source % PAD < CAP, source // PAD * CAP + source % PAD, -1)
+    return (kept == iota((TALL, EXPERTS * PAD), 0)).astype(BF16)
+
+
+def choose_deep(here, held, features):
+    notes = held[:, features:].astype(F32)
+    count = held.shape[0]
+    number = iota((count, 1), 0)
+    apart = (number // SLOTS) ^ (number % SLOTS // CAP)
+    place = apart * CAP + notes[:, 1:2].astype(jnp.int32)
+    mine = (notes[:, 0:1].astype(jnp.int32) == here) & (notes[:, 8:9] > 0.5)
+    place = jnp.where(mine, place, -1)
+    return (iota((TALL, count), 0) == to_row(place, count)).astype(BF16)
+
+
+def up_block(rows, means, weights):
+    product = dot(rows, weights)
+    columns = product[SLOTS : SLOTS + 1]
+    row = iota(product.shape, 0)
+    centred = product - means * columns
+    return row, centred, columns
+
+
+def up_first_kernel(deep, place_ref, h0, h1, h2, h3, weight_ref, sent_ref, rows_ref, stats_ref):
+    features = weight_ref.shape[0]
+
+    @pl.when(pl.program_id(0) == 0)
+    def _():
+        held = jnp.concatenate([h0[...], h1[...], h2[...], h3[...]], axis=0)
+        choose = choose_deep(place_ref[1], held, features) if deep else choose_shallow()
+        picked = dot(choose, held)
+        ones = (iota(picked.shape, 0) == SLOTS) & (iota(picked.shape, 1) < features)
+        rows_ref[...] = jnp.where(ones, 1.0, picked).astype(BF16)
+        wide = picked[:, :features]
+        lane = iota((TALL, META), 1)
+        total = jnp.sum(wide, axis=1, keepdims=True)
+        square = jnp.sum(wide * wide, axis=1, keepdims=True)
+        stats_ref[...] = jnp.where(lane == 0, total, jnp.where(lane == 1, square, 0.0))
+
+    means = stats_ref[:, 0:1] / features
+    row, centred, columns = up_block(rows_ref[:, :features], means, weight_ref[...])
+    high = columns.astype(BF16).astype(F32)
+    tail = jnp.where(row == SLOTS, high, jnp.where(row == SLOTS + 1, columns - high, 0.0))
+    sent_ref[...] = jnp.where(row < SLOTS, centred, tail).astype(BF16)
+
+
+def up_first(deep, place, held, weights, step):
+    features, width = weights.shape
+    half = width // 2
+    count = half // step
+    return pl.pallas_call(
+        functools.partial(up_first_kernel, deep),
+        grid_spec=pltpu.PrefetchScalarGridSpec(
+            num_scalar_prefetch=1,
+            grid=(count,),
+            in_specs=[pl.BlockSpec(h.shape, lambda i, p: (0, 0)) for h in held]
+            + [pl.BlockSpec((features, step), lambda i, p: (0, (1 - p[0]) * count + i))],
+            out_specs=[
+                pl.BlockSpec((TALL, step), lambda i, p: (0, i)),
+                pl.BlockSpec((TALL, features + META), lambda i, p: (0, 0)),
+                pl.BlockSpec((TALL, META), lambda i, p: (0, 0)),
+            ],
+        ),
+        out_shape=[
+            jax.ShapeDtypeStruct((TALL, half), BF16),
+            jax.ShapeDtypeStruct((TALL, features + META), BF16),
+            jax.ShapeDtypeStruct((TALL, META), F32),
+        ],
+        compiler_params=params(40),
+        cost_estimate=cost(2 * TALL * features * half, 2 * features * half),
+        name="up_first",
+    )(place, *held, weights)
+
+
+def up_second_kernel(place_ref, rows_ref, stats_ref, weight_ref, kept_ref):
+    features = weight_ref.shape[0]
+    means = stats_ref[:, 0:1] / features
+    row, centred, columns = up_block(rows_ref[:, :features], means, weight_ref[...])
+    kept_ref[...] = jnp.where(row < SLOTS, centred, jnp.where(row == SLOTS, columns, 0.0))
+
+
+def up_second(place, rows, stats, weights, step):
+    features, width = weights.shape
+    half = width // 2
+    count = half // step
+    return pl.pallas_call(
+        up_second_kernel,
+        grid_spec=pltpu.PrefetchScalarGridSpec(
+            num_scalar_prefetch=1,
+            grid=(count,),
+            in_specs=[
+                pl.BlockSpec(rows.shape, lambda i, p: (0, 0)),
+                pl.BlockSpec(stats.shape, lambda i, p: (0, 0)),
+                pl.BlockSpec((features, step), lambda i, p: (0, p[0] * count + i)),
+            ],
+            out_specs=pl.BlockSpec((TALL, step), lambda i, p: (0, i)),
+        ),
+        out_shape=jax.ShapeDtypeStruct((TALL, half), F32),
+        compiler_params=params(40),
+        cost_estimate=cost(2 * TALL * features * half, 2 * features * half),
+        name="up_second",
+    )(place, rows, stats, weights)
+
+
+def merge_kernel(features, kept_ref, got_ref, stats_ref, got_stats_ref, sent_ref, sum_ref, sums_ref):
+    width = kept_ref.shape[1]
+    stats, other = stats_ref[...], got_stats_ref[...]
+    apart = (stats[:, 0:1] - other[:, 0:1]) * (0.5 / features)
+    sums = stats + other
+    sums_ref[...] = sums
+    step = 512
+    for at in range(0, width, step):
+        kept = kept_ref[:, at : at + step]
+        got = got_ref[:, at : at + step].astype(F32)
+        mine = kept[SLOTS : SLOTS + 1]
+        theirs = got[SLOTS : SLOTS + 1] + got[SLOTS + 1 : SLOTS + 2]
+        row = iota(kept.shape, 0)
+        columns = mine + theirs
+        merged = jnp.where(row < SLOTS, kept + got + apart * (mine - theirs), columns)
+        sum_ref[:, at : at + step] = merged
+        high = columns.astype(BF16).astype(F32)
+        tail = jnp.where(row == SLOTS, high, jnp.where(row == SLOTS + 1, columns - high, 0.0))
+        sent_ref[:, at : at + step] = jnp.where(row < SLOTS, merged, tail).astype(BF16)
+    lane = iota((TALL, META), 1)
+    packed = jnp.zeros((TALL, META), F32)
+    for which in range(2):
+        for at, piece in enumerate(split3(sums[:, which : which + 1])):
+            packed = jnp.where(lane == 3 * which + at, piece, packed)
+    sent_ref[:, width:] = packed.astype(BF16)
+
+
+def merge(features, kept, got, stats, got_stats):
+    width = kept.shape[1]
+    return pl.pallas_call(
+        functools.partial(merge_kernel, features),
+        in_specs=[VM] * 4,
+        out_specs=[VM] * 3,
+        out_shape=[
+            jax.ShapeDtypeStruct((TALL, width + META), BF16),
+            jax.ShapeDtypeStruct((TALL, width), F32),
+            jax.ShapeDtypeStruct((TALL, META), F32),
+        ],
+        compiler_params=params(16),
+        name="merge",
+    )(kept, got, stats, got_stats)
+
+
+def hidden_kernel(features, sum_ref, sums_ref, got_ref, hidden_ref):
+    width = sum_ref.shape[1]
+    packed = got_ref[:, width:].astype(F32)
+    theirs_total = packed[:, 0:1] + packed[:, 1:2] + packed[:, 2:3]
+    theirs_square = packed[:, 3:4] + packed[:, 4:5] + packed[:, 5:6]
+    total, square = sums_ref[:, 0:1], sums_ref[:, 1:2]
+    apart = (total - theirs_total) * (0.5 / (2 * features))
+    center = (total + theirs_total) / D
+    spread = (square + theirs_square) / D - center * center
+    scale = lax.rsqrt(spread + epsilon)
+    step = 512
+    for at in range(0, width, step):
+        mine = sum_ref[:, at : at + step]
+        got = got_ref[:, at : at + step].astype(F32)
+        columns = mine[SLOTS : SLOTS + 1] - (got[SLOTS : SLOTS + 1] + got[SLOTS + 1 : SLOTS + 2])
+        pre = ((mine + got + apart * columns) * scale)[:SLOTS]
+        hidden_ref[:, at : at + step] = jax.nn.gelu(pre, approximate=True).astype(BF16)
+
+
+def hidden_units(features, total, sums, got):
+    return pl.pallas_call(
+        functools.partial(hidden_kernel, features),
+        in_specs=[VM] * 3,
+        out_specs=VM,
+        out_shape=jax.ShapeDtypeStruct((SLOTS, total.shape[1]), BF16),
+        compiler_params=params(16),
+        name="hidden",
+    )(total, sums, got)
+
+
+def down_first_kernel(place_ref, hidden_ref, weight_ref, out_ref):
+    @pl.when(pl.program_id(0) == 0)
+    def _():
+        out_ref[...] = jnp.zeros_like(out_ref)
+
+    out_ref[...] += dot(hidden_ref[...], weight_ref[...])
+
+
+def down_first(place, hidden, weights, step):
+    width, features = weights.shape
+    half = width // 2
+    count = half // step
+    return pl.pallas_call(
+        down_first_kernel,
+        grid_spec=pltpu.PrefetchScalarGridSpec(
+            num_scalar_prefetch=1,
+            grid=(count,),
+            in_specs=[
+                pl.BlockSpec((SLOTS, step), lambda i, p: (0, i)),
+                pl.BlockSpec((step, features), lambda i, p: (p[0] * count + i, 0)),
+            ],
+            out_specs=pl.BlockSpec((SLOTS, features), lambda i, p: (0, 0)),
+        ),
+        out_shape=jax.ShapeDtypeStruct((SLOTS, features), F32),
+        compiler_params=params(40),
+        cost_estimate=cost(2 * SLOTS * features * half, 2 * features * half),
+        name="down_first",
+    )(place, hidden, weights)
+
+
+def down_second_kernel(deep, place_ref, part_ref, rows_ref, hidden_ref, weight_ref, *rest):
+    outs, total_ref = rest[:-1], rest[-1]
+    features = weight_ref.shape[1]
+
+    @pl.when(pl.program_id(0) == 0)
+    def _():
+        total_ref[...] = part_ref[...]
+
+    total_ref[...] += dot(hidden_ref[...], weight_ref[...])
+
+    @pl.when(pl.program_id(0) == pl.num_programs(0) - 1)
+    def _():
+        rows = rows_ref[...].astype(F32)[:SLOTS]
+        notes = rows[:, features:]
+        first = 5 if deep else 2
+        gate = notes[:, first : first + 1] + notes[:, first + 1 : first + 2]
+        gate = gate + notes[:, first + 2 : first + 3]
+        result = rows[:, :features] + gate * total_ref[...]
+        if not deep:
+            outs[0][...] = jnp.concatenate([result, notes], axis=1).astype(BF16)
+        else:
+            target = iota((EXPERTS * PAD, SLOTS), 0)
+            kept = jnp.where(target % PAD < CAP, target // PAD * CAP + target % PAD, -1)
+            spread = (kept == iota((EXPERTS * PAD, SLOTS), 1)).astype(BF16)
+            placed = dot(spread, result.astype(BF16))
+            for at, out in enumerate(outs):
+                out[...] = placed[at * PAD : (at + 1) * PAD].astype(BF16)
+
+
+def down_second(deep, place, part, rows, hidden, weights, step):
+    width, features = weights.shape
+    half = width // 2
+    count = half // step
+    fixed = lambda i, p: (0, 0)
+    shapes = [(PAD, features)] * EXPERTS if deep else [(SLOTS, features + META)]
+    return pl.pallas_call(
+        functools.partial(down_second_kernel, deep),
+        grid_spec=pltpu.PrefetchScalarGridSpec(
+            num_scalar_prefetch=1,
+            grid=(count,),
+            in_specs=[
+                pl.BlockSpec(part.shape, fixed),
+                pl.BlockSpec(rows.shape, fixed),
+                pl.BlockSpec((SLOTS, step), lambda i, p: (0, i)),
+                pl.BlockSpec((step, features), lambda i, p: ((1 - p[0]) * count + i, 0)),
+            ],
+            out_specs=[pl.BlockSpec(shape, fixed) for shape in shapes],
+            scratch_shapes=[pltpu.VMEM((SLOTS, features), F32)],
+        ),
+        out_shape=[jax.ShapeDtypeStruct(shape, BF16) for shape in shapes],
+        compiler_params=params(40),
+        cost_estimate=cost(2 * SLOTS * features * half, 2 * features * half),
+        name="down_second",
+    )(place, part, rows, hidden, weights)
+
+
+def finish_kernel(place_ref, deep_ref, g0, g1, g2, g3, out_ref):
+    rows = out_ref.shape[0]
+    deep = deep_ref[...]
+    column = to_column(deep, rows)
+    place = (column ^ place_ref[1]) * PAD + ranks(deep, column, rows)
+    choose = (iota((rows, EXPERTS * PAD), 1) == place).astype(BF16)
+    held = jnp.concatenate([g0[...], g1[...], g2[...], g3[...]], axis=0)
+    out_ref[...] = dot(choose, held).astype(BF16)
+
+
+def finish(place, deep, got, rows):
+    return pl.pallas_call(
+        finish_kernel,
+        in_specs=[SM] + [VM] * 5,
+        out_specs=VM,
+        out_shape=jax.ShapeDtypeStruct((rows, got[0].shape[1]), BF16),
+        compiler_params=params(16),
+        name="finish",
+    )(place, deep, *got)
+
+
+def swap(value, axis, apart):
+    count = lax.axis_size(axis)
+    return lax.ppermute(value, axis, [(i, i ^ apart) for i in range(count)])
+
+
+def swap_all(blocks):
+    return [blocks[0]] + [swap(blocks[k], "ep", k) for k in (1, 2, 3)]
+
+
+def expert_block(deep, place, held, up, down):
+    features = up.shape[0]
+    step = min(1024, up.shape[1] // 2)
+    sent, rows, stats = up_first(deep, place, held, up, step)
+    got, got_stats = swap(sent, "tp", 1), swap(stats, "tp", 1)
+    kept = up_second(place, rows, stats, up, step)
+    sent, total, sums = merge(features, kept, got, stats, got_stats)
+    hidden = hidden_units(features, total, sums, swap(sent, "tp", 2))
+    other = swap(hidden, "tp", 1)
+    part = down_first(place, hidden, down, step)
+    return down_second(deep, place, part, rows, other, down, step)
+
+
+def fast_body(
+    resid,
+    query,
+    new_key,
+    new_value,
+    cache_keys,
+    cache_values,
+    cache_lengths,
+    shallow_expert,
+    shallow_gate,
+    shallow_up,
+    shallow_down,
+    deep_expert,
+    deep_gate,
+    deep_up,
+    deep_down,
+):
+    rows = resid.shape[0]
+    place = jnp.stack([lax.axis_index("tp") % 2, lax.axis_index("ep")]).astype(jnp.int32)
+    deep_ids = deep_expert.reshape(1, rows)
+    blocks = attend(
+        place,
+        (
+            resid,
+            query,
+            new_key,
+            new_value,
+            cache_keys,
+            cache_values,
+            cache_lengths.reshape(1, rows),
+            shallow_expert.reshape(1, rows),
+            shallow_gate.reshape(1, rows),
+            deep_ids,
+            deep_gate.reshape(1, rows),
+        ),
+    )
+    held = swap_all(blocks)
+    (after,) = expert_block(False, place, held, shallow_up, shallow_down)
+    held = swap_all([after] * EXPERTS)
+    blocks = expert_block(True, place, held, deep_up, deep_down)
+    return finish(place, deep_ids, swap_all(blocks), rows)
+
+
 def solution(mesh):
+    fits = mesh.shape["ep"] == EXPERTS and mesh.shape["tp"] == 4
     return jax.shard_map(
-        body,
+        fast_body if fits else general_body,
         mesh=mesh,
         in_specs=(
             P(("groups", "ep"), "tp"),

time: 220 us -> 118 us (0.54)
  waiting for transfers between devices: 102 us -> 39 us
  Pallas kernels: 0 us -> 50.6 us
  blocking collectives: 43.8 us -> 0 us
  matrix products: 40.7 us -> 0 us
  between operations: 13.7 us -> 0.22 us
  starting transfers between devices: 9.2 us -> 19 us
  other arithmetic: 2.72 us -> 0.07 us
    psum x2 -> x0, waiting for transfers between devices: 84 us -> none  [expert_layer(): summed = lax.psum(flat_pre, 'tp')]
    pallas_call x0 -> x14, Pallas kernels: none -> 50.6 us  [the longest x2 11.9 us: up_first(): pl.pallas_call(functools.partial(up_first_kernel, deep), grid_spec=pltpu....]
    dot_general x8 -> x0, matrix products: 40.7 us -> none  [the longest x2 19.9 us: expert_layer(): jnp.einsum('scd,df->scf', chosen, up_weight, preferred_element_type=jnp.f...]
    ppermute x0 -> x17, waiting for transfers between devices: none -> 39 us  [swap(): return lax.ppermute(value, axis, [(i, i ^ apart) for i in range(count)])]
    all_gather x2 -> x0, blocking collectives: 29.8 us -> none  [expert_layer(): lax.all_gather(compact[None], 'ep', axis=0, tiled=True)]
    ppermute x0 -> x17, starting transfers between devices: none -> 19 us  [swap(): return lax.ppermute(value, axis, [(i, i ^ apart) for i in range(count)])]
    all_to_all x2 -> x0, waiting for transfers between devices: 17.5 us -> none  [expert_layer(): lax.all_to_all(partial_value.reshape(ep_count, slots, feature_count), 'ep...]
    psum x2 -> x0, blocking collectives: 14 us -> none  [expert_layer(): lax.psum((jnp.sum(wide, axis=1), jnp.sum(wide * wide, axis=1)), 'tp')]
  transfers between devices with their start and end apart: 4 -> 17, of which waited for: 4 -> 8; matrix products, arithmetic and copies ran while one was open for 0% -> 0% of each run, Pallas kernels for 0% -> 19%
where the time goes in v1:
time: 118 us
  Pallas kernels  50.6 us (43%)
  waiting for transfers between devices  39 us (33%)
  starting transfers between devices  19 us (16%)
  local copies, waits for them, and re-layouts  8.72 us (7%)
    ppermute x17, waiting for transfers between devices, swap(): return lax.ppermute(value, axis, [(i, i ^ apart) for i in range(count)])  39 us
    ppermute x17, starting transfers between devices, swap(): return lax.ppermute(value, axis, [(i, i ^ apart) for i in range(count)])  19 us
    pallas_call x2, Pallas kernels, up_first(): pl.pallas_call(functools.partial(up_first_kernel, deep), grid_spec=pltpu....  11.9 us
    pallas_call x2, Pallas kernels, down_second(): pl.pallas_call(functools.partial(down_second_kernel, deep), grid_spec=plt...  11.5 us
    pallas_call x2, Pallas kernels, up_second(): pl.pallas_call(up_second_kernel, grid_spec=pltpu.PrefetchScalarGridSpec(n...  11.2 us
    pallas_call x2, Pallas kernels, down_first(): pl.pallas_call(down_first_kernel, grid_spec=pltpu.PrefetchScalarGridSpec(...  11.1 us
    unnamed x24, local copies, waits for them, and re-layouts  8.72 us
  transfers between devices with their start and end apart: 17, of which 8 were waited for; matrix products, arithmetic and copies ran while one was open for 0% of the time, Pallas kernels for 19%

profile of v1, /device:TPU:0, one launch (start us, length us, event | category | flops | bytes accessed | tf_op | source)
XLA Modules:
  0.0 117.6 jit_solution(3276887204930927492)
XLA Ops:
  0.1 1.0 copy-done
  1.1 1.0 copy-done.1
  2.2 0.8 copy-done.2
  3.0 0.8 copy-done.3
  3.8 0.8 copy-done.4
  4.7 0.8 copy-done.5
  5.5 0.7 copy-done.6
  6.2 0.7 copy-done.8
  8.8 1.9 %attend.1 = (bf16[16,1152]{1,0:T(8,128)(2,1)S(1)}, bf16[16,1152]{1,0:T(8,128)(2,1)S(1)}, bf16[16,1152]{1,0:T(8,128)(2,1)S(1)}, bf16[16,1152]{1,0:T(8,128)(2,1)S(1)}) custom-call(s32[2]{0:T(128)S(1)} %pad_add_fusion.place_ref, bf16[32,1024]{1,0:T(8,128)(2,1)S(1)} %copy-done.2, bf16[32,1024]{1,0:T(8,128)(2,1)S(1)} %copy-done.3, ...), custom_call_target="tpu_custom_call" | custom-call | tf_op jit(solution)/shard_map/attend/pallas_call | solution.py:231
  10.7 3.1 %collective-permute-start = (bf16[16,1152]{1,0:T(8,128)(2,1)S(1)}, bf16[16,1152]{1,0:T(8,128)(2,1)S(1)}, u32[]{:S(2)}, u32[]{:S(2)}) collective-permute-start(bf16[16,1152]{1,0:T(8,128)(2,1)S(1)} %get-tuple-element.26), channel_id=1, source_target_pairs={{0,4},{4,0},{8,12},{12,8},{1,5},{5,1},{9,13},{13,9},{2,6},{6,2},{1... | collective-permute-start | bytes 110600 | tf_op jit(solution)/shard_map/ppermute | solution.py:529
  13.8 2.6 %collective-permute-start.1 = (bf16[16,1152]{1,0:T(8,128)(2,1)S(1)}, bf16[16,1152]{1,0:T(8,128)(2,1)S(1)}, u32[]{:S(2)}, u32[]{:S(2)}) collective-permute-start(bf16[16,1152]{1,0:T(8,128)(2,1)S(1)} %get-tuple-element.27), channel_id=1, source_target_pairs={{0,8},{4,12},{8,0},{12,4},{1,9},{5,13},{9,1},{13,5},{2,10},{6,14},... | collective-permute-start | bytes 110600 | tf_op jit(solution)/shard_map/ppermute | solution.py:529
  16.4 2.9 %collective-permute-done.1.h2 = bf16[16,1152]{1,0:T(8,128)(2,1)S(1)} collective-permute-done((bf16[16,1152]{1,0:T(8,128)(2,1)S(1)}, bf16[16,1152]{1,0:T(8,128)(2,1)S(1)}, u32[]{:S(2)}, u32[]{:S(2)}) %collective-permute-start.1) | collective-permute-done | bytes 36896 | tf_op jit(solution)/shard_map/ppermute | solution.py:529
  19.3 2.8 %collective-permute-done.2.h3 = bf16[16,1152]{1,0:T(8,128)(2,1)S(1)} collective-permute-done((bf16[16,1152]{1,0:T(8,128)(2,1)S(1)}, bf16[16,1152]{1,0:T(8,128)(2,1)S(1)}, u32[]{:S(2)}, u32[]{:S(2)}) %collective-permute-start.2) | collective-permute-done | bytes 36896 | tf_op jit(solution)/shard_map/ppermute | solution.py:529
  22.1 5.8 %up_first.2 = (bf16[56,4096]{1,0:T(8,128)(2,1)S(1)}, bf16[56,1152]{1,0:T(8,128)(2,1)S(1)}, f32[56,128]{1,0:T(8,128)S(1)}) custom-call(s32[2]{0:T(128)S(1)} %pad_add_fusion.place_ref, bf16[16,1152]{1,0:T(8,128)(2,1)S(1)} %get-tuple-element.25.h0, bf16[16,1152]{1,0:T(8,128)(2,1)S(1)} %collective-permute-done.h1, ...), custom_call_target="tpu_custom_call" | custom-call | flops 469762048 | bytes 8388608 | tf_op jit(solution)/shard_map/up_first/pallas_call | solution.py:293
  28.5 5.6 %up_second.2.kept_ref = f32[56,4096]{1,0:T(8,128)S(1)} custom-call(s32[2]{0:T(128)S(1)} %pad_add_fusion.place_ref, bf16[56,1152]{1,0:T(8,128)(2,1)S(1)} %get-tuple-element.29.rows_ref, f32[56,128]{1,0:T(8,128)S(1)} %get-tuple-element.30.stats_ref, bf16[1024,8192]{1,0:T(8,128)(2,1)} %weight_ref.9), custom_call_target="tpu_custom_call" | custom-call | flops 469762048 | bytes 8388608 | tf_op jit(solution)/shard_map/up_second/pallas_call | solution.py:328
  34.3 1.6 %collective-permute-start.5 = (bf16[56,4224]{1,0:T(8,128)(2,1)S(1)}, bf16[56,4224]{1,0:T(8,128)(2,1)S(1)}, u32[]{:S(2)}, u32[]{:S(2)}) collective-permute-start(bf16[56,4224]{1,0:T(8,128)(2,1)S(1)} %get-tuple-element.34), channel_id=1, source_target_pairs={{0,2},{1,3},{2,0},{3,1},{4,6},{5,7},{6,4},{7,5},{8,10},{9,11},{10,... | collective-permute-start | bytes 1419272 | tf_op jit(solution)/shard_map/ppermute | solution.py:529
  35.9 11.3 %collective-permute-done.5.got_ref = bf16[56,4224]{1,0:T(8,128)(2,1)S(1)} collective-permute-done((bf16[56,4224]{1,0:T(8,128)(2,1)S(1)}, bf16[56,4224]{1,0:T(8,128)(2,1)S(1)}, u32[]{:S(2)}, u32[]{:S(2)}) %collective-permute-start.5) | collective-permute-done | bytes 473120 | tf_op jit(solution)/shard_map/ppermute | solution.py:529
  47.9 5.5 %down_first.2.part_ref = f32[48,1024]{1,0:T(8,128)S(1)} custom-call(s32[2]{0:T(128)S(1)} %pad_add_fusion.place_ref, bf16[48,4096]{1,0:T(8,128)(2,1)S(1)} %hidden.2.hidden_ref, bf16[8192,1024]{1,0:T(8,128)(2,1)} %weight_ref.11), custom_call_target="tpu_custom_call" | custom-call | flops 402653184 | bytes 8388608 | tf_op jit(solution)/shard_map/down_first/pallas_call | solution.py:432
  53.4 5.7 %down_second.2.h0 = bf16[48,1152]{1,0:T(8,128)(2,1)S(1)} custom-call(s32[2]{0:T(128)S(1)} %pad_add_fusion.place_ref, f32[48,1024]{1,0:T(8,128)S(1)} %down_first.2.part_ref, bf16[56,1152]{1,0:T(8,128)(2,1)S(1)} %get-tuple-element.29.rows_ref, bf16[48,4096]{1,0:T(8,128)(2,1)S(1)} %collective-permute-done.6.hidden_ref, bf16[8192,1024]{1,0:T(8,128)(2,1)} %weight_ref.11), custom_call_target="tpu_custom_call" | custom-call | flops 402653184 | bytes 8388608 | tf_op jit(solution)/shard_map/down_second/pallas_call | solution.py:485
  59.7 3.9 %collective-permute-start.7 = (bf16[48,1152]{1,0:T(8,128)(2,1)S(1)}, bf16[48,1152]{1,0:T(8,128)(2,1)S(1)}, u32[]{:S(2)}, u32[]{:S(2)}) collective-permute-start(bf16[48,1152]{1,0:T(8,128)(2,1)S(1)} %down_second.2.h0), channel_id=1, source_target_pairs={{0,4},{4,0},{8,12},{12,8},{1,5},{5,1},{9,13},{13,9},{2,6},{6,2},{1... | collective-permute-start | bytes 331784 | tf_op jit(solution)/shard_map/ppermute | solution.py:529
  63.6 3.4 %collective-permute-done.9.h3 = bf16[48,1152]{1,0:T(8,128)(2,1)S(1)} collective-permute-done((bf16[48,1152]{1,0:T(8,128)(2,1)S(1)}, bf16[48,1152]{1,0:T(8,128)(2,1)S(1)}, u32[]{:S(2)}, u32[]{:S(2)}) %collective-permute-start.9) | collective-permute-done | bytes 110624 | tf_op jit(solution)/shard_map/ppermute | solution.py:529
  67.0 3.6 %collective-permute-done.8.h2 = bf16[48,1152]{1,0:T(8,128)(2,1)S(1)} collective-permute-done((bf16[48,1152]{1,0:T(8,128)(2,1)S(1)}, bf16[48,1152]{1,0:T(8,128)(2,1)S(1)}, u32[]{:S(2)}, u32[]{:S(2)}) %collective-permute-start.8) | collective-permute-done | bytes 110624 | tf_op jit(solution)/shard_map/ppermute | solution.py:529
  70.5 6.1 %up_first.3 = (bf16[56,4096]{1,0:T(8,128)(2,1)S(1)}, bf16[56,1152]{1,0:T(8,128)(2,1)S(1)}, f32[56,128]{1,0:T(8,128)S(1)}) custom-call(s32[2]{0:T(128)S(1)} %pad_add_fusion.place_ref, bf16[48,1152]{1,0:T(8,128)(2,1)S(1)} %down_second.2.h0, bf16[48,1152]{1,0:T(8,128)(2,1)S(1)} %collective-permute-done.7.h1, bf16[48,1152]{1,0:T(8,128)(2,1)S(1)} %collective-permute-done.8.h2, ...), custom_call_target="tpu_custom_call" | custom-call | flops 469762048 | bytes 8388608 | tf_op jit(solution)/shard_map/up_first/pallas_call | solution.py:293
  77.2 5.6 %up_second.3.kept_ref = f32[56,4096]{1,0:T(8,128)S(1)} custom-call(s32[2]{0:T(128)S(1)} %pad_add_fusion.place_ref, bf16[56,1152]{1,0:T(8,128)(2,1)S(1)} %get-tuple-element.35.rows_ref, f32[56,128]{1,0:T(8,128)S(1)} %get-tuple-element.36.stats_ref, bf16[1024,8192]{1,0:T(8,128)(2,1)} %weight_ref.13), custom_call_target="tpu_custom_call" | custom-call | flops 469762048 | bytes 8388608 | tf_op jit(solution)/shard_map/up_second/pallas_call | solution.py:328
  83.0 1.6 %collective-permute-start.12 = (bf16[56,4224]{1,0:T(8,128)(2,1)S(1)}, bf16[56,4224]{1,0:T(8,128)(2,1)S(1)}, u32[]{:S(2)}, u32[]{:S(2)}) collective-permute-start(bf16[56,4224]{1,0:T(8,128)(2,1)S(1)} %get-tuple-element.40), channel_id=1, source_target_pairs={{0,2},{1,3},{2,0},{3,1},{4,6},{5,7},{6,4},{7,5},{8,10},{9,11},{10,... | collective-permute-start | bytes 1419272 | tf_op jit(solution)/shard_map/ppermute | solution.py:529
  84.6 11.3 %collective-permute-done.12.got_ref = bf16[56,4224]{1,0:T(8,128)(2,1)S(1)} collective-permute-done((bf16[56,4224]{1,0:T(8,128)(2,1)S(1)}, bf16[56,4224]{1,0:T(8,128)(2,1)S(1)}, u32[]{:S(2)}, u32[]{:S(2)}) %collective-permute-start.12) | collective-permute-done | bytes 473120 | tf_op jit(solution)/shard_map/ppermute | solution.py:529
  96.6 5.5 %down_first.3.part_ref = f32[48,1024]{1,0:T(8,128)S(1)} custom-call(s32[2]{0:T(128)S(1)} %pad_add_fusion.place_ref, bf16[48,4096]{1,0:T(8,128)(2,1)S(1)} %hidden.3.hidden_ref, bf16[8192,1024]{1,0:T(8,128)(2,1)} %weight_ref.15), custom_call_target="tpu_custom_call" | custom-call | flops 402653184 | bytes 8388608 | tf_op jit(solution)/shard_map/down_first/pallas_call | solution.py:432
  102.1 5.8 %down_second.3 = (bf16[16,1024]{1,0:T(8,128)(2,1)S(1)}, bf16[16,1024]{1,0:T(8,128)(2,1)S(1)}, bf16[16,1024]{1,0:T(8,128)(2,1)S(1)}, bf16[16,1024]{1,0:T(8,128)(2,1)S(1)}) custom-call(s32[2]{0:T(128)S(1)} %pad_add_fusion.place_ref, f32[48,1024]{1,0:T(8,128)S(1)} %down_first.3.part_ref, bf16[56,1152]{1,0:T(8,128)(2,1)S(1)} %get-tuple-element.35.rows_ref, ...), custom_call_target="tpu_custom_call" | custom-call | flops 402653184 | bytes 8388608 | tf_op jit(solution)/shard_map/down_second/pallas_call | solution.py:485
  108.1 2.3 %collective-permute-start.15 = (bf16[16,1024]{1,0:T(8,128)(2,1)S(1)}, bf16[16,1024]{1,0:T(8,128)(2,1)S(1)}, u32[]{:S(2)}, u32[]{:S(2)}) collective-permute-start(bf16[16,1024]{1,0:T(8,128)(2,1)S(1)} %get-tuple-element.43), channel_id=1, source_target_pairs={{0,8},{4,12},{8,0},{12,4},{1,9},{5,13},{9,1},{13,5},{2,10},{6,14},... | collective-permute-start | bytes 98312 | tf_op jit(solution)/shard_map/ppermute | solution.py:529
  110.4 2.0 %collective-permute-start.16 = (bf16[16,1024]{1,0:T(8,128)(2,1)S(1)}, bf16[16,1024]{1,0:T(8,128)(2,1)S(1)}, u32[]{:S(2)}, u32[]{:S(2)}) collective-permute-start(bf16[16,1024]{1,0:T(8,128)(2,1)S(1)} %get-tuple-element.44), channel_id=1, source_target_pairs={{0,12},{4,8},{8,4},{12,0},{1,13},{5,9},{9,5},{13,1},{2,14},{6,10},... | collective-permute-start | bytes 98312 | tf_op jit(solution)/shard_map/ppermute | solution.py:529
  113.0 3.2 %collective-permute-done.16.g3 = bf16[16,1024]{1,0:T(8,128)(2,1)S(1)} collective-permute-done((bf16[16,1024]{1,0:T(8,128)(2,1)S(1)}, bf16[16,1024]{1,0:T(8,128)(2,1)S(1)}, u32[]{:S(2)}, u32[]{:S(2)}) %collective-permute-start.16) | collective-permute-done | bytes 32800 | tf_op jit(solution)/shard_map/ppermute | solution.py:529
  116.1 1.5 %finish.1 = bf16[32,1024]{1,0:T(8,128)(2,1)} custom-call(s32[2]{0:T(128)S(1)} %pad_add_fusion.place_ref, s32[1,32]{1,0:T(1,128)S(1)} %bitcast.8, bf16[16,1024]{1,0:T(8,128)(2,1)S(1)} %get-tuple-element.41.g0, bf16[16,1024]{1,0:T(8,128)(2,1)S(1)} %collective-permute-done.14.g1, bf16[16,1024]{1,0:T(8,128)(2,1)S(1)} %collective-permute-done.15.g2, ...), custom_call_target="tpu_custom_call" | custom-call | tf_op jit(solution)/shard_map/finish/pallas_call | solution.py:517
  (41 shorter events, 6.1 us)
Async XLA Ops:
  0.1 1.0 copy-start
  1.1 1.0 copy-start.1
  2.2 0.8 copy-start.2
  3.0 0.8 copy-start.3
  3.8 0.8 copy-start.4
  4.7 0.8 copy-start.5
  5.5 0.7 copy-start.6
  6.2 0.7 copy-start.8
  6.8 0.7 copy-start.9
  7.5 0.7 copy-start.10
  8.1 0.7 copy-start.11
  10.7 5.7 %collective-permute-start = (bf16[16,1152]{1,0:T(8,128)(2,1)S(1)}, bf16[16,1152]{1,0:T(8,128)(2,1)S(1)}, u32[]{:S(2)}, u32[]{:S(2)}) collective-permute-start(bf16[16,1152]{1,0:T(8,128)(2,1)S(1)} %get-tuple-element.26), channel_id=1, source_target_pairs={{0,4},{4,0},{8,12},{12,8},{1,5},{5,1},{9,13},{13,9},{2,6},{6,2},{1... | collective-permute-start | bytes 110600 | tf_op jit(solution)/shard_map/ppermute | solution.py:529
  13.8 5.5 %collective-permute-start.1 = (bf16[16,1152]{1,0:T(8,128)(2,1)S(1)}, bf16[16,1152]{1,0:T(8,128)(2,1)S(1)}, u32[]{:S(2)}, u32[]{:S(2)}) collective-permute-start(bf16[16,1152]{1,0:T(8,128)(2,1)S(1)} %get-tuple-element.27), channel_id=1, source_target_pairs={{0,8},{4,12},{8,0},{12,4},{1,9},{5,13},{9,1},{13,5},{2,10},{6,14},... | collective-permute-start | bytes 110600 | tf_op jit(solution)/shard_map/ppermute | solution.py:529
  16.4 5.8 %collective-permute-start.2 = (bf16[16,1152]{1,0:T(8,128)(2,1)S(1)}, bf16[16,1152]{1,0:T(8,128)(2,1)S(1)}, u32[]{:S(2)}, u32[]{:S(2)}) collective-permute-start(bf16[16,1152]{1,0:T(8,128)(2,1)S(1)} %get-tuple-element.28), channel_id=1, source_target_pairs={{0,12},{4,8},{8,4},{12,0},{1,13},{5,9},{9,5},{13,1},{2,14},{6,10},... | collective-permute-start | bytes 110600 | tf_op jit(solution)/shard_map/ppermute | solution.py:529
  27.9 6.2 %collective-permute-start.3 = (bf16[56,4096]{1,0:T(8,128)(2,1)S(1)}, bf16[56,4096]{1,0:T(8,128)(2,1)S(1)}, u32[]{:S(2)}, u32[]{:S(2)}) collective-permute-start(bf16[56,4096]{1,0:T(8,128)(2,1)S(1)} %get-tuple-element.31), channel_id=1, source_target_pairs={{0,1},{1,0},{2,3},{3,2},{4,5},{5,4},{6,7},{7,6},{8,9},{9,8},{10,11... | collective-permute-start | bytes 1376264 | tf_op jit(solution)/shard_map/ppermute | solution.py:529
  28.0 6.1 %collective-permute-start.4 = (f32[56,128]{1,0:T(8,128)S(1)}, f32[56,128]{1,0:T(8,128)S(1)}, u32[]{:S(2)}, u32[]{:S(2)}) collective-permute-start(f32[56,128]{1,0:T(8,128)S(1)} %get-tuple-element.30.stats_ref), channel_id=1, source_target_pairs={{0,1},{1,0},{2,3},{3,2},{4,5},{5,4},{6,7},{7,6},{8,9},{9,8},{10,11... | collective-permute-start | bytes 86024 | tf_op jit(solution)/shard_map/ppermute | solution.py:529
  34.3 12.9 %collective-permute-start.5 = (bf16[56,4224]{1,0:T(8,128)(2,1)S(1)}, bf16[56,4224]{1,0:T(8,128)(2,1)S(1)}, u32[]{:S(2)}, u32[]{:S(2)}) collective-permute-start(bf16[56,4224]{1,0:T(8,128)(2,1)S(1)} %get-tuple-element.34), channel_id=1, source_target_pairs={{0,2},{1,3},{2,0},{3,1},{4,6},{5,7},{6,4},{7,5},{8,10},{9,11},{10,... | collective-permute-start | bytes 1419272 | tf_op jit(solution)/shard_map/ppermute | solution.py:529
  47.8 5.6 %collective-permute-start.6 = (bf16[48,4096]{1,0:T(8,128)(2,1)S(1)}, bf16[48,4096]{1,0:T(8,128)(2,1)S(1)}, u32[]{:S(2)}, u32[]{:S(2)}) collective-permute-start(bf16[48,4096]{1,0:T(8,128)(2,1)S(1)} %hidden.2.hidden_ref), channel_id=1, source_target_pairs={{0,1},{1,0},{2,3},{3,2},{4,5},{5,4},{6,7},{7,6},{8,9},{9,8},{10,11... | collective-permute-start | bytes 1179656 | tf_op jit(solution)/shard_map/ppermute | solution.py:529
  59.1 7.9 %collective-permute-start.9 = (bf16[48,1152]{1,0:T(8,128)(2,1)S(1)}, bf16[48,1152]{1,0:T(8,128)(2,1)S(1)}, u32[]{:S(2)}, u32[]{:S(2)}) collective-permute-start(bf16[48,1152]{1,0:T(8,128)(2,1)S(1)} %down_second.2.h0), channel_id=1, source_target_pairs={{0,12},{4,8},{8,4},{12,0},{1,13},{5,9},{9,5},{13,1},{2,14},{6,10},... | collective-permute-start | bytes 331784 | tf_op jit(solution)/shard_map/ppermute | solution.py:529
  59.7 10.8 %collective-permute-start.8 = (bf16[48,1152]{1,0:T(8,128)(2,1)S(1)}, bf16[48,1152]{1,0:T(8,128)(2,1)S(1)}, u32[]{:S(2)}, u32[]{:S(2)}) collective-permute-start(bf16[48,1152]{1,0:T(8,128)(2,1)S(1)} %down_second.2.h0), channel_id=1, source_target_pairs={{0,8},{4,12},{8,0},{12,4},{1,9},{5,13},{9,1},{13,5},{2,10},{6,14},... | collective-permute-start | bytes 331784 | tf_op jit(solution)/shard_map/ppermute | solution.py:529
  59.7 10.8 %collective-permute-start.7 = (bf16[48,1152]{1,0:T(8,128)(2,1)S(1)}, bf16[48,1152]{1,0:T(8,128)(2,1)S(1)}, u32[]{:S(2)}, u32[]{:S(2)}) collective-permute-start(bf16[48,1152]{1,0:T(8,128)(2,1)S(1)} %down_second.2.h0), channel_id=1, source_target_pairs={{0,4},{4,0},{8,12},{12,8},{1,5},{5,1},{9,13},{13,9},{2,6},{6,2},{1... | collective-permute-start | bytes 331784 | tf_op jit(solution)/shard_map/ppermute | solution.py:529
  76.6 6.2 %collective-permute-start.10 = (bf16[56,4096]{1,0:T(8,128)(2,1)S(1)}, bf16[56,4096]{1,0:T(8,128)(2,1)S(1)}, u32[]{:S(2)}, u32[]{:S(2)}) collective-permute-start(bf16[56,4096]{1,0:T(8,128)(2,1)S(1)} %get-tuple-element.37), channel_id=1, source_target_pairs={{0,1},{1,0},{2,3},{3,2},{4,5},{5,4},{6,7},{7,6},{8,9},{9,8},{10,11... | collective-permute-start | bytes 1376264 | tf_op jit(solution)/shard_map/ppermute | solution.py:529
  76.7 6.1 %collective-permute-start.11 = (f32[56,128]{1,0:T(8,128)S(1)}, f32[56,128]{1,0:T(8,128)S(1)}, u32[]{:S(2)}, u32[]{:S(2)}) collective-permute-start(f32[56,128]{1,0:T(8,128)S(1)} %get-tuple-element.36.stats_ref), channel_id=1, source_target_pairs={{0,1},{1,0},{2,3},{3,2},{4,5},{5,4},{6,7},{7,6},{8,9},{9,8},{10,11... | collective-permute-start | bytes 86024 | tf_op jit(solution)/shard_map/ppermute | solution.py:529
  83.0 12.9 %collective-permute-start.12 = (bf16[56,4224]{1,0:T(8,128)(2,1)S(1)}, bf16[56,4224]{1,0:T(8,128)(2,1)S(1)}, u32[]{:S(2)}, u32[]{:S(2)}) collective-permute-start(bf16[56,4224]{1,0:T(8,128)(2,1)S(1)} %get-tuple-element.40), channel_id=1, source_target_pairs={{0,2},{1,3},{2,0},{3,1},{4,6},{5,7},{6,4},{7,5},{8,10},{9,11},{10,... | collective-permute-start | bytes 1419272 | tf_op jit(solution)/shard_map/ppermute | solution.py:529
  96.5 19.6 %copy-start.7 = (s32[32,1]{0,1:T(1,128)S(1)}, s32[32,1]{0,1:T(1,128)}, u32[]{:S(2)}) copy-start(s32[32,1]{0,1:T(1,128)} %param.26) | copy-start | bytes 388
  96.5 5.6 %collective-permute-start.13 = (bf16[48,4096]{1,0:T(8,128)(2,1)S(1)}, bf16[48,4096]{1,0:T(8,128)(2,1)S(1)}, u32[]{:S(2)}, u32[]{:S(2)}) collective-permute-start(bf16[48,4096]{1,0:T(8,128)(2,1)S(1)} %hidden.3.hidden_ref), channel_id=1, source_target_pairs={{0,1},{1,0},{2,3},{3,2},{4,5},{5,4},{6,7},{7,6},{8,9},{9,8},{10,11... | collective-permute-start | bytes 1179656 | tf_op jit(solution)/shard_map/ppermute | solution.py:529
  108.0 4.5 %collective-permute-start.14 = (bf16[16,1024]{1,0:T(8,128)(2,1)S(1)}, bf16[16,1024]{1,0:T(8,128)(2,1)S(1)}, u32[]{:S(2)}, u32[]{:S(2)}) collective-permute-start(bf16[16,1024]{1,0:T(8,128)(2,1)S(1)} %get-tuple-element.42), channel_id=1, source_target_pairs={{0,4},{4,0},{8,12},{12,8},{1,5},{5,1},{9,13},{13,9},{2,6},{6,2},{1... | collective-permute-start | bytes 98312 | tf_op jit(solution)/shard_map/ppermute | solution.py:529
  108.1 4.9 %collective-permute-start.15 = (bf16[16,1024]{1,0:T(8,128)(2,1)S(1)}, bf16[16,1024]{1,0:T(8,128)(2,1)S(1)}, u32[]{:S(2)}, u32[]{:S(2)}) collective-permute-start(bf16[16,1024]{1,0:T(8,128)(2,1)S(1)} %get-tuple-element.43), channel_id=1, source_target_pairs={{0,8},{4,12},{8,0},{12,4},{1,9},{5,13},{9,1},{13,5},{2,10},{6,14},... | collective-permute-start | bytes 98312 | tf_op jit(solution)/shard_map/ppermute | solution.py:529
  110.4 5.7 %collective-permute-start.16 = (bf16[16,1024]{1,0:T(8,128)(2,1)S(1)}, bf16[16,1024]{1,0:T(8,128)(2,1)S(1)}, u32[]{:S(2)}, u32[]{:S(2)}) collective-permute-start(bf16[16,1024]{1,0:T(8,128)(2,1)S(1)} %get-tuple-element.44), channel_id=1, source_target_pairs={{0,12},{4,8},{8,4},{12,0},{1,13},{5,9},{9,5},{13,1},{2,14},{6,10},... | collective-permute-start | bytes 98312 | tf_op jit(solution)/shard_map/ppermute | solution.py:529

commit v2 on v1

v2 whole, which is shorter than its diff:
```python
import functools
import math

import jax
import jax.numpy as jnp
from jax import lax
from jax.experimental import pallas as pl
from jax.experimental.pallas import tpu as pltpu
from jax.sharding import PartitionSpec as P

D = 4096
HD = 128
EXPERTS = 4
CAP = 12


epsilon = 1e-05


def attention(resid, query, new_key, new_value, cache_keys, cache_values, cache_lengths):
    row_count, feature_count = resid.shape
    heads_here = feature_count // HD
    depth = cache_keys.shape[1]
    queries = query.reshape(row_count, heads_here, HD)
    own_keys = new_key.reshape(row_count, heads_here, HD)
    own_values = new_value.reshape(row_count, heads_here, HD)
    past_keys = cache_keys.reshape(row_count, depth, heads_here, HD)
    past_values = cache_values.reshape(row_count, depth, heads_here, HD)
    factor = 1.0 / math.sqrt(HD)
    cached = (
        jnp.einsum("rhd,rjhd->rhj", queries, past_keys, preferred_element_type=jnp.float32) * factor
    )
    own_score = (
        jnp.einsum("rhd,rhd->rh", queries, own_keys, preferred_element_type=jnp.float32) * factor
    )
    valid = jnp.arange(depth)[None, None, :] < cache_lengths[:, None, None]
    masked = jnp.where(valid, cached, -1e30)
    highest = jnp.maximum(jnp.max(masked, axis=-1), own_score)
    cached_exp = jnp.where(valid, jnp.exp(masked - highest[..., None]), 0.0)
    own_exp = jnp.exp(own_score - highest)
    total = jnp.sum(cached_exp, axis=-1) + own_exp
    past_weights = (cached_exp / total[..., None]).astype(jnp.bfloat16)
    own_weight = (own_exp / total).astype(jnp.bfloat16)
    attended = jnp.einsum(
        "rhj,rjhd->rhd", past_weights, past_values, preferred_element_type=jnp.float32
    )
    attended = attended + own_weight.astype(jnp.float32)[..., None] * own_values.astype(jnp.float32)
    return (resid.astype(jnp.float32) + attended.reshape(row_count, feature_count)).astype(
        jnp.bfloat16
    )


def expert_layer(states, expert_ids, gates, up_weight, down_weight):
    row_count, feature_count = states.shape
    ep_count = lax.axis_size("ep")
    sharing = ep_count // EXPERTS
    mine = lax.axis_index("ep") // sharing
    wide = states.astype(jnp.float32)
    row_sum, row_square = lax.psum((jnp.sum(wide, axis=1), jnp.sum(wide * wide, axis=1)), "tp")
    center = row_sum / D
    spread = row_square / D - center * center
    normalized = ((wide - center[:, None]) * lax.rsqrt(spread + epsilon)[:, None]).astype(
        jnp.bfloat16
    )
    slots = CAP
    routed = expert_ids[:, 0]
    onehot = (routed[:, None] == jnp.arange(EXPERTS)[None, :]).astype(jnp.int32)
    earlier = jnp.cumsum(onehot, axis=0) - onehot
    rank_in = jnp.sum(earlier * onehot, axis=1)
    position = routed * slots + rank_in
    placing = (position[None, :] == jnp.arange(EXPERTS * slots)[:, None]).astype(jnp.bfloat16)
    compact = jnp.dot(placing, normalized, preferred_element_type=jnp.float32).astype(jnp.bfloat16)
    compact = compact.reshape(EXPERTS, slots, feature_count)
    chosen = lax.dynamic_index_in_dim(
        lax.all_gather(compact[None], "ep", axis=0, tiled=True), mine, axis=1, keepdims=False
    )
    pre = jnp.einsum("scd,df->scf", chosen, up_weight, preferred_element_type=jnp.float32)
    hidden_width = pre.shape[2]
    flat_pre = pre.reshape(ep_count * slots, hidden_width)
    summed = lax.psum(flat_pre, "tp")
    activated = jax.nn.gelu(summed, approximate=True).astype(jnp.bfloat16)
    partial_value = jnp.dot(activated, down_weight, preferred_element_type=jnp.float32)
    returned = lax.all_to_all(
        partial_value.reshape(ep_count, slots, feature_count),
        "ep",
        split_axis=0,
        concat_axis=0,
        tiled=True,
    )
    combined = jnp.sum(returned.reshape(EXPERTS, sharing, slots, feature_count), axis=1)
    combined = combined.reshape(EXPERTS * slots, feature_count)
    produced = jnp.take(combined, position, axis=0)
    return (wide + gates[:, None] * produced).astype(jnp.bfloat16)


def general_body(
    resid,
    query,
    new_key,
    new_value,
    cache_keys,
    cache_values,
    cache_lengths,
    shallow_expert,
    shallow_gate,
    shallow_up,
    shallow_down,
    deep_expert,
    deep_gate,
    deep_up,
    deep_down,
):
    shallow_in = attention(
        resid, query, new_key, new_value, cache_keys, cache_values, cache_lengths
    )
    shallow_out = expert_layer(shallow_in, shallow_expert, shallow_gate, shallow_up, shallow_down)
    return expert_layer(shallow_out, deep_expert, deep_gate, deep_up, deep_down)


SLOTS = EXPERTS * CAP
PAD = 16
TALL = 56
META = 128
MIB = 1 << 20
STEP = 1024
FIRST_SHARE = 0.5
F32 = jnp.float32
BF16 = jnp.bfloat16


def iota(shape, dim):
    return lax.broadcasted_iota(jnp.int32, shape, dim)


def to_column(row, count):
    same = iota((count, count), 0) == iota((count, count), 1)
    return jnp.sum(jnp.where(same, row, jnp.zeros_like(row)), axis=1, keepdims=True)


def to_row(column, count):
    same = iota((count, count), 0) == iota((count, count), 1)
    return jnp.sum(jnp.where(same, column, jnp.zeros_like(column)), axis=0, keepdims=True)


def ranks(id_row, id_column, count):
    earlier = iota((count, count), 1) < iota((count, count), 0)
    same = (id_row == id_column) & earlier
    return jnp.sum(same.astype(jnp.int32), axis=1, keepdims=True)


def split3(value):
    high = value.astype(BF16).astype(F32)
    middle = (value - high).astype(BF16).astype(F32)
    low = (value - high - middle).astype(BF16).astype(F32)
    return high, middle, low


def dot(left, right):
    return jnp.dot(left, right, preferred_element_type=F32)


def params(mib):
    return pltpu.CompilerParams(vmem_limit_bytes=mib * MIB)


def cost(flops, moved):
    return pl.CostEstimate(flops=flops, bytes_accessed=moved, transcendentals=0)


VM = pl.BlockSpec(memory_space=pltpu.VMEM)
SM = pl.BlockSpec(memory_space=pltpu.SMEM)
HB = pl.BlockSpec(memory_space=pltpu.HBM)


def attend_kernel(
    place_ref, resid_in, query_in, key_in, value_in, keys_in, values_in, length_in,
    shallow_in, sgate_in, deep_in, dgate_in, out0, out1, out2, out3, home_ref,
    resid_ref, query_ref, key_ref, value_ref, keys_ref, values_ref, length_ref,
    shallow_ref, sgate_ref, deep_ref, dgate_ref, sems,
):
    rows, features = resid_ref.shape
    depth = keys_ref.shape[1]
    flat = rows * depth
    factor = 1.0 / math.sqrt(HD)
    order = (
        (query_in, query_ref), (keys_in, keys_ref), (key_in, key_ref), (length_in, length_ref),
        (values_in, values_ref), (value_in, value_ref), (resid_in, resid_ref),
        (shallow_in, shallow_ref), (sgate_in, sgate_ref), (deep_in, deep_ref), (dgate_in, dgate_ref),
    )
    copies = [pltpu.make_async_copy(a, b, sems.at[i]) for i, (a, b) in enumerate(order)]
    for copy in copies:
        copy.start()
    spread = (iota((features, META), 0) // HD == iota((features, META), 1)).astype(BF16)
    gather = (iota((META, features), 1) // HD == iota((META, features), 0)).astype(BF16)

    def head_sums(products):
        high = products.astype(BF16)
        low = (products - high.astype(F32)).astype(BF16)
        return dot(high, spread) + dot(low, spread)

    for copy in copies[:4]:
        copy.wait()
    query = query_ref[...].astype(F32)
    own = head_sums(query * key_ref[...].astype(F32)) * factor
    products = query[:, None, :] * keys_ref[...].astype(F32)
    cached = head_sums(products.reshape(flat, features)) * factor
    repeated = iota((flat, rows), 0) // depth == iota((flat, rows), 1)
    length = jnp.sum(jnp.where(repeated, length_ref[...], 0), axis=1, keepdims=True)
    valid = (iota((flat, META), 0) % depth) < length
    masked = jnp.where(valid, cached, -1e30).reshape(rows, depth, META)
    highest = jnp.maximum(jnp.max(masked, axis=1), own)
    past = jnp.exp(masked - highest[:, None, :])
    past = jnp.where(valid, past.reshape(flat, META), 0.0).reshape(rows, depth, META)
    own_exp = jnp.exp(own - highest)
    total = jnp.sum(past, axis=1) + own_exp
    weights = (past / total[:, None, :]).reshape(flat, META).astype(BF16)
    own_weight = (own_exp / total).astype(BF16)
    for copy in copies[4:]:
        copy.wait()
    wide = dot(weights, gather).reshape(rows, depth, features)
    attended = jnp.sum(wide * values_ref[...].astype(F32), axis=1)
    attended = attended + dot(own_weight, gather) * value_ref[...].astype(F32)
    states = (resid_ref[...].astype(F32) + attended).astype(BF16)

    here = place_ref[1]
    shallow = shallow_ref[...]
    deep = deep_ref[...]
    shallow_column = to_column(shallow, rows)
    deep_column = to_column(deep, rows)
    place = (shallow_column ^ here) * PAD + ranks(shallow, shallow_column, rows)
    lane = iota((rows, META), 1)
    notes = jnp.where(lane == 0, deep_column.astype(F32), 0.0)
    deep_rank = ranks(deep, deep_column, rows)
    home_ref[...] = jnp.broadcast_to((deep_column ^ here) * PAD + deep_rank, (rows, META))
    notes = jnp.where(lane == 1, deep_rank.astype(F32), notes)
    for start, gate_ref in ((2, sgate_ref), (5, dgate_ref)):
        for at, piece in enumerate(split3(to_column(gate_ref[...], rows))):
            notes = jnp.where(lane == start + at, piece, notes)
    notes = jnp.where(lane == 8, 1.0, notes)
    full = jnp.concatenate([states, notes.astype(BF16)], axis=1)
    choose = (iota((EXPERTS * PAD, rows), 0) == to_row(place, rows)).astype(BF16)
    sent = dot(choose, full)
    for at, out in enumerate((out0, out1, out2, out3)):
        out[...] = sent[at * PAD : (at + 1) * PAD].astype(BF16)


def attend(place, arrays):
    rows, features = arrays[0].shape
    shape = jax.ShapeDtypeStruct((PAD, features + META), BF16)
    return pl.pallas_call(
        attend_kernel,
        in_specs=[SM] + [HB] * len(arrays),
        out_specs=[VM] * 5,
        out_shape=[shape] * 4 + [jax.ShapeDtypeStruct((rows, META), jnp.int32)],
        scratch_shapes=[pltpu.VMEM(a.shape, a.dtype) for a in arrays]
        + [pltpu.SemaphoreType.DMA((len(arrays),))],
        compiler_params=params(16),
        name="attend",
    )(place, *[pltpu.with_memory_space_constraint(a, pltpu.HBM) for a in arrays])


def load_kernel(weight_ref, after_ref, out_ref, sems):
    count = sems.shape[0]
    rows = weight_ref.shape[0] // count
    copies = [
        pltpu.make_async_copy(
            weight_ref.at[pl.ds(i * rows, rows)], out_ref.at[pl.ds(i * rows, rows)], sems.at[i]
        )
        for i in range(count)
    ]
    for copy in copies:
        copy.start()
    for copy in copies:
        copy.wait()


def load(weights, after):
    return pl.pallas_call(
        load_kernel,
        in_specs=[HB, pl.BlockSpec(memory_space=pl.ANY)],
        out_specs=VM,
        out_shape=jax.ShapeDtypeStruct(weights.shape, weights.dtype),
        scratch_shapes=[pltpu.SemaphoreType.DMA((4,))],
        compiler_params=params(4),
        cost_estimate=cost(0, 2 * weights.size),
        name="load",
    )(pltpu.with_memory_space_constraint(weights, pltpu.HBM), after)


def choose_shallow():
    source = iota((TALL, EXPERTS * PAD), 1)
    kept = jnp.where(source % PAD < CAP, source // PAD * CAP + source % PAD, -1)
    return (kept == iota((TALL, EXPERTS * PAD), 0)).astype(BF16)


def choose_deep(here, held, features):
    notes = held[:, features:].astype(F32)
    count = held.shape[0]
    number = iota((count, 1), 0)
    apart = (number // SLOTS) ^ (number % SLOTS // CAP)
    place = apart * CAP + notes[:, 1:2].astype(jnp.int32)
    mine = (notes[:, 0:1].astype(jnp.int32) == here) & (notes[:, 8:9] > 0.5)
    place = jnp.where(mine, place, -1)
    return (iota((TALL, count), 0) == to_row(place, count)).astype(BF16)


def up_block(rows, means, weights):
    product = dot(rows, weights)
    columns = product[SLOTS : SLOTS + 1]
    row = iota(product.shape, 0)
    centred = product - means * columns
    return row, centred, columns


def cuts_of(half):
    unit = 4 * META
    first = max(unit, int(half * FIRST_SHARE) // unit * unit)
    return (0, first), (first, half - first)


def columns_at(place_ref, weight_ref, own, at, step):
    half = weight_ref.shape[1] // 2
    which = place_ref[0] if own else 1 - place_ref[0]
    return weight_ref[:, pl.ds(pl.multiple_of(which * half + at, 128), step)]


def steps_of(width):
    return [(at, min(STEP, width - at)) for at in range(0, width, STEP)]


def up_first_kernel(deep, cuts, place_ref, h0, h1, h2, h3, weight_ref, rows_ref, stats_ref, *sent):
    features = weight_ref.shape[0]
    held = jnp.concatenate([h0[...], h1[...], h2[...], h3[...]], axis=0)
    choose = choose_deep(place_ref[1], held, features) if deep else choose_shallow()
    picked = dot(choose, held)
    ones = (iota(picked.shape, 0) == SLOTS) & (iota(picked.shape, 1) < features)
    rows_ref[...] = jnp.where(ones, 1.0, picked).astype(BF16)
    wide = picked[:, :features]
    lane = iota((TALL, META), 1)
    total = jnp.sum(wide, axis=1, keepdims=True)
    square = jnp.sum(wide * wide, axis=1, keepdims=True)
    stats_ref[...] = jnp.where(lane == 0, total, jnp.where(lane == 1, square, 0.0))
    means = total / features
    for (start, width), sent_ref in zip(cuts, sent):
        for at, step in steps_of(width):
            weights = columns_at(place_ref, weight_ref, False, start + at, step)
            row, centred, columns = up_block(rows_ref[:, :features], means, weights)
            high = columns.astype(BF16).astype(F32)
            tail = jnp.where(row == SLOTS, high, jnp.where(row == SLOTS + 1, columns - high, 0.0))
            sent_ref[:, at : at + step] = jnp.where(row < SLOTS, centred, tail).astype(BF16)


def up_first(deep, cuts, place, held, weights):
    features, width = weights.shape
    half = width // 2
    return pl.pallas_call(
        functools.partial(up_first_kernel, deep, cuts),
        in_specs=[SM] + [VM] * 5,
        out_specs=[VM] * 4,
        out_shape=[
            jax.ShapeDtypeStruct((TALL, features + META), BF16),
            jax.ShapeDtypeStruct((TALL, META), F32),
        ]
        + [jax.ShapeDtypeStruct((TALL, cut[1]), BF16) for cut in cuts],
        compiler_params=params(8),
        cost_estimate=cost(2 * TALL * features * half, 2 * features * half),
        name="up_first",
    )(place, *held, weights)


def up_second_kernel(start, place_ref, rows_ref, stats_ref, weight_ref, kept_ref):
    features = weight_ref.shape[0]
    means = stats_ref[:, 0:1] / features
    for at, step in steps_of(kept_ref.shape[1]):
        weights = columns_at(place_ref, weight_ref, True, start + at, step)
        row, centred, columns = up_block(rows_ref[:, :features], means, weights)
        kept_ref[:, at : at + step] = jnp.where(
            row < SLOTS, centred, jnp.where(row == SLOTS, columns, 0.0)
        )


def up_second(place, rows, stats, weights, cut):
    start, width = cut
    features = weights.shape[0]
    return pl.pallas_call(
        functools.partial(up_second_kernel, start),
        in_specs=[SM] + [VM] * 3,
        out_specs=VM,
        out_shape=jax.ShapeDtypeStruct((TALL, width), F32),
        compiler_params=params(8),
        cost_estimate=cost(2 * TALL * features * width, 2 * features * width),
        name="up_second",
    )(place, rows, stats, weights)


def merge_into(features, source, width, got_ref, stats, other, sum_ref, sent_ref):
    apart = (stats[:, 0:1] - other[:, 0:1]) * (0.5 / features)
    held = jnp.zeros((SLOTS, META), F32)
    slot = iota((SLOTS, META), 0)
    for at, step in steps_of(width):
        kept = source(at, step)
        got = got_ref[:, at : at + step].astype(F32)
        mine = kept[SLOTS : SLOTS + 1]
        theirs = got[SLOTS : SLOTS + 1] + got[SLOTS + 1 : SLOTS + 2]
        row = iota(kept.shape, 0)
        columns = mine + theirs
        merged = jnp.where(row < SLOTS, kept + got + apart * (mine - theirs), columns)
        sum_ref[:, at : at + step] = merged
        sent_ref[:, at : at + step] = merged[:SLOTS].astype(BF16)
        for part in range(0, step, META):
            held = jnp.where(slot == (at + part) // META, columns[:, part : part + META], held)
    sent_ref[:, width : width + META] = held.astype(BF16)


def merge_kernel(features, kept_ref, got_ref, stats_ref, got_stats_ref, sent_ref, sum_ref, sums_ref):
    width = kept_ref.shape[1]
    stats, other = stats_ref[...], got_stats_ref[...]
    sums = stats + other
    sums_ref[...] = sums
    source = lambda at, step: kept_ref[:, at : at + step]
    merge_into(features, source, width, got_ref, stats, other, sum_ref, sent_ref)
    lane = iota((SLOTS, META), 1)
    packed = jnp.zeros((SLOTS, META), F32)
    for which in range(2):
        for at, piece in enumerate(split3(sums[:SLOTS, which : which + 1])):
            packed = jnp.where(lane == 3 * which + at, piece, packed)
    sent_ref[:, width + META :] = packed.astype(BF16)


def merge(features, kept, got, stats, got_stats):
    width = kept.shape[1]
    return pl.pallas_call(
        functools.partial(merge_kernel, features),
        in_specs=[VM] * 4,
        out_specs=[VM] * 3,
        out_shape=[
            jax.ShapeDtypeStruct((SLOTS, width + 2 * META), BF16),
            jax.ShapeDtypeStruct((TALL, width), F32),
            jax.ShapeDtypeStruct((TALL, META), F32),
        ],
        compiler_params=params(8),
        name="merge",
    )(kept, got, stats, got_stats)


def up_merge_kernel(
    start, place_ref, rows_ref, stats_ref, got_stats_ref, weight_ref, got_ref, sent_ref, sum_ref
):
    features = weight_ref.shape[0]
    stats = stats_ref[...]
    means = stats[:, 0:1] / features

    def source(at, step):
        weights = columns_at(place_ref, weight_ref, True, start + at, step)
        row, centred, columns = up_block(rows_ref[:, :features], means, weights)
        return jnp.where(row < SLOTS, centred, jnp.where(row == SLOTS, columns, 0.0))

    merge_into(features, source, sum_ref.shape[1], got_ref, stats, got_stats_ref[...], sum_ref, sent_ref)


def up_merge(place, rows, stats, got_stats, weights, got, cut):
    start, width = cut
    features = weights.shape[0]
    return pl.pallas_call(
        functools.partial(up_merge_kernel, start),
        in_specs=[SM] + [VM] * 5,
        out_specs=[VM] * 2,
        out_shape=[
            jax.ShapeDtypeStruct((SLOTS, width + META), BF16),
            jax.ShapeDtypeStruct((TALL, width), F32),
        ],
        compiler_params=params(8),
        cost_estimate=cost(2 * TALL * features * width, 2 * features * width),
        name="up_merge",
    )(place, rows, stats, got_stats, weights, got)


def hidden_kernel(features, sum_ref, sums_ref, got_ref, packed_ref, hidden_ref):
    width = sum_ref.shape[1]
    packed = packed_ref[:, packed_ref.shape[1] - META :].astype(F32)
    held = got_ref[:, width : width + META].astype(F32)
    theirs_total = packed[:, 0:1] + packed[:, 1:2] + packed[:, 2:3]
    theirs_square = packed[:, 3:4] + packed[:, 4:5] + packed[:, 5:6]
    total, square = sums_ref[:SLOTS, 0:1], sums_ref[:SLOTS, 1:2]
    apart = (total - theirs_total) * (0.5 / (2 * features))
    center = (total + theirs_total) / D
    spread = (square + theirs_square) / D - center * center
    scale = lax.rsqrt(spread + epsilon)
    step = 4 * META
    for at in range(0, width, step):
        mine = sum_ref[:, at : at + step]
        got = got_ref[:, at : at + step].astype(F32)
        first = at // META
        theirs = jnp.concatenate([held[i : i + 1] for i in range(first, first + step // META)], axis=1)
        columns = mine[SLOTS : SLOTS + 1] - theirs
        pre = (mine[:SLOTS] + got + apart * columns) * scale
        hidden_ref[:, at : at + step] = jax.nn.gelu(pre, approximate=True).astype(BF16)


def hidden_units(features, total, sums, got, packed):
    return pl.pallas_call(
        functools.partial(hidden_kernel, features),
        in_specs=[VM] * 4,
        out_specs=VM,
        out_shape=jax.ShapeDtypeStruct((SLOTS, total.shape[1]), BF16),
        compiler_params=params(8),
        cost_estimate=cost(1, 1),
        name="hidden",
    )(total, sums, got, packed)


def rows_at(place_ref, weight_ref, own, start, width):
    half = weight_ref.shape[0] // 2
    which = place_ref[0] if own else 1 - place_ref[0]
    return weight_ref[pl.ds(pl.multiple_of(which * half + start, 128), width), :]


def down_part_kernel(own, start, place_ref, hidden_ref, weight_ref, *rest):
    *earlier, out_ref = rest
    product = dot(hidden_ref[...], rows_at(place_ref, weight_ref, own, start, hidden_ref.shape[1]))
    for part in earlier:
        product = product + part[...]
    out_ref[...] = product


def down_part(place, hidden, weights, own, cut, *earlier):
    start, width = cut
    features = weights.shape[1]
    return pl.pallas_call(
        functools.partial(down_part_kernel, own, start),
        in_specs=[SM] + [VM] * (2 + len(earlier)),
        out_specs=VM,
        out_shape=jax.ShapeDtypeStruct((SLOTS, features), F32),
        compiler_params=params(8),
        cost_estimate=cost(1, 1),
        name="down_part",
    )(place, hidden, weights, *earlier)


def down_last_kernel(deep, start, place_ref, part_ref, rows_ref, hidden_ref, weight_ref, *outs):
    features = weight_ref.shape[1]
    weights = rows_at(place_ref, weight_ref, False, start, hidden_ref.shape[1])
    total = part_ref[...] + dot(hidden_ref[...], weights)
    rows = rows_ref[...].astype(F32)[:SLOTS]
    notes = rows[:, features:]
    first = 5 if deep else 2
    gate = notes[:, first : first + 1] + notes[:, first + 1 : first + 2]
    gate = gate + notes[:, first + 2 : first + 3]
    result = rows[:, :features] + gate * total
    if not deep:
        outs[0][...] = jnp.concatenate([result, notes], axis=1).astype(BF16)
    else:
        target = iota((EXPERTS * PAD, SLOTS), 0)
        kept = jnp.where(target % PAD < CAP, target // PAD * CAP + target % PAD, -1)
        spread = (kept == iota((EXPERTS * PAD, SLOTS), 1)).astype(BF16)
        placed = dot(spread, result.astype(BF16))
        for at, out in enumerate(outs):
            out[...] = placed[at * PAD : (at + 1) * PAD].astype(BF16)


def down_last(deep, place, part, rows, hidden, weights, cut):
    start, width = cut
    features = weights.shape[1]
    shapes = [(PAD, features)] * EXPERTS if deep else [(SLOTS, features + META)]
    return pl.pallas_call(
        functools.partial(down_last_kernel, deep, start),
        in_specs=[SM] + [VM] * 4,
        out_specs=[VM] * len(shapes),
        out_shape=[jax.ShapeDtypeStruct(shape, BF16) for shape in shapes],
        compiler_params=params(8),
        cost_estimate=cost(2 * SLOTS * features * width, 2 * features * width),
        name="down_last",
    )(place, part, rows, hidden, weights)


def finish_kernel(home_ref, g0, g1, g2, g3, out_ref):
    rows = out_ref.shape[0]
    choose = (iota((rows, EXPERTS * PAD), 1) == home_ref[:, 0:1]).astype(BF16)
    held = jnp.concatenate([g0[...], g1[...], g2[...], g3[...]], axis=0)
    out_ref[...] = dot(choose, held).astype(BF16)


def finish(home, got):
    return pl.pallas_call(
        finish_kernel,
        in_specs=[VM] * 5,
        out_specs=VM,
        out_shape=jax.ShapeDtypeStruct((home.shape[0], got[0].shape[1]), BF16),
        compiler_params=params(8),
        name="finish",
    )(home, *got)


def swap(value, axis, apart):
    count = lax.axis_size(axis)
    return lax.ppermute(value, axis, [(i, i ^ apart) for i in range(count)])


def swap_all(blocks):
    return [blocks[0]] + [swap(blocks[k], "ep", k) for k in (1, 2, 3)]


def after(value, earlier):
    return lax.optimization_barrier((value, earlier))[0]


def expert_block(deep, place, held, up, down):
    features, width = up.shape
    first, second = cuts = cuts_of(width // 2)
    rows, stats, sent_a, sent_b = up_first(deep, cuts, place, held, up)
    got_a, got_stats = swap(sent_a, "tp", 1), swap(stats, "tp", 1)
    got_b = swap(sent_b, "tp", 1)
    kept = up_second(place, rows, stats, up, first)
    sent_a, total_a, sums = merge(features, kept, got_a, stats, got_stats)
    over_a = swap(sent_a, "tp", 2)
    later = after(rows, sent_a)
    sent_b, total_b = up_merge(place, later, stats, got_stats, up, got_b, second)
    over_b = swap(sent_b, "tp", 2)
    hidden_a = hidden_units(features, after(total_a, sent_b), sums, over_a, over_a)
    other_a = swap(hidden_a, "tp", 1)
    part = down_part(place, hidden_a, down, True, first)
    part = down_part(place, other_a, down, False, first, part)
    hidden_b = hidden_units(features, after(total_b, part), sums, over_b, over_a)
    other_b = swap(hidden_b, "tp", 1)
    part = down_part(place, hidden_b, down, True, second, part)
    return down_last(deep, place, part, rows, other_b, down, second)


def fast_body(
    resid,
    query,
    new_key,
    new_value,
    cache_keys,
    cache_values,
    cache_lengths,
    shallow_expert,
    shallow_gate,
    shallow_up,
    shallow_down,
    deep_expert,
    deep_gate,
    deep_up,
    deep_down,
):
    rows = resid.shape[0]
    place = jnp.stack([lax.axis_index("tp") % 2, lax.axis_index("ep")]).astype(jnp.int32)
    *blocks, home = attend(
        place,
        (
            resid,
            query,
            new_key,
            new_value,
            cache_keys,
            cache_values,
            cache_lengths.reshape(1, rows),
            shallow_expert.reshape(1, rows),
            shallow_gate.reshape(1, rows),
            deep_expert.reshape(1, rows),
            deep_gate.reshape(1, rows),
        ),
    )
    weights = load(shallow_up, blocks[0])
    (between,) = expert_block(False, place, swap_all(blocks), weights, shallow_down)
    blocks = expert_block(True, place, swap_all([between] * EXPERTS), deep_up, deep_down)
    return finish(home, swap_all(blocks))


def solution(mesh):
    fits = mesh.shape["ep"] == EXPERTS and mesh.shape["tp"] == 4
    return jax.shard_map(
        fast_body if fits else general_body,
        mesh=mesh,
        in_specs=(
            P(("groups", "ep"), "tp"),
            P(("groups", "ep"), "tp"),
            P(("groups", "ep"), "tp"),
            P(("groups", "ep"), "tp"),
            P(("groups", "ep"), None, "tp"),
            P(("groups", "ep"), None, "tp"),
            P(("groups", "ep")),
            P(("groups", "ep"), None),
            P(("groups", "ep")),
            P("tp", "ep"),
            P("ep", "tp"),
            P(("groups", "ep"), None),
            P(("groups", "ep")),
            P("tp", "ep"),
            P("ep", "tp"),
        ),
        out_specs=P(("groups", "ep"), "tp"),
        check_vma=False,
    )
```

time: 118 us -> 78.4 us (0.66)
  Pallas kernels: 50.6 us -> 33.4 us
  waiting for transfers between devices: 39 us -> 23.7 us
  local copies, waits for them, and re-layouts: 8.72 us -> 0.07 us
  starting transfers between devices: 19 us -> 20.5 us
    pallas_call x10 -> x17, Pallas kernels: 49 us -> 31.7 us  [the longest x6 8.26 us: down_part(): pl.pallas_call(functools.partial(down_part_kernel, own, start), in_specs=...]
    ppermute x17 -> x23, waiting for transfers between devices: 39 us -> 23.7 us  [swap(): return lax.ppermute(value, axis, [(i, i ^ apart) for i in range(count)])]
    unnamed x24, local copies, waits for them, and re-layouts: 8.72 us -> 0.07 us
    ppermute x17 -> x23, starting transfers between devices: 19 us -> 20.5 us  [swap(): return lax.ppermute(value, axis, [(i, i ^ apart) for i in range(count)])]
  transfers between devices with their start and end apart: 17 -> 23, of which waited for: 8 -> 8; matrix products, arithmetic and copies ran while one was open for 0% -> 0% of each run, Pallas kernels for 19% -> 27%
where the time goes in v2:
time: 78.4 us; the launch traced here: 78.3 us
  Pallas kernels  33.4 us (43%)
  waiting for transfers between devices  23.7 us (30%)
  starting transfers between devices  20.5 us (26%)
    ppermute x23, waiting for transfers between devices, swap(): return lax.ppermute(value, axis, [(i, i ^ apart) for i in range(count)])  23.7 us
    ppermute x23, starting transfers between devices, swap(): return lax.ppermute(value, axis, [(i, i ^ apart) for i in range(count)])  20.5 us
    pallas_call x6, Pallas kernels, down_part(): pl.pallas_call(functools.partial(down_part_kernel, own, start), in_specs=...  8.26 us
    pallas_call x1, Pallas kernels, load(): pl.pallas_call(load_kernel, in_specs=[HB, pl.BlockSpec(memory_space=pl.AN...  5.89 us
    pallas_call x2, Pallas kernels, up_first(): pl.pallas_call(functools.partial(up_first_kernel, deep, cuts), in_specs=[...  4.89 us
    pallas_call x1, Pallas kernels, attend(): pl.pallas_call(attend_kernel, in_specs=[SM] + [HB] * len(arrays), out_spe...  3.08 us
    pallas_call x2, Pallas kernels, up_merge(): pl.pallas_call(functools.partial(up_merge_kernel, start), in_specs=[SM] +...  2.95 us
    pallas_call x2, Pallas kernels, down_last(): pl.pallas_call(functools.partial(down_last_kernel, deep, start), in_specs...  2.94 us
  transfers between devices with their start and end apart: 23, of which 8 were waited for; matrix products, arithmetic and copies ran while one was open for 0% of the time, Pallas kernels for 27%

profile of v2, /device:TPU:0, one launch (start us, length us, event | category | flops | bytes accessed | tf_op | source)
XLA Modules:
  0.0 78.3 jit_solution(6262933819099060021)
XLA Ops:
  0.1 3.1 %attend.1 = (bf16[16,1152]{1,0:T(8,128)(2,1)S(1)}, bf16[16,1152]{1,0:T(8,128)(2,1)S(1)}, bf16[16,1152]{1,0:T(8,128)(2,1)S(1)}, bf16[16,1152]{1,0:T(8,128)(2,1)S(1)}, s32[32,128]{1,0:T(8,128)S(1)}) custom-call(s32[2]{0:T(128)S(1)} %pad_add_fusion.place_ref, bf16[32,1024]{1,0:T(8,128)(2,1)} %resid_in.1, bf16[32,1024]{1,0:T(8,128)(2,1)} %query_in.1, ...), custom_call_target="tpu_custom_call" | custom-call | tf_op jit(solution)/shard_map/attend/pallas_call | solution.py:250
  3.2 3.1 %collective-permute-start = (bf16[16,1152]{1,0:T(8,128)(2,1)S(1)}, bf16[16,1152]{1,0:T(8,128)(2,1)S(1)}, u32[]{:S(2)}, u32[]{:S(2)}) collective-permute-start(bf16[16,1152]{1,0:T(8,128)(2,1)S(1)} %get-tuple-element.40), channel_id=1, source_target_pairs={{0,4},{4,0},{8,12},{12,8},{1,5},{5,1},{9,13},{13,9},{2,6},{6,2},{1... | collective-permute-start | bytes 110600 | tf_op jit(solution)/shard_map/ppermute | solution.py:596
  6.2 2.6 %collective-permute-start.1 = (bf16[16,1152]{1,0:T(8,128)(2,1)S(1)}, bf16[16,1152]{1,0:T(8,128)(2,1)S(1)}, u32[]{:S(2)}, u32[]{:S(2)}) collective-permute-start(bf16[16,1152]{1,0:T(8,128)(2,1)S(1)} %get-tuple-element.41), channel_id=1, source_target_pairs={{0,8},{4,12},{8,0},{12,4},{1,9},{5,13},{9,1},{13,5},{2,10},{6,14},... | collective-permute-start | bytes 110600 | tf_op jit(solution)/shard_map/ppermute | solution.py:596
  8.8 5.9 %load.1.weight_ref = bf16[1024,8192]{1,0:T(8,128)(2,1)S(1)} custom-call(bf16[1024,8192]{1,0:T(8,128)(2,1)} %weight_ref.12, bf16[16,1152]{1,0:T(8,128)(2,1)S(1)} %get-tuple-element.39.after_ref.h0), custom_call_target="tpu_custom_call" | custom-call | bytes 16777216 | tf_op jit(solution)/shard_map/load/pallas_call | solution.py:278
  14.8 2.3 %up_first.2 = (bf16[56,1152]{1,0:T(8,128)(2,1)S(1)}, f32[56,128]{1,0:T(8,128)S(1)}, bf16[56,2048]{1,0:T(8,128)(2,1)S(1)}, bf16[56,2048]{1,0:T(8,128)(2,1)S(1)}) custom-call(s32[2]{0:T(128)S(1)} %pad_add_fusion.place_ref, bf16[16,1152]{1,0:T(8,128)(2,1)S(1)} %get-tuple-element.39.after_ref.h0, bf16[16,1152]{1,0:T(8,128)(2,1)S(1)} %collective-permute-done.h1, ...), custom_call_target="tpu_custom_call" | custom-call | flops 469762048 | bytes 8388608 | tf_op jit(solution)/shard_map/up_first/pallas_call | solution.py:356
  17.7 1.4 %up_second.2.kept_ref = f32[56,2048]{1,0:T(8,128)S(1)} custom-call(s32[2]{0:T(128)S(1)} %pad_add_fusion.place_ref, bf16[56,1152]{1,0:T(8,128)(2,1)S(1)} %get-tuple-element.47.rows_ref, f32[56,128]{1,0:T(8,128)S(1)} %get-tuple-element.44.stats_ref, bf16[1024,8192]{1,0:T(8,128)(2,1)S(1)} %load.1.weight_ref), custom_call_target="tpu_custom_call" | custom-call | flops 234881024 | bytes 4194304 | tf_op jit(solution)/shard_map/up_second/pallas_call | solution.py:385
  19.3 1.8 %collective-permute-start.6 = (bf16[48,2304]{1,0:T(8,128)(2,1)S(1)}, bf16[48,2304]{1,0:T(8,128)(2,1)S(1)}, u32[]{:S(2)}, u32[]{:S(2)}) collective-permute-start(bf16[48,2304]{1,0:T(8,128)(2,1)S(1)} %get-tuple-element.46), channel_id=1, source_target_pairs={{0,2},{1,3},{2,0},{3,1},{4,6},{5,7},{6,4},{7,5},{8,10},{9,11},{10,... | collective-permute-start | bytes 663560 | tf_op jit(solution)/shard_map/ppermute | solution.py:596
  21.1 1.5 %up_merge.2 = (bf16[48,2176]{1,0:T(8,128)(2,1)S(1)}, f32[56,2048]{1,0:T(8,128)S(1)}) custom-call(s32[2]{0:T(128)S(1)} %pad_add_fusion.place_ref, bf16[56,1152]{1,0:T(8,128)(2,1)S(1)} %get-tuple-element.47.rows_ref, f32[56,128]{1,0:T(8,128)S(1)} %get-tuple-element.44.stats_ref, f32[56,128]{1,0:T(8,128)S(1)} %collective-permute-done.4.got_stats_ref, ...), custom_call_target="tpu_custom_call" | custom-call | flops 234881024 | bytes 4194304 | tf_op jit(solution)/shard_map/up_merge/pallas_call | solution.py:464
  23.0 4.7 %collective-permute-done.6.got_ref.packed_ref = bf16[48,2304]{1,0:T(8,128)(2,1)S(1)} collective-permute-done((bf16[48,2304]{1,0:T(8,128)(2,1)S(1)}, bf16[48,2304]{1,0:T(8,128)(2,1)S(1)}, u32[]{:S(2)}, u32[]{:S(2)}) %collective-permute-start.6) | collective-permute-done | bytes 221216 | tf_op jit(solution)/shard_map/ppermute | solution.py:596
  28.1 1.4 %down_part.6.rest_0_ = f32[48,1024]{1,0:T(8,128)S(1)} custom-call(s32[2]{0:T(128)S(1)} %pad_add_fusion.place_ref, bf16[48,2048]{1,0:T(8,128)(2,1)S(1)} %hidden.4.hidden_ref, bf16[8192,1024]{1,0:T(8,128)(2,1)S(1)} %bitcast.8), custom_call_target="tpu_custom_call" | custom-call | flops 1 | bytes 1 | tf_op jit(solution)/shard_map/down_part/pallas_call | solution.py:529
  29.5 1.4 %down_part.7.rest_0_ = f32[48,1024]{1,0:T(8,128)S(1)} custom-call(s32[2]{0:T(128)S(1)} %pad_add_fusion.place_ref, bf16[48,2048]{1,0:T(8,128)(2,1)S(1)} %collective-permute-done.7.hidden_ref, bf16[8192,1024]{1,0:T(8,128)(2,1)S(1)} %bitcast.8, f32[48,1024]{1,0:T(8,128)S(1)} %down_part.6.rest_0_), custom_call_target="tpu_custom_call" | custom-call | flops 1 | bytes 1 | tf_op jit(solution)/shard_map/down_part/pallas_call | solution.py:529
  30.9 0.7 collective-permute-done.8.got_ref
  32.1 1.4 %down_part.8.part_ref = f32[48,1024]{1,0:T(8,128)S(1)} custom-call(s32[2]{0:T(128)S(1)} %pad_add_fusion.place_ref, bf16[48,2048]{1,0:T(8,128)(2,1)S(1)} %hidden.5.hidden_ref, bf16[8192,1024]{1,0:T(8,128)(2,1)S(1)} %bitcast.8, f32[48,1024]{1,0:T(8,128)S(1)} %down_part.7.rest_0_), custom_call_target="tpu_custom_call" | custom-call | flops 1 | bytes 1 | tf_op jit(solution)/shard_map/down_part/pallas_call | solution.py:529
  33.6 1.4 %down_last.2.h0 = bf16[48,1152]{1,0:T(8,128)(2,1)S(1)} custom-call(s32[2]{0:T(128)S(1)} %pad_add_fusion.place_ref, f32[48,1024]{1,0:T(8,128)S(1)} %down_part.8.part_ref, bf16[56,1152]{1,0:T(8,128)(2,1)S(1)} %get-tuple-element.47.rows_ref, bf16[48,2048]{1,0:T(8,128)(2,1)S(1)} %collective-permute-done.9.hidden_ref, bf16[8192,1024]{1,0:T(8,128)(2,1)S(1)} %bitcast.8), custom_call_target="tpu_custom_call" | custom-call | flops 201326592 | bytes 4194304 | tf_op jit(solution)/shard_map/down_last/pallas_call | solution.py:565
  35.0 3.9 %collective-permute-start.12 = (bf16[48,1152]{1,0:T(8,128)(2,1)S(1)}, bf16[48,1152]{1,0:T(8,128)(2,1)S(1)}, u32[]{:S(2)}, u32[]{:S(2)}) collective-permute-start(bf16[48,1152]{1,0:T(8,128)(2,1)S(1)} %down_last.2.h0), channel_id=1, source_target_pairs={{0,12},{4,8},{8,4},{12,0},{1,13},{5,9},{9,5},{13,1},{2,14},{6,10},... | collective-permute-start | bytes 331784 | tf_op jit(solution)/shard_map/ppermute | solution.py:596
  39.5 3.4 %collective-permute-done.12.h3 = bf16[48,1152]{1,0:T(8,128)(2,1)S(1)} collective-permute-done((bf16[48,1152]{1,0:T(8,128)(2,1)S(1)}, bf16[48,1152]{1,0:T(8,128)(2,1)S(1)}, u32[]{:S(2)}, u32[]{:S(2)}) %collective-permute-start.12) | collective-permute-done | bytes 110624 | tf_op jit(solution)/shard_map/ppermute | solution.py:596
  42.9 5.1 %collective-permute-done.11.h2 = bf16[48,1152]{1,0:T(8,128)(2,1)S(1)} collective-permute-done((bf16[48,1152]{1,0:T(8,128)(2,1)S(1)}, bf16[48,1152]{1,0:T(8,128)(2,1)S(1)}, u32[]{:S(2)}, u32[]{:S(2)}) %collective-permute-start.11) | collective-permute-done | bytes 110624 | tf_op jit(solution)/shard_map/ppermute | solution.py:596
  48.0 2.6 %up_first.3 = (bf16[56,1152]{1,0:T(8,128)(2,1)S(1)}, f32[56,128]{1,0:T(8,128)S(1)}, bf16[56,2048]{1,0:T(8,128)(2,1)S(1)}, bf16[56,2048]{1,0:T(8,128)(2,1)S(1)}) custom-call(s32[2]{0:T(128)S(1)} %pad_add_fusion.place_ref, bf16[48,1152]{1,0:T(8,128)(2,1)S(1)} %down_last.2.h0, bf16[48,1152]{1,0:T(8,128)(2,1)S(1)} %collective-permute-done.10.h1, ...), custom_call_target="tpu_custom_call" | custom-call | flops 469762048 | bytes 8388608 | tf_op jit(solution)/shard_map/up_first/pallas_call | solution.py:356
  51.2 1.4 %up_second.3.kept_ref = f32[56,2048]{1,0:T(8,128)S(1)} custom-call(s32[2]{0:T(128)S(1)} %pad_add_fusion.place_ref, bf16[56,1152]{1,0:T(8,128)(2,1)S(1)} %get-tuple-element.59.rows_ref, f32[56,128]{1,0:T(8,128)S(1)} %get-tuple-element.56.stats_ref, bf16[1024,8192]{1,0:T(8,128)(2,1)S(1)} %bitcast.12), custom_call_target="tpu_custom_call" | custom-call | flops 234881024 | bytes 4194304 | tf_op jit(solution)/shard_map/up_second/pallas_call | solution.py:385
  52.8 1.6 %collective-permute-start.16 = (bf16[48,2304]{1,0:T(8,128)(2,1)S(1)}, bf16[48,2304]{1,0:T(8,128)(2,1)S(1)}, u32[]{:S(2)}, u32[]{:S(2)}) collective-permute-start(bf16[48,2304]{1,0:T(8,128)(2,1)S(1)} %get-tuple-element.58), channel_id=1, source_target_pairs={{0,2},{1,3},{2,0},{3,1},{4,6},{5,7},{6,4},{7,5},{8,10},{9,11},{10,... | collective-permute-start | bytes 663560 | tf_op jit(solution)/shard_map/ppermute | solution.py:596
  54.4 1.5 %up_merge.3 = (bf16[48,2176]{1,0:T(8,128)(2,1)S(1)}, f32[56,2048]{1,0:T(8,128)S(1)}) custom-call(s32[2]{0:T(128)S(1)} %pad_add_fusion.place_ref, bf16[56,1152]{1,0:T(8,128)(2,1)S(1)} %get-tuple-element.59.rows_ref, f32[56,128]{1,0:T(8,128)S(1)} %get-tuple-element.56.stats_ref, f32[56,128]{1,0:T(8,128)S(1)} %collective-permute-done.14.got_stats_ref, ...), custom_call_target="tpu_custom_call" | custom-call | flops 234881024 | bytes 4194304 | tf_op jit(solution)/shard_map/up_merge/pallas_call | solution.py:464
  56.5 4.7 %collective-permute-done.16.got_ref.packed_ref = bf16[48,2304]{1,0:T(8,128)(2,1)S(1)} collective-permute-done((bf16[48,2304]{1,0:T(8,128)(2,1)S(1)}, bf16[48,2304]{1,0:T(8,128)(2,1)S(1)}, u32[]{:S(2)}, u32[]{:S(2)}) %collective-permute-start.16) | collective-permute-done | bytes 221216 | tf_op jit(solution)/shard_map/ppermute | solution.py:596
  61.6 1.4 %down_part.9.rest_0_ = f32[48,1024]{1,0:T(8,128)S(1)} custom-call(s32[2]{0:T(128)S(1)} %pad_add_fusion.place_ref, bf16[48,2048]{1,0:T(8,128)(2,1)S(1)} %hidden.6.hidden_ref, bf16[8192,1024]{1,0:T(8,128)(2,1)S(1)} %bitcast.10), custom_call_target="tpu_custom_call" | custom-call | flops 1 | bytes 1 | tf_op jit(solution)/shard_map/down_part/pallas_call | solution.py:529
  63.0 1.4 %down_part.10.rest_0_ = f32[48,1024]{1,0:T(8,128)S(1)} custom-call(s32[2]{0:T(128)S(1)} %pad_add_fusion.place_ref, bf16[48,2048]{1,0:T(8,128)(2,1)S(1)} %collective-permute-done.17.hidden_ref, bf16[8192,1024]{1,0:T(8,128)(2,1)S(1)} %bitcast.10, f32[48,1024]{1,0:T(8,128)S(1)} %down_part.9.rest_0_), custom_call_target="tpu_custom_call" | custom-call | flops 1 | bytes 1 | tf_op jit(solution)/shard_map/down_part/pallas_call | solution.py:529
  65.6 1.4 %down_part.11.part_ref = f32[48,1024]{1,0:T(8,128)S(1)} custom-call(s32[2]{0:T(128)S(1)} %pad_add_fusion.place_ref, bf16[48,2048]{1,0:T(8,128)(2,1)S(1)} %hidden.7.hidden_ref, bf16[8192,1024]{1,0:T(8,128)(2,1)S(1)} %bitcast.10, f32[48,1024]{1,0:T(8,128)S(1)} %down_part.10.rest_0_), custom_call_target="tpu_custom_call" | custom-call | flops 1 | bytes 1 | tf_op jit(solution)/shard_map/down_part/pallas_call | solution.py:529
  67.0 1.5 %down_last.3 = (bf16[16,1024]{1,0:T(8,128)(2,1)S(1)}, bf16[16,1024]{1,0:T(8,128)(2,1)S(1)}, bf16[16,1024]{1,0:T(8,128)(2,1)S(1)}, bf16[16,1024]{1,0:T(8,128)(2,1)S(1)}) custom-call(s32[2]{0:T(128)S(1)} %pad_add_fusion.place_ref, f32[48,1024]{1,0:T(8,128)S(1)} %down_part.11.part_ref, bf16[56,1152]{1,0:T(8,128)(2,1)S(1)} %get-tuple-element.59.rows_ref, ...), custom_call_target="tpu_custom_call" | custom-call | flops 201326592 | bytes 4194304 | tf_op jit(solution)/shard_map/down_last/pallas_call | solution.py:565
  68.6 1.3 %collective-permute-start.20 = (bf16[16,1024]{1,0:T(8,128)(2,1)S(1)}, bf16[16,1024]{1,0:T(8,128)(2,1)S(1)}, u32[]{:S(2)}, u32[]{:S(2)}) collective-permute-start(bf16[16,1024]{1,0:T(8,128)(2,1)S(1)} %get-tuple-element.68), channel_id=1, source_target_pairs={{0,4},{4,0},{8,12},{12,8},{1,5},{5,1},{9,13},{13,9},{2,6},{6,2},{1... | collective-permute-start | bytes 98312 | tf_op jit(solution)/shard_map/ppermute | solution.py:596
  69.8 1.9 %collective-permute-start.21 = (bf16[16,1024]{1,0:T(8,128)(2,1)S(1)}, bf16[16,1024]{1,0:T(8,128)(2,1)S(1)}, u32[]{:S(2)}, u32[]{:S(2)}) collective-permute-start(bf16[16,1024]{1,0:T(8,128)(2,1)S(1)} %get-tuple-element.69), channel_id=1, source_target_pairs={{0,8},{4,12},{8,0},{12,4},{1,9},{5,13},{9,1},{13,5},{2,10},{6,14},... | collective-permute-start | bytes 98312 | tf_op jit(solution)/shard_map/ppermute | solution.py:596
  71.7 1.3 %collective-permute-start.22 = (bf16[16,1024]{1,0:T(8,128)(2,1)S(1)}, bf16[16,1024]{1,0:T(8,128)(2,1)S(1)}, u32[]{:S(2)}, u32[]{:S(2)}) collective-permute-start(bf16[16,1024]{1,0:T(8,128)(2,1)S(1)} %get-tuple-element.70), channel_id=1, source_target_pairs={{0,12},{4,8},{8,4},{12,0},{1,13},{5,9},{9,5},{13,1},{2,14},{6,10},... | collective-permute-start | bytes 98312 | tf_op jit(solution)/shard_map/ppermute | solution.py:596
  73.0 2.2 %collective-permute-done.21.g2 = bf16[16,1024]{1,0:T(8,128)(2,1)S(1)} collective-permute-done((bf16[16,1024]{1,0:T(8,128)(2,1)S(1)}, bf16[16,1024]{1,0:T(8,128)(2,1)S(1)}, u32[]{:S(2)}, u32[]{:S(2)}) %collective-permute-start.21) | collective-permute-done | bytes 32800 | tf_op jit(solution)/shard_map/ppermute | solution.py:596
  75.3 2.2 %collective-permute-done.22.g3 = bf16[16,1024]{1,0:T(8,128)(2,1)S(1)} collective-permute-done((bf16[16,1024]{1,0:T(8,128)(2,1)S(1)}, bf16[16,1024]{1,0:T(8,128)(2,1)S(1)}, u32[]{:S(2)}, u32[]{:S(2)}) %collective-permute-start.22) | collective-permute-done | bytes 32800 | tf_op jit(solution)/shard_map/ppermute | solution.py:596
  77.4 0.8 %finish.1 = bf16[32,1024]{1,0:T(8,128)(2,1)} custom-call(s32[32,128]{1,0:T(8,128)S(1)} %get-tuple-element.38.home_ref, bf16[16,1024]{1,0:T(8,128)(2,1)S(1)} %get-tuple-element.67.g0, bf16[16,1024]{1,0:T(8,128)(2,1)S(1)} %collective-permute-done.20.g1, bf16[16,1024]{1,0:T(8,128)(2,1)S(1)} %collective-permute-done.21.g2, ...), custom_call_target="tpu_custom_call" | custom-call | tf_op jit(solution)/shard_map/finish/pallas_call | solution.py:584
  (65 shorter events, 5.9 us)
Async XLA Ops:
  3.2 11.6 %collective-permute-start = (bf16[16,1152]{1,0:T(8,128)(2,1)S(1)}, bf16[16,1152]{1,0:T(8,128)(2,1)S(1)}, u32[]{:S(2)}, u32[]{:S(2)}) collective-permute-start(bf16[16,1152]{1,0:T(8,128)(2,1)S(1)} %get-tuple-element.40), channel_id=1, source_target_pairs={{0,4},{4,0},{8,12},{12,8},{1,5},{5,1},{9,13},{13,9},{2,6},{6,2},{1... | collective-permute-start | bytes 110600 | tf_op jit(solution)/shard_map/ppermute | solution.py:596
  6.2 8.5 %collective-permute-start.1 = (bf16[16,1152]{1,0:T(8,128)(2,1)S(1)}, bf16[16,1152]{1,0:T(8,128)(2,1)S(1)}, u32[]{:S(2)}, u32[]{:S(2)}) collective-permute-start(bf16[16,1152]{1,0:T(8,128)(2,1)S(1)} %get-tuple-element.41), channel_id=1, source_target_pairs={{0,8},{4,12},{8,0},{12,4},{1,9},{5,13},{9,1},{13,5},{2,10},{6,14},... | collective-permute-start | bytes 110600 | tf_op jit(solution)/shard_map/ppermute | solution.py:596
  8.8 5.9 %collective-permute-start.2 = (bf16[16,1152]{1,0:T(8,128)(2,1)S(1)}, bf16[16,1152]{1,0:T(8,128)(2,1)S(1)}, u32[]{:S(2)}, u32[]{:S(2)}) collective-permute-start(bf16[16,1152]{1,0:T(8,128)(2,1)S(1)} %get-tuple-element.42), channel_id=1, source_target_pairs={{0,12},{4,8},{8,4},{12,0},{1,13},{5,9},{9,5},{13,1},{2,14},{6,10},... | collective-permute-start | bytes 110600 | tf_op jit(solution)/shard_map/ppermute | solution.py:596
  17.1 2.1 %collective-permute-start.3 = (bf16[56,2048]{1,0:T(8,128)(2,1)S(1)}, bf16[56,2048]{1,0:T(8,128)(2,1)S(1)}, u32[]{:S(2)}, u32[]{:S(2)}) collective-permute-start(bf16[56,2048]{1,0:T(8,128)(2,1)S(1)} %get-tuple-element.45), channel_id=1, source_target_pairs={{0,1},{1,0},{2,3},{3,2},{4,5},{5,4},{6,7},{7,6},{8,9},{9,8},{10,11... | collective-permute-start | bytes 688136 | tf_op jit(solution)/shard_map/ppermute | solution.py:596
  17.2 3.9 %collective-permute-start.5 = (bf16[56,2048]{1,0:T(8,128)(2,1)S(1)}, bf16[56,2048]{1,0:T(8,128)(2,1)S(1)}, u32[]{:S(2)}, u32[]{:S(2)}) collective-permute-start(bf16[56,2048]{1,0:T(8,128)(2,1)S(1)} %get-tuple-element.48), channel_id=1, source_target_pairs={{0,1},{1,0},{2,3},{3,2},{4,5},{5,4},{6,7},{7,6},{8,9},{9,8},{10,11... | collective-permute-start | bytes 688136 | tf_op jit(solution)/shard_map/ppermute | solution.py:596
  17.7 1.5 %collective-permute-start.4 = (f32[56,128]{1,0:T(8,128)S(1)}, f32[56,128]{1,0:T(8,128)S(1)}, u32[]{:S(2)}, u32[]{:S(2)}) collective-permute-start(f32[56,128]{1,0:T(8,128)S(1)} %get-tuple-element.44.stats_ref), channel_id=1, source_target_pairs={{0,1},{1,0},{2,3},{3,2},{4,5},{5,4},{6,7},{7,6},{8,9},{9,8},{10,11... | collective-permute-start | bytes 86024 | tf_op jit(solution)/shard_map/ppermute | solution.py:596
  17.7 10.4 %slice-start = ((s8[16777216]{0:T(1024)(128)(4,1)}), s8[4194304]{0:T(1024)(128)(4,1)S(1)}, s32[]{:S(2)}) async-start(s8[16777216]{0:T(1024)(128)(4,1)} %bitcast.7), calls=%async_computation | async-start | bytes 8388608
  17.7 10.4 %slice-start.1 = ((s8[16777216]{0:T(1024)(128)(4,1)}), s8[4194304]{0:T(1024)(128)(4,1)S(1)}, s32[]{:S(2)}) async-start(s8[16777216]{0:T(1024)(128)(4,1)} %bitcast.7), calls=%async_computation.1 | async-start | bytes 8388608
  19.3 8.8 %slice-start.2 = ((s8[16777216]{0:T(1024)(128)(4,1)}), s8[4194304]{0:T(1024)(128)(4,1)S(1)}, s32[]{:S(2)}) async-start(s8[16777216]{0:T(1024)(128)(4,1)} %bitcast.7), calls=%async_computation.2 | async-start | bytes 8388608
  19.3 8.3 %collective-permute-start.6 = (bf16[48,2304]{1,0:T(8,128)(2,1)S(1)}, bf16[48,2304]{1,0:T(8,128)(2,1)S(1)}, u32[]{:S(2)}, u32[]{:S(2)}) collective-permute-start(bf16[48,2304]{1,0:T(8,128)(2,1)S(1)} %get-tuple-element.46), channel_id=1, source_target_pairs={{0,2},{1,3},{2,0},{3,1},{4,6},{5,7},{6,4},{7,5},{8,10},{9,11},{10,... | collective-permute-start | bytes 663560 | tf_op jit(solution)/shard_map/ppermute | solution.py:596
  22.6 9.1 %collective-permute-start.8 = (bf16[48,2176]{1,0:T(8,128)(2,1)S(1)}, bf16[48,2176]{1,0:T(8,128)(2,1)S(1)}, u32[]{:S(2)}, u32[]{:S(2)}) collective-permute-start(bf16[48,2176]{1,0:T(8,128)(2,1)S(1)} %get-tuple-element.51), channel_id=1, source_target_pairs={{0,2},{1,3},{2,0},{3,1},{4,6},{5,7},{6,4},{7,5},{8,10},{9,11},{10,... | collective-permute-start | bytes 626696 | tf_op jit(solution)/shard_map/ppermute | solution.py:596
  28.0 1.5 %collective-permute-start.7 = (bf16[48,2048]{1,0:T(8,128)(2,1)S(1)}, bf16[48,2048]{1,0:T(8,128)(2,1)S(1)}, u32[]{:S(2)}, u32[]{:S(2)}) collective-permute-start(bf16[48,2048]{1,0:T(8,128)(2,1)S(1)} %hidden.4.hidden_ref), channel_id=1, source_target_pairs={{0,1},{1,0},{2,3},{3,2},{4,5},{5,4},{6,7},{7,6},{8,9},{9,8},{10,11... | collective-permute-start | bytes 589832 | tf_op jit(solution)/shard_map/ppermute | solution.py:596
  32.0 15.9 %slice-start.8 = ((s8[16777216]{0:T(1024)(128)(4,1)}), s8[4194304]{0:T(1024)(128)(4,1)S(1)}, s32[]{:S(2)}) async-start(s8[16777216]{0:T(1024)(128)(4,1)} %bitcast.11), calls=%async_computation.8 | async-start | bytes 8388608
  32.1 15.9 %slice-start.9 = ((s8[16777216]{0:T(1024)(128)(4,1)}), s8[4194304]{0:T(1024)(128)(4,1)S(1)}, s32[]{:S(2)}) async-start(s8[16777216]{0:T(1024)(128)(4,1)} %bitcast.11), calls=%async_computation.9 | async-start | bytes 8388608
  32.1 1.5 %collective-permute-start.9 = (bf16[48,2048]{1,0:T(8,128)(2,1)S(1)}, bf16[48,2048]{1,0:T(8,128)(2,1)S(1)}, u32[]{:S(2)}, u32[]{:S(2)}) collective-permute-start(bf16[48,2048]{1,0:T(8,128)(2,1)S(1)} %hidden.5.hidden_ref), channel_id=1, source_target_pairs={{0,1},{1,0},{2,3},{3,2},{4,5},{5,4},{6,7},{7,6},{8,9},{9,8},{10,11... | collective-permute-start | bytes 589832 | tf_op jit(solution)/shard_map/ppermute | solution.py:596
  33.5 14.4 %slice-start.10 = ((s8[16777216]{0:T(1024)(128)(4,1)}), s8[4194304]{0:T(1024)(128)(4,1)S(1)}, s32[]{:S(2)}) async-start(s8[16777216]{0:T(1024)(128)(4,1)} %bitcast.11), calls=%async_computation.10 | async-start | bytes 8388608
  33.5 14.4 %slice-start.11 = ((s8[16777216]{0:T(1024)(128)(4,1)}), s8[4194304]{0:T(1024)(128)(4,1)S(1)}, s32[]{:S(2)}) async-start(s8[16777216]{0:T(1024)(128)(4,1)} %bitcast.11), calls=%async_computation.11 | async-start | bytes 8388608
  35.0 7.9 %collective-permute-start.12 = (bf16[48,1152]{1,0:T(8,128)(2,1)S(1)}, bf16[48,1152]{1,0:T(8,128)(2,1)S(1)}, u32[]{:S(2)}, u32[]{:S(2)}) collective-permute-start(bf16[48,1152]{1,0:T(8,128)(2,1)S(1)} %down_last.2.h0), channel_id=1, source_target_pairs={{0,12},{4,8},{8,4},{12,0},{1,13},{5,9},{9,5},{13,1},{2,14},{6,10},... | collective-permute-start | bytes 331784 | tf_op jit(solution)/shard_map/ppermute | solution.py:596
  38.9 9.1 %collective-permute-start.11 = (bf16[48,1152]{1,0:T(8,128)(2,1)S(1)}, bf16[48,1152]{1,0:T(8,128)(2,1)S(1)}, u32[]{:S(2)}, u32[]{:S(2)}) collective-permute-start(bf16[48,1152]{1,0:T(8,128)(2,1)S(1)} %down_last.2.h0), channel_id=1, source_target_pairs={{0,8},{4,12},{8,0},{12,4},{1,9},{5,13},{9,1},{13,5},{2,10},{6,14},... | collective-permute-start | bytes 331784 | tf_op jit(solution)/shard_map/ppermute | solution.py:596
  38.9 9.1 %collective-permute-start.10 = (bf16[48,1152]{1,0:T(8,128)(2,1)S(1)}, bf16[48,1152]{1,0:T(8,128)(2,1)S(1)}, u32[]{:S(2)}, u32[]{:S(2)}) collective-permute-start(bf16[48,1152]{1,0:T(8,128)(2,1)S(1)} %down_last.2.h0), channel_id=1, source_target_pairs={{0,4},{4,0},{8,12},{12,8},{1,5},{5,1},{9,13},{13,9},{2,6},{6,2},{1... | collective-permute-start | bytes 331784 | tf_op jit(solution)/shard_map/ppermute | solution.py:596
  50.6 2.1 %collective-permute-start.13 = (bf16[56,2048]{1,0:T(8,128)(2,1)S(1)}, bf16[56,2048]{1,0:T(8,128)(2,1)S(1)}, u32[]{:S(2)}, u32[]{:S(2)}) collective-permute-start(bf16[56,2048]{1,0:T(8,128)(2,1)S(1)} %get-tuple-element.57), channel_id=1, source_target_pairs={{0,1},{1,0},{2,3},{3,2},{4,5},{5,4},{6,7},{7,6},{8,9},{9,8},{10,11... | collective-permute-start | bytes 688136 | tf_op jit(solution)/shard_map/ppermute | solution.py:596
  50.6 3.7 %collective-permute-start.15 = (bf16[56,2048]{1,0:T(8,128)(2,1)S(1)}, bf16[56,2048]{1,0:T(8,128)(2,1)S(1)}, u32[]{:S(2)}, u32[]{:S(2)}) collective-permute-start(bf16[56,2048]{1,0:T(8,128)(2,1)S(1)} %get-tuple-element.60), channel_id=1, source_target_pairs={{0,1},{1,0},{2,3},{3,2},{4,5},{5,4},{6,7},{7,6},{8,9},{9,8},{10,11... | collective-permute-start | bytes 688136 | tf_op jit(solution)/shard_map/ppermute | solution.py:596
  51.1 1.5 %collective-permute-start.14 = (f32[56,128]{1,0:T(8,128)S(1)}, f32[56,128]{1,0:T(8,128)S(1)}, u32[]{:S(2)}, u32[]{:S(2)}) collective-permute-start(f32[56,128]{1,0:T(8,128)S(1)} %get-tuple-element.56.stats_ref), channel_id=1, source_target_pairs={{0,1},{1,0},{2,3},{3,2},{4,5},{5,4},{6,7},{7,6},{8,9},{9,8},{10,11... | collective-permute-start | bytes 86024 | tf_op jit(solution)/shard_map/ppermute | solution.py:596
  51.2 10.4 %slice-start.4 = ((s8[16777216]{0:T(1024)(128)(4,1)}), s8[4194304]{0:T(1024)(128)(4,1)S(1)}, s32[]{:S(2)}) async-start(s8[16777216]{0:T(1024)(128)(4,1)} %bitcast.9), calls=%async_computation.4 | async-start | bytes 8388608
  51.2 10.4 %slice-start.5 = ((s8[16777216]{0:T(1024)(128)(4,1)}), s8[4194304]{0:T(1024)(128)(4,1)S(1)}, s32[]{:S(2)}) async-start(s8[16777216]{0:T(1024)(128)(4,1)} %bitcast.9), calls=%async_computation.5 | async-start | bytes 8388608
  52.8 8.3 %collective-permute-start.16 = (bf16[48,2304]{1,0:T(8,128)(2,1)S(1)}, bf16[48,2304]{1,0:T(8,128)(2,1)S(1)}, u32[]{:S(2)}, u32[]{:S(2)}) collective-permute-start(bf16[48,2304]{1,0:T(8,128)(2,1)S(1)} %get-tuple-element.58), channel_id=1, source_target_pairs={{0,2},{1,3},{2,0},{3,1},{4,6},{5,7},{6,4},{7,5},{8,10},{9,11},{10,... | collective-permute-start | bytes 663560 | tf_op jit(solution)/shard_map/ppermute | solution.py:596
  55.9 9.3 %collective-permute-start.18 = (bf16[48,2176]{1,0:T(8,128)(2,1)S(1)}, bf16[48,2176]{1,0:T(8,128)(2,1)S(1)}, u32[]{:S(2)}, u32[]{:S(2)}) collective-permute-start(bf16[48,2176]{1,0:T(8,128)(2,1)S(1)} %get-tuple-element.63), channel_id=1, source_target_pairs={{0,2},{1,3},{2,0},{3,1},{4,6},{5,7},{6,4},{7,5},{8,10},{9,11},{10,... | collective-permute-start | bytes 626696 | tf_op jit(solution)/shard_map/ppermute | solution.py:596
  61.5 1.5 %collective-permute-start.17 = (bf16[48,2048]{1,0:T(8,128)(2,1)S(1)}, bf16[48,2048]{1,0:T(8,128)(2,1)S(1)}, u32[]{:S(2)}, u32[]{:S(2)}) collective-permute-start(bf16[48,2048]{1,0:T(8,128)(2,1)S(1)} %hidden.6.hidden_ref), channel_id=1, source_target_pairs={{0,1},{1,0},{2,3},{3,2},{4,5},{5,4},{6,7},{7,6},{8,9},{9,8},{10,11... | collective-permute-start | bytes 589832 | tf_op jit(solution)/shard_map/ppermute | solution.py:596
  65.5 1.5 %collective-permute-start.19 = (bf16[48,2048]{1,0:T(8,128)(2,1)S(1)}, bf16[48,2048]{1,0:T(8,128)(2,1)S(1)}, u32[]{:S(2)}, u32[]{:S(2)}) collective-permute-start(bf16[48,2048]{1,0:T(8,128)(2,1)S(1)} %hidden.7.hidden_ref), channel_id=1, source_target_pairs={{0,1},{1,0},{2,3},{3,2},{4,5},{5,4},{6,7},{7,6},{8,9},{9,8},{10,11... | collective-permute-start | bytes 589832 | tf_op jit(solution)/shard_map/ppermute | solution.py:596
  68.6 4.5 %collective-permute-start.20 = (bf16[16,1024]{1,0:T(8,128)(2,1)S(1)}, bf16[16,1024]{1,0:T(8,128)(2,1)S(1)}, u32[]{:S(2)}, u32[]{:S(2)}) collective-permute-start(bf16[16,1024]{1,0:T(8,128)(2,1)S(1)} %get-tuple-element.68), channel_id=1, source_target_pairs={{0,4},{4,0},{8,12},{12,8},{1,5},{5,1},{9,13},{13,9},{2,6},{6,2},{1... | collective-permute-start | bytes 98312 | tf_op jit(solution)/shard_map/ppermute | solution.py:596
  69.8 5.4 %collective-permute-start.21 = (bf16[16,1024]{1,0:T(8,128)(2,1)S(1)}, bf16[16,1024]{1,0:T(8,128)(2,1)S(1)}, u32[]{:S(2)}, u32[]{:S(2)}) collective-permute-start(bf16[16,1024]{1,0:T(8,128)(2,1)S(1)} %get-tuple-element.69), channel_id=1, source_target_pairs={{0,8},{4,12},{8,0},{12,4},{1,9},{5,13},{9,1},{13,5},{2,10},{6,14},... | collective-permute-start | bytes 98312 | tf_op jit(solution)/shard_map/ppermute | solution.py:596
  71.7 5.7 %collective-permute-start.22 = (bf16[16,1024]{1,0:T(8,128)(2,1)S(1)}, bf16[16,1024]{1,0:T(8,128)(2,1)S(1)}, u32[]{:S(2)}, u32[]{:S(2)}) collective-permute-start(bf16[16,1024]{1,0:T(8,128)(2,1)S(1)} %get-tuple-element.70), channel_id=1, source_target_pairs={{0,12},{4,8},{8,4},{12,0},{1,13},{5,9},{9,5},{13,1},{2,14},{6,10},... | collective-permute-start | bytes 98312 | tf_op jit(solution)/shard_map/ppermute | solution.py:596
  (3 other events, 26.4 us)

commit v3 on v2

--- a/solution.py
+++ b/solution.py
@@ -155,6 +155,10 @@
     return high, middle, low
 
 
+def core_here():
+    return lax.axis_index("tp") & 1
+
+
 def dot(left, right):
     return jnp.dot(left, right, preferred_element_type=F32)
 
@@ -168,12 +172,11 @@
 
 
 VM = pl.BlockSpec(memory_space=pltpu.VMEM)
-SM = pl.BlockSpec(memory_space=pltpu.SMEM)
 HB = pl.BlockSpec(memory_space=pltpu.HBM)
 
 
 def attend_kernel(
-    place_ref, resid_in, query_in, key_in, value_in, keys_in, values_in, length_in,
+    resid_in, query_in, key_in, value_in, keys_in, values_in, length_in,
     shallow_in, sgate_in, deep_in, dgate_in, out0, out1, out2, out3, home_ref,
     resid_ref, query_ref, key_ref, value_ref, keys_ref, values_ref, length_ref,
     shallow_ref, sgate_ref, deep_ref, dgate_ref, sems,
@@ -222,7 +225,7 @@
     attended = attended + dot(own_weight, gather) * value_ref[...].astype(F32)
     states = (resid_ref[...].astype(F32) + attended).astype(BF16)
 
-    here = place_ref[1]
+    here = lax.axis_index("ep")
     shallow = shallow_ref[...]
     deep = deep_ref[...]
     shallow_column = to_column(shallow, rows)
@@ -244,19 +247,19 @@
         out[...] = sent[at * PAD : (at + 1) * PAD].astype(BF16)
 
 
-def attend(place, arrays):
+def attend(arrays):
     rows, features = arrays[0].shape
     shape = jax.ShapeDtypeStruct((PAD, features + META), BF16)
     return pl.pallas_call(
         attend_kernel,
-        in_specs=[SM] + [HB] * len(arrays),
+        in_specs=[HB] * len(arrays),
         out_specs=[VM] * 5,
         out_shape=[shape] * 4 + [jax.ShapeDtypeStruct((rows, META), jnp.int32)],
         scratch_shapes=[pltpu.VMEM(a.shape, a.dtype) for a in arrays]
         + [pltpu.SemaphoreType.DMA((len(arrays),))],
         compiler_params=params(16),
         name="attend",
-    )(place, *[pltpu.with_memory_space_constraint(a, pltpu.HBM) for a in arrays])
+    )(*[pltpu.with_memory_space_constraint(a, pltpu.HBM) for a in arrays])
 
 
 def load_kernel(weight_ref, after_ref, out_ref, sems):
@@ -318,9 +321,9 @@
     return (0, first), (first, half - first)
 
 
-def columns_at(place_ref, weight_ref, own, at, step):
+def columns_at(weight_ref, own, at, step):
     half = weight_ref.shape[1] // 2
-    which = place_ref[0] if own else 1 - place_ref[0]
+    which = core_here() if own else 1 - core_here()
     return weight_ref[:, pl.ds(pl.multiple_of(which * half + at, 128), step)]
 
 
@@ -328,10 +331,10 @@
     return [(at, min(STEP, width - at)) for at in range(0, width, STEP)]
 
 
-def up_first_kernel(deep, cuts, place_ref, h0, h1, h2, h3, weight_ref, rows_ref, stats_ref, *sent):
+def up_first_kernel(deep, cuts, h0, h1, h2, h3, weight_ref, rows_ref, stats_ref, *sent):
     features = weight_ref.shape[0]
     held = jnp.concatenate([h0[...], h1[...], h2[...], h3[...]], axis=0)
-    choose = choose_deep(place_ref[1], held, features) if deep else choose_shallow()
+    choose = choose_deep(lax.axis_index("ep"), held, features) if deep else choose_shallow()
     picked = dot(choose, held)
     ones = (iota(picked.shape, 0) == SLOTS) & (iota(picked.shape, 1) < features)
     rows_ref[...] = jnp.where(ones, 1.0, picked).astype(BF16)
@@ -343,19 +346,19 @@
     means = total / features
     for (start, width), sent_ref in zip(cuts, sent):
         for at, step in steps_of(width):
-            weights = columns_at(place_ref, weight_ref, False, start + at, step)
+            weights = columns_at(weight_ref, False, start + at, step)
             row, centred, columns = up_block(rows_ref[:, :features], means, weights)
             high = columns.astype(BF16).astype(F32)
             tail = jnp.where(row == SLOTS, high, jnp.where(row == SLOTS + 1, columns - high, 0.0))
             sent_ref[:, at : at + step] = jnp.where(row < SLOTS, centred, tail).astype(BF16)
 
 
-def up_first(deep, cuts, place, held, weights):
+def up_first(deep, cuts, held, weights):
     features, width = weights.shape
     half = width // 2
     return pl.pallas_call(
         functools.partial(up_first_kernel, deep, cuts),
-        in_specs=[SM] + [VM] * 5,
+        in_specs=[VM] * 5,
         out_specs=[VM] * 4,
         out_shape=[
             jax.ShapeDtypeStruct((TALL, features + META), BF16),
@@ -365,32 +368,32 @@
         compiler_params=params(8),
         cost_estimate=cost(2 * TALL * features * half, 2 * features * half),
         name="up_first",
-    )(place, *held, weights)
-
-
-def up_second_kernel(start, place_ref, rows_ref, stats_ref, weight_ref, kept_ref):
+    )(*held, weights)
+
+
+def up_second_kernel(start, rows_ref, stats_ref, weight_ref, kept_ref):
     features = weight_ref.shape[0]
     means = stats_ref[:, 0:1] / features
     for at, step in steps_of(kept_ref.shape[1]):
-        weights = columns_at(place_ref, weight_ref, True, start + at, step)
+        weights = columns_at(weight_ref, True, start + at, step)
         row, centred, columns = up_block(rows_ref[:, :features], means, weights)
         kept_ref[:, at : at + step] = jnp.where(
             row < SLOTS, centred, jnp.where(row == SLOTS, columns, 0.0)
         )
 
 
-def up_second(place, rows, stats, weights, cut):
+def up_second(rows, stats, weights, cut):
     start, width = cut
     features = weights.shape[0]
     return pl.pallas_call(
         functools.partial(up_second_kernel, start),
-        in_specs=[SM] + [VM] * 3,
+        in_specs=[VM] * 3,
         out_specs=VM,
         out_shape=jax.ShapeDtypeStruct((TALL, width), F32),
         compiler_params=params(8),
         cost_estimate=cost(2 * TALL * features * width, 2 * features * width),
         name="up_second",
-    )(place, rows, stats, weights)
+    )(rows, stats, weights)
 
 
 def merge_into(features, source, width, got_ref, stats, other, sum_ref, sent_ref):
@@ -444,26 +447,26 @@
 
 
 def up_merge_kernel(
-    start, place_ref, rows_ref, stats_ref, got_stats_ref, weight_ref, got_ref, sent_ref, sum_ref
+    start, rows_ref, stats_ref, got_stats_ref, weight_ref, got_ref, sent_ref, sum_ref
 ):
     features = weight_ref.shape[0]
     stats = stats_ref[...]
     means = stats[:, 0:1] / features
 
     def source(at, step):
-        weights = columns_at(place_ref, weight_ref, True, start + at, step)
+        weights = columns_at(weight_ref, True, start + at, step)
         row, centred, columns = up_block(rows_ref[:, :features], means, weights)
         return jnp.where(row < SLOTS, centred, jnp.where(row == SLOTS, columns, 0.0))
 
     merge_into(features, source, sum_ref.shape[1], got_ref, stats, got_stats_ref[...], sum_ref, sent_ref)
 
 
-def up_merge(place, rows, stats, got_stats, weights, got, cut):
+def up_merge(rows, stats, got_stats, weights, got, cut):
     start, width = cut
     features = weights.shape[0]
     return pl.pallas_call(
         functools.partial(up_merge_kernel, start),
-        in_specs=[SM] + [VM] * 5,
+        in_specs=[VM] * 5,
         out_specs=[VM] * 2,
         out_shape=[
             jax.ShapeDtypeStruct((SLOTS, width + META), BF16),
@@ -472,7 +475,7 @@
         compiler_params=params(8),
         cost_estimate=cost(2 * TALL * features * width, 2 * features * width),
         name="up_merge",
-    )(place, rows, stats, got_stats, weights, got)
+    )(rows, stats, got_stats, weights, got)
 
 
 def hidden_kernel(features, sum_ref, sums_ref, got_ref, packed_ref, hidden_ref):
@@ -509,37 +512,37 @@
     )(total, sums, got, packed)
 
 
-def rows_at(place_ref, weight_ref, own, start, width):
+def rows_at(weight_ref, own, start, width):
     half = weight_ref.shape[0] // 2
-    which = place_ref[0] if own else 1 - place_ref[0]
+    which = core_here() if own else 1 - core_here()
     return weight_ref[pl.ds(pl.multiple_of(which * half + start, 128), width), :]
 
 
-def down_part_kernel(own, start, place_ref, hidden_ref, weight_ref, *rest):
+def down_part_kernel(own, start, hidden_ref, weight_ref, *rest):
     *earlier, out_ref = rest
-    product = dot(hidden_ref[...], rows_at(place_ref, weight_ref, own, start, hidden_ref.shape[1]))
+    product = dot(hidden_ref[...], rows_at(weight_ref, own, start, hidden_ref.shape[1]))
     for part in earlier:
         product = product + part[...]
     out_ref[...] = product
 
 
-def down_part(place, hidden, weights, own, cut, *earlier):
+def down_part(hidden, weights, own, cut, *earlier):
     start, width = cut
     features = weights.shape[1]
     return pl.pallas_call(
         functools.partial(down_part_kernel, own, start),
-        in_specs=[SM] + [VM] * (2 + len(earlier)),
+        in_specs=[VM] * (2 + len(earlier)),
         out_specs=VM,
         out_shape=jax.ShapeDtypeStruct((SLOTS, features), F32),
         compiler_params=params(8),
         cost_estimate=cost(1, 1),
         name="down_part",
-    )(place, hidden, weights, *earlier)
-
-
-def down_last_kernel(deep, start, place_ref, part_ref, rows_ref, hidden_ref, weight_ref, *outs):
+    )(hidden, weights, *earlier)
+
+
+def down_last_kernel(deep, start, part_ref, rows_ref, hidden_ref, weight_ref, *outs):
     features = weight_ref.shape[1]
-    weights = rows_at(place_ref, weight_ref, False, start, hidden_ref.shape[1])
+    weights = rows_at(weight_ref, False, start, hidden_ref.shape[1])
     total = part_ref[...] + dot(hidden_ref[...], weights)
     rows = rows_ref[...].astype(F32)[:SLOTS]
     notes = rows[:, features:]
@@ -558,19 +561,19 @@
             out[...] = placed[at * PAD : (at + 1) * PAD].astype(BF16)
 
 
-def down_last(deep, place, part, rows, hidden, weights, cut):
+def down_last(deep, part, rows, hidden, weights, cut):
     start, width = cut
     features = weights.shape[1]
     shapes = [(PAD, features)] * EXPERTS if deep else [(SLOTS, features + META)]
     return pl.pallas_call(
         functools.partial(down_last_kernel, deep, start),
-        in_specs=[SM] + [VM] * 4,
+        in_specs=[VM] * 4,
         out_specs=[VM] * len(shapes),
         out_shape=[jax.ShapeDtypeStruct(shape, BF16) for shape in shapes],
         compiler_params=params(8),
         cost_estimate=cost(2 * SLOTS * features * width, 2 * features * width),
         name="down_last",
-    )(place, part, rows, hidden, weights)
+    )(part, rows, hidden, weights)
 
 
 def finish_kernel(home_ref, g0, g1, g2, g3, out_ref):
@@ -604,26 +607,26 @@
     return lax.optimization_barrier((value, earlier))[0]
 
 
-def expert_block(deep, place, held, up, down):
+def expert_block(deep, held, up, down):
     features, width = up.shape
     first, second = cuts = cuts_of(width // 2)
-    rows, stats, sent_a, sent_b = up_first(deep, cuts, place, held, up)
+    rows, stats, sent_a, sent_b = up_first(deep, cuts, held, up)
     got_a, got_stats = swap(sent_a, "tp", 1), swap(stats, "tp", 1)
     got_b = swap(sent_b, "tp", 1)
-    kept = up_second(place, rows, stats, up, first)
+    kept = up_second(rows, stats, up, first)
     sent_a, total_a, sums = merge(features, kept, got_a, stats, got_stats)
     over_a = swap(sent_a, "tp", 2)
     later = after(rows, sent_a)
-    sent_b, total_b = up_merge(place, later, stats, got_stats, up, got_b, second)
+    sent_b, total_b = up_merge(later, stats, got_stats, up, got_b, second)
     over_b = swap(sent_b, "tp", 2)
     hidden_a = hidden_units(features, after(total_a, sent_b), sums, over_a, over_a)
     other_a = swap(hidden_a, "tp", 1)
-    part = down_part(place, hidden_a, down, True, first)
-    part = down_part(place, other_a, down, False, first, part)
+    part = down_part(hidden_a, down, True, first)
+    part = down_part(other_a, down, False, first, part)
     hidden_b = hidden_units(features, after(total_b, part), sums, over_b, over_a)
     other_b = swap(hidden_b, "tp", 1)
-    part = down_part(place, hidden_b, down, True, second, part)
-    return down_last(deep, place, part, rows, other_b, down, second)
+    part = down_part(hidden_b, down, True, second, part)
+    return down_last(deep, part, rows, other_b, down, second)
 
 
 def fast_body(
@@ -644,9 +647,7 @@
     deep_down,
 ):
     rows = resid.shape[0]
-    place = jnp.stack([lax.axis_index("tp") % 2, lax.axis_index("ep")]).astype(jnp.int32)
     *blocks, home = attend(
-        place,
         (
             resid,
             query,
@@ -662,8 +663,8 @@
         ),
     )
     weights = load(shallow_up, blocks[0])
-    (between,) = expert_block(False, place, swap_all(blocks), weights, shallow_down)
-    blocks = expert_block(True, place, swap_all([between] * EXPERTS), deep_up, deep_down)
+    (between,) = expert_block(False, swap_all(blocks), weights, shallow_down)
+    blocks = expert_block(True, swap_all([between] * EXPERTS), load(deep_up, between), deep_down)
     return finish(home, swap_all(blocks))
 
 

time: 78.4 us -> 74.3 us (0.948)
  Pallas kernels: 33.4 us -> 31.2 us
  waiting for transfers between devices: 23.7 us -> 22 us
    pallas_call x1 -> x2, Pallas kernels: 5.89 us -> 11.8 us  [load(): pl.pallas_call(load_kernel, in_specs=[HB, pl.BlockSpec(memory_space=pl.AN...]
    pallas_call x6, Pallas kernels: 8.26 us -> 5.03 us  [down_part(): pl.pallas_call(functools.partial(down_part_kernel, own, start), in_specs=...]
    pallas_call x5, Pallas kernels: 8.85 us -> 6.14 us  [the longest x1 2.54 us: attend(): pl.pallas_call(attend_kernel, in_specs=[HB] * len(arrays), out_specs=[VM]...]
    ppermute x23, waiting for transfers between devices: 23.7 us -> 22 us  [swap(): return lax.ppermute(value, axis, [(i, i ^ apart) for i in range(count)])]
    pallas_call x2, Pallas kernels: 2.94 us -> 1.86 us  [down_last(): pl.pallas_call(functools.partial(down_last_kernel, deep, start), in_specs...]
    pallas_call x2, Pallas kernels: 4.89 us -> 3.83 us  [up_first(): pl.pallas_call(functools.partial(up_first_kernel, deep, cuts), in_specs=[...]
  transfers between devices with their start and end apart: 23 -> 23, of which waited for: 8 -> 13; matrix products, arithmetic and copies ran while one was open for 0% -> 0% of each run, Pallas kernels for 27% -> 29%
where the time goes in v3:
time: 74.3 us; the launch traced here: 74.2 us
  Pallas kernels  31.2 us (42%)
  waiting for transfers between devices  22 us (30%)
  starting transfers between devices  20.6 us (28%)
    ppermute x23, waiting for transfers between devices, swap(): return lax.ppermute(value, axis, [(i, i ^ apart) for i in range(count)])  22 us
    ppermute x23, starting transfers between devices, swap(): return lax.ppermute(value, axis, [(i, i ^ apart) for i in range(count)])  20.6 us
    pallas_call x2, Pallas kernels, load(): pl.pallas_call(load_kernel, in_specs=[HB, pl.BlockSpec(memory_space=pl.AN...  11.8 us
    pallas_call x6, Pallas kernels, down_part(): pl.pallas_call(functools.partial(down_part_kernel, own, start), in_specs=...  5.03 us
    pallas_call x2, Pallas kernels, up_first(): pl.pallas_call(functools.partial(up_first_kernel, deep, cuts), in_specs=[...  3.83 us
    pallas_call x1, Pallas kernels, attend(): pl.pallas_call(attend_kernel, in_specs=[HB] * len(arrays), out_specs=[VM]...  2.54 us
    pallas_call x2, Pallas kernels, down_last(): pl.pallas_call(functools.partial(down_last_kernel, deep, start), in_specs...  1.86 us
    pallas_call x2, Pallas kernels, up_merge(): pl.pallas_call(functools.partial(up_merge_kernel, start), in_specs=[VM] *...  1.85 us
  transfers between devices with their start and end apart: 23, of which 13 were waited for; matrix products, arithmetic and copies ran while one was open for 0% of the time, Pallas kernels for 29%

profile of v3, /device:TPU:0, one launch (start us, length us, event | category | flops | bytes accessed | tf_op | source)
XLA Modules:
  0.0 74.2 jit_solution(1465967710520823742)
XLA Ops:
  0.0 2.5 %attend.1 = (bf16[16,1152]{1,0:T(8,128)(2,1)S(1)}, bf16[16,1152]{1,0:T(8,128)(2,1)S(1)}, bf16[16,1152]{1,0:T(8,128)(2,1)S(1)}, bf16[16,1152]{1,0:T(8,128)(2,1)S(1)}, s32[32,128]{1,0:T(8,128)S(1)}) custom-call(bf16[32,1024]{1,0:T(8,128)(2,1)} %resid_in.1, bf16[32,1024]{1,0:T(8,128)(2,1)} %query_in.1, bf16[32,1024]{1,0:T(8,128)(2,1)} %key_in.1, ...), custom_call_target="tpu_custom_call" | custom-call | tf_op jit(solution)/shard_map/attend/pallas_call | solution.py:253
  2.5 3.1 %collective-permute-start = (bf16[16,1152]{1,0:T(8,128)(2,1)S(1)}, bf16[16,1152]{1,0:T(8,128)(2,1)S(1)}, u32[]{:S(2)}, u32[]{:S(2)}) collective-permute-start(bf16[16,1152]{1,0:T(8,128)(2,1)S(1)} %get-tuple-element.40), channel_id=1, source_target_pairs={{0,4},{4,0},{8,12},{12,8},{1,5},{5,1},{9,13},{13,9},{2,6},{6,2},{1... | collective-permute-start | bytes 110600 | tf_op jit(solution)/shard_map/ppermute | solution.py:599
  5.6 2.6 %collective-permute-start.1 = (bf16[16,1152]{1,0:T(8,128)(2,1)S(1)}, bf16[16,1152]{1,0:T(8,128)(2,1)S(1)}, u32[]{:S(2)}, u32[]{:S(2)}) collective-permute-start(bf16[16,1152]{1,0:T(8,128)(2,1)S(1)} %get-tuple-element.41), channel_id=1, source_target_pairs={{0,8},{4,12},{8,0},{12,4},{1,9},{5,13},{9,1},{13,5},{2,10},{6,14},... | collective-permute-start | bytes 110600 | tf_op jit(solution)/shard_map/ppermute | solution.py:599
  8.2 5.9 %load.2.weight_ref = bf16[1024,8192]{1,0:T(8,128)(2,1)S(1)} custom-call(bf16[1024,8192]{1,0:T(8,128)(2,1)} %weight_ref.10, bf16[16,1152]{1,0:T(8,128)(2,1)S(1)} %get-tuple-element.39.after_ref.h0), custom_call_target="tpu_custom_call" | custom-call | bytes 16777216 | tf_op jit(solution)/shard_map/load/pallas_call | solution.py:281
  14.2 1.8 %up_first.2 = (bf16[56,1152]{1,0:T(8,128)(2,1)S(1)}, f32[56,128]{1,0:T(8,128)S(1)}, bf16[56,2048]{1,0:T(8,128)(2,1)S(1)}, bf16[56,2048]{1,0:T(8,128)(2,1)S(1)}) custom-call(bf16[16,1152]{1,0:T(8,128)(2,1)S(1)} %get-tuple-element.39.after_ref.h0, bf16[16,1152]{1,0:T(8,128)(2,1)S(1)} %collective-permute-done.h1, ...), custom_call_target="tpu_custom_call" | custom-call | flops 469762048 | bytes 8388608 | tf_op jit(solution)/shard_map/up_first/pallas_call | solution.py:359
  16.6 0.9 %up_second.2.kept_ref = f32[56,2048]{1,0:T(8,128)S(1)} custom-call(bf16[56,1152]{1,0:T(8,128)(2,1)S(1)} %get-tuple-element.47.rows_ref, f32[56,128]{1,0:T(8,128)S(1)} %get-tuple-element.44.stats_ref, bf16[1024,8192]{1,0:T(8,128)(2,1)S(1)} %load.2.weight_ref), custom_call_target="tpu_custom_call" | custom-call | flops 234881024 | bytes 4194304 | tf_op jit(solution)/shard_map/up_second/pallas_call | solution.py:388
  18.0 1.8 %collective-permute-start.6 = (bf16[48,2304]{1,0:T(8,128)(2,1)S(1)}, bf16[48,2304]{1,0:T(8,128)(2,1)S(1)}, u32[]{:S(2)}, u32[]{:S(2)}) collective-permute-start(bf16[48,2304]{1,0:T(8,128)(2,1)S(1)} %get-tuple-element.46), channel_id=1, source_target_pairs={{0,2},{1,3},{2,0},{3,1},{4,6},{5,7},{6,4},{7,5},{8,10},{9,11},{10,... | collective-permute-start | bytes 663560 | tf_op jit(solution)/shard_map/ppermute | solution.py:599
  19.8 0.9 %up_merge.2 = (bf16[48,2176]{1,0:T(8,128)(2,1)S(1)}, f32[56,2048]{1,0:T(8,128)S(1)}) custom-call(bf16[56,1152]{1,0:T(8,128)(2,1)S(1)} %get-tuple-element.47.rows_ref, f32[56,128]{1,0:T(8,128)S(1)} %get-tuple-element.44.stats_ref, f32[56,128]{1,0:T(8,128)S(1)} %collective-permute-done.4.got_stats_ref, bf16[1024,8192]{1,0:T(8,128)(2,1)S(1)} %load.2.weight_ref, ...), custom_call_target="tpu_custom_call" | custom-call | flops 234881024 | bytes 4194304 | tf_op jit(solution)/shard_map/up_merge/pallas_call | solution.py:467
  21.1 5.2 %collective-permute-done.6.got_ref.packed_ref = bf16[48,2304]{1,0:T(8,128)(2,1)S(1)} collective-permute-done((bf16[48,2304]{1,0:T(8,128)(2,1)S(1)}, bf16[48,2304]{1,0:T(8,128)(2,1)S(1)}, u32[]{:S(2)}, u32[]{:S(2)}) %collective-permute-start.6) | collective-permute-done | bytes 221216 | tf_op jit(solution)/shard_map/ppermute | solution.py:599
  26.9 0.8 %down_part.6.rest_0_ = f32[48,1024]{1,0:T(8,128)S(1)} custom-call(bf16[48,2048]{1,0:T(8,128)(2,1)S(1)} %hidden.4.hidden_ref, bf16[8192,1024]{1,0:T(8,128)(2,1)S(1)} %bitcast.6), custom_call_target="tpu_custom_call" | custom-call | flops 1 | bytes 1 | tf_op jit(solution)/shard_map/down_part/pallas_call | solution.py:532
  28.2 0.8 %down_part.7.rest_0_ = f32[48,1024]{1,0:T(8,128)S(1)} custom-call(bf16[48,2048]{1,0:T(8,128)(2,1)S(1)} %collective-permute-done.7.hidden_ref, bf16[8192,1024]{1,0:T(8,128)(2,1)S(1)} %bitcast.6, f32[48,1024]{1,0:T(8,128)S(1)} %down_part.6.rest_0_), custom_call_target="tpu_custom_call" | custom-call | flops 1 | bytes 1 | tf_op jit(solution)/shard_map/down_part/pallas_call | solution.py:532
  29.1 1.0 %collective-permute-done.8.got_ref = bf16[48,2176]{1,0:T(8,128)(2,1)S(1)} collective-permute-done((bf16[48,2176]{1,0:T(8,128)(2,1)S(1)}, bf16[48,2176]{1,0:T(8,128)(2,1)S(1)}, u32[]{:S(2)}, u32[]{:S(2)}) %collective-permute-start.8) | collective-permute-done | bytes 208928 | tf_op jit(solution)/shard_map/ppermute | solution.py:599
  30.5 0.8 %down_part.8.part_ref = f32[48,1024]{1,0:T(8,128)S(1)} custom-call(bf16[48,2048]{1,0:T(8,128)(2,1)S(1)} %hidden.5.hidden_ref, bf16[8192,1024]{1,0:T(8,128)(2,1)S(1)} %bitcast.6, f32[48,1024]{1,0:T(8,128)S(1)} %down_part.7.rest_0_), custom_call_target="tpu_custom_call" | custom-call | flops 1 | bytes 1 | tf_op jit(solution)/shard_map/down_part/pallas_call | solution.py:532
  32.0 0.9 %down_last.2.after_ref.h0 = bf16[48,1152]{1,0:T(8,128)(2,1)S(1)} custom-call(f32[48,1024]{1,0:T(8,128)S(1)} %down_part.8.part_ref, bf16[56,1152]{1,0:T(8,128)(2,1)S(1)} %get-tuple-element.47.rows_ref, bf16[48,2048]{1,0:T(8,128)(2,1)S(1)} %collective-permute-done.9.hidden_ref, bf16[8192,1024]{1,0:T(8,128)(2,1)S(1)} %bitcast.6), custom_call_target="tpu_custom_call" | custom-call | flops 201326592 | bytes 4194304 | tf_op jit(solution)/shard_map/down_last/pallas_call | solution.py:568
  32.8 3.9 %collective-permute-start.12 = (bf16[48,1152]{1,0:T(8,128)(2,1)S(1)}, bf16[48,1152]{1,0:T(8,128)(2,1)S(1)}, u32[]{:S(2)}, u32[]{:S(2)}) collective-permute-start(bf16[48,1152]{1,0:T(8,128)(2,1)S(1)} %down_last.2.after_ref.h0), channel_id=1, source_target_pairs={{0,12},{4,8},{8,4},{12,0},{1,13},{5,9},{9,5},{13,1},{2,14},{6,10},... | collective-permute-start | bytes 331784 | tf_op jit(solution)/shard_map/ppermute | solution.py:599
  37.4 5.9 %load.3.weight_ref = bf16[1024,8192]{1,0:T(8,128)(2,1)S(1)} custom-call(bf16[1024,8192]{1,0:T(8,128)(2,1)} %weight_ref.15, bf16[48,1152]{1,0:T(8,128)(2,1)S(1)} %down_last.2.after_ref.h0), custom_call_target="tpu_custom_call" | custom-call | bytes 16777216 | tf_op jit(solution)/shard_map/load/pallas_call | solution.py:281
  43.3 2.2 %collective-permute-done.11.h2 = bf16[48,1152]{1,0:T(8,128)(2,1)S(1)} collective-permute-done((bf16[48,1152]{1,0:T(8,128)(2,1)S(1)}, bf16[48,1152]{1,0:T(8,128)(2,1)S(1)}, u32[]{:S(2)}, u32[]{:S(2)}) %collective-permute-start.11) | collective-permute-done | bytes 110624 | tf_op jit(solution)/shard_map/ppermute | solution.py:599
  45.4 2.1 %up_first.3 = (bf16[56,1152]{1,0:T(8,128)(2,1)S(1)}, f32[56,128]{1,0:T(8,128)S(1)}, bf16[56,2048]{1,0:T(8,128)(2,1)S(1)}, bf16[56,2048]{1,0:T(8,128)(2,1)S(1)}) custom-call(bf16[48,1152]{1,0:T(8,128)(2,1)S(1)} %down_last.2.after_ref.h0, bf16[48,1152]{1,0:T(8,128)(2,1)S(1)} %collective-permute-done.10.h1, bf16[48,1152]{1,0:T(8,128)(2,1)S(1)} %collective-permute-done.11.h2, ...), custom_call_target="tpu_custom_call" | custom-call | flops 469762048 | bytes 8388608 | tf_op jit(solution)/shard_map/up_first/pallas_call | solution.py:359
  48.2 0.9 %up_second.3.kept_ref = f32[56,2048]{1,0:T(8,128)S(1)} custom-call(bf16[56,1152]{1,0:T(8,128)(2,1)S(1)} %get-tuple-element.59.rows_ref, f32[56,128]{1,0:T(8,128)S(1)} %get-tuple-element.56.stats_ref, bf16[1024,8192]{1,0:T(8,128)(2,1)S(1)} %load.3.weight_ref), custom_call_target="tpu_custom_call" | custom-call | flops 234881024 | bytes 4194304 | tf_op jit(solution)/shard_map/up_second/pallas_call | solution.py:388
  49.6 1.6 %collective-permute-start.16 = (bf16[48,2304]{1,0:T(8,128)(2,1)S(1)}, bf16[48,2304]{1,0:T(8,128)(2,1)S(1)}, u32[]{:S(2)}, u32[]{:S(2)}) collective-permute-start(bf16[48,2304]{1,0:T(8,128)(2,1)S(1)} %get-tuple-element.58), channel_id=1, source_target_pairs={{0,2},{1,3},{2,0},{3,1},{4,6},{5,7},{6,4},{7,5},{8,10},{9,11},{10,... | collective-permute-start | bytes 663560 | tf_op jit(solution)/shard_map/ppermute | solution.py:599
  51.1 0.9 %up_merge.3 = (bf16[48,2176]{1,0:T(8,128)(2,1)S(1)}, f32[56,2048]{1,0:T(8,128)S(1)}) custom-call(bf16[56,1152]{1,0:T(8,128)(2,1)S(1)} %get-tuple-element.59.rows_ref, f32[56,128]{1,0:T(8,128)S(1)} %get-tuple-element.56.stats_ref, f32[56,128]{1,0:T(8,128)S(1)} %collective-permute-done.14.got_stats_ref, bf16[1024,8192]{1,0:T(8,128)(2,1)S(1)} %load.3.weight_ref, ...), custom_call_target="tpu_custom_call" | custom-call | flops 234881024 | bytes 4194304 | tf_op jit(solution)/shard_map/up_merge/pallas_call | solution.py:467
  52.7 5.2 %collective-permute-done.16.got_ref.packed_ref = bf16[48,2304]{1,0:T(8,128)(2,1)S(1)} collective-permute-done((bf16[48,2304]{1,0:T(8,128)(2,1)S(1)}, bf16[48,2304]{1,0:T(8,128)(2,1)S(1)}, u32[]{:S(2)}, u32[]{:S(2)}) %collective-permute-start.16) | collective-permute-done | bytes 221216 | tf_op jit(solution)/shard_map/ppermute | solution.py:599
  59.8 0.8 %down_part.10.rest_0_ = f32[48,1024]{1,0:T(8,128)S(1)} custom-call(bf16[48,2048]{1,0:T(8,128)(2,1)S(1)} %collective-permute-done.17.hidden_ref, bf16[8192,1024]{1,0:T(8,128)(2,1)S(1)} %bitcast.8, f32[48,1024]{1,0:T(8,128)S(1)} %down_part.9.rest_0_), custom_call_target="tpu_custom_call" | custom-call | flops 1 | bytes 1 | tf_op jit(solution)/shard_map/down_part/pallas_call | solution.py:532
  60.6 1.0 %collective-permute-done.18.got_ref = bf16[48,2176]{1,0:T(8,128)(2,1)S(1)} collective-permute-done((bf16[48,2176]{1,0:T(8,128)(2,1)S(1)}, bf16[48,2176]{1,0:T(8,128)(2,1)S(1)}, u32[]{:S(2)}, u32[]{:S(2)}) %collective-permute-start.18) | collective-permute-done | bytes 208928 | tf_op jit(solution)/shard_map/ppermute | solution.py:599
  62.1 0.8 %down_part.11.part_ref = f32[48,1024]{1,0:T(8,128)S(1)} custom-call(bf16[48,2048]{1,0:T(8,128)(2,1)S(1)} %hidden.7.hidden_ref, bf16[8192,1024]{1,0:T(8,128)(2,1)S(1)} %bitcast.8, f32[48,1024]{1,0:T(8,128)S(1)} %down_part.10.rest_0_), custom_call_target="tpu_custom_call" | custom-call | flops 1 | bytes 1 | tf_op jit(solution)/shard_map/down_part/pallas_call | solution.py:532
  63.5 1.0 %down_last.3 = (bf16[16,1024]{1,0:T(8,128)(2,1)S(1)}, bf16[16,1024]{1,0:T(8,128)(2,1)S(1)}, bf16[16,1024]{1,0:T(8,128)(2,1)S(1)}, bf16[16,1024]{1,0:T(8,128)(2,1)S(1)}) custom-call(f32[48,1024]{1,0:T(8,128)S(1)} %down_part.11.part_ref, bf16[56,1152]{1,0:T(8,128)(2,1)S(1)} %get-tuple-element.59.rows_ref, ...), custom_call_target="tpu_custom_call" | custom-call | flops 201326592 | bytes 4194304 | tf_op jit(solution)/shard_map/down_last/pallas_call | solution.py:568
  64.5 1.2 %collective-permute-start.20 = (bf16[16,1024]{1,0:T(8,128)(2,1)S(1)}, bf16[16,1024]{1,0:T(8,128)(2,1)S(1)}, u32[]{:S(2)}, u32[]{:S(2)}) collective-permute-start(bf16[16,1024]{1,0:T(8,128)(2,1)S(1)} %get-tuple-element.68), channel_id=1, source_target_pairs={{0,4},{4,0},{8,12},{12,8},{1,5},{5,1},{9,13},{13,9},{2,6},{6,2},{1... | collective-permute-start | bytes 98312 | tf_op jit(solution)/shard_map/ppermute | solution.py:599
  65.7 1.9 %collective-permute-start.21 = (bf16[16,1024]{1,0:T(8,128)(2,1)S(1)}, bf16[16,1024]{1,0:T(8,128)(2,1)S(1)}, u32[]{:S(2)}, u32[]{:S(2)}) collective-permute-start(bf16[16,1024]{1,0:T(8,128)(2,1)S(1)} %get-tuple-element.69), channel_id=1, source_target_pairs={{0,8},{4,12},{8,0},{12,4},{1,9},{5,13},{9,1},{13,5},{2,10},{6,14},... | collective-permute-start | bytes 98312 | tf_op jit(solution)/shard_map/ppermute | solution.py:599
  67.6 1.3 %collective-permute-start.22 = (bf16[16,1024]{1,0:T(8,128)(2,1)S(1)}, bf16[16,1024]{1,0:T(8,128)(2,1)S(1)}, u32[]{:S(2)}, u32[]{:S(2)}) collective-permute-start(bf16[16,1024]{1,0:T(8,128)(2,1)S(1)} %get-tuple-element.70), channel_id=1, source_target_pairs={{0,12},{4,8},{8,4},{12,0},{1,13},{5,9},{9,5},{13,1},{2,14},{6,10},... | collective-permute-start | bytes 98312 | tf_op jit(solution)/shard_map/ppermute | solution.py:599
  69.0 1.6 %collective-permute-done.21.g2 = bf16[16,1024]{1,0:T(8,128)(2,1)S(1)} collective-permute-done((bf16[16,1024]{1,0:T(8,128)(2,1)S(1)}, bf16[16,1024]{1,0:T(8,128)(2,1)S(1)}, u32[]{:S(2)}, u32[]{:S(2)}) %collective-permute-start.21) | collective-permute-done | bytes 32800 | tf_op jit(solution)/shard_map/ppermute | solution.py:599
  70.6 2.8 %collective-permute-done.22.g3 = bf16[16,1024]{1,0:T(8,128)(2,1)S(1)} collective-permute-done((bf16[16,1024]{1,0:T(8,128)(2,1)S(1)}, bf16[16,1024]{1,0:T(8,128)(2,1)S(1)}, u32[]{:S(2)}, u32[]{:S(2)}) %collective-permute-start.22) | collective-permute-done | bytes 32800 | tf_op jit(solution)/shard_map/ppermute | solution.py:599
  73.3 0.8 %finish.1 = bf16[32,1024]{1,0:T(8,128)(2,1)} custom-call(s32[32,128]{1,0:T(8,128)S(1)} %get-tuple-element.38.home_ref, bf16[16,1024]{1,0:T(8,128)(2,1)S(1)} %get-tuple-element.67.g0, bf16[16,1024]{1,0:T(8,128)(2,1)S(1)} %collective-permute-done.20.g1, bf16[16,1024]{1,0:T(8,128)(2,1)S(1)} %collective-permute-done.21.g2, ...), custom_call_target="tpu_custom_call" | custom-call | tf_op jit(solution)/shard_map/finish/pallas_call | solution.py:587
  (56 shorter events, 8.8 us)
Async XLA Ops:
  2.5 11.6 %collective-permute-start = (bf16[16,1152]{1,0:T(8,128)(2,1)S(1)}, bf16[16,1152]{1,0:T(8,128)(2,1)S(1)}, u32[]{:S(2)}, u32[]{:S(2)}) collective-permute-start(bf16[16,1152]{1,0:T(8,128)(2,1)S(1)} %get-tuple-element.40), channel_id=1, source_target_pairs={{0,4},{4,0},{8,12},{12,8},{1,5},{5,1},{9,13},{13,9},{2,6},{6,2},{1... | collective-permute-start | bytes 110600 | tf_op jit(solution)/shard_map/ppermute | solution.py:599
  5.6 8.5 %collective-permute-start.1 = (bf16[16,1152]{1,0:T(8,128)(2,1)S(1)}, bf16[16,1152]{1,0:T(8,128)(2,1)S(1)}, u32[]{:S(2)}, u32[]{:S(2)}) collective-permute-start(bf16[16,1152]{1,0:T(8,128)(2,1)S(1)} %get-tuple-element.41), channel_id=1, source_target_pairs={{0,8},{4,12},{8,0},{12,4},{1,9},{5,13},{9,1},{13,5},{2,10},{6,14},... | collective-permute-start | bytes 110600 | tf_op jit(solution)/shard_map/ppermute | solution.py:599
  8.2 5.9 %collective-permute-start.2 = (bf16[16,1152]{1,0:T(8,128)(2,1)S(1)}, bf16[16,1152]{1,0:T(8,128)(2,1)S(1)}, u32[]{:S(2)}, u32[]{:S(2)}) collective-permute-start(bf16[16,1152]{1,0:T(8,128)(2,1)S(1)} %get-tuple-element.42), channel_id=1, source_target_pairs={{0,12},{4,8},{8,4},{12,0},{1,13},{5,9},{9,5},{13,1},{2,14},{6,10},... | collective-permute-start | bytes 110600 | tf_op jit(solution)/shard_map/ppermute | solution.py:599
  15.9 1.9 %collective-permute-start.3 = (bf16[56,2048]{1,0:T(8,128)(2,1)S(1)}, bf16[56,2048]{1,0:T(8,128)(2,1)S(1)}, u32[]{:S(2)}, u32[]{:S(2)}) collective-permute-start(bf16[56,2048]{1,0:T(8,128)(2,1)S(1)} %get-tuple-element.45), channel_id=1, source_target_pairs={{0,1},{1,0},{2,3},{3,2},{4,5},{5,4},{6,7},{7,6},{8,9},{9,8},{10,11... | collective-permute-start | bytes 688136 | tf_op jit(solution)/shard_map/ppermute | solution.py:599
  16.0 3.8 %collective-permute-start.5 = (bf16[56,2048]{1,0:T(8,128)(2,1)S(1)}, bf16[56,2048]{1,0:T(8,128)(2,1)S(1)}, u32[]{:S(2)}, u32[]{:S(2)}) collective-permute-start(bf16[56,2048]{1,0:T(8,128)(2,1)S(1)} %get-tuple-element.48), channel_id=1, source_target_pairs={{0,1},{1,0},{2,3},{3,2},{4,5},{5,4},{6,7},{7,6},{8,9},{9,8},{10,11... | collective-permute-start | bytes 688136 | tf_op jit(solution)/shard_map/ppermute | solution.py:599
  16.5 1.3 %collective-permute-start.4 = (f32[56,128]{1,0:T(8,128)S(1)}, f32[56,128]{1,0:T(8,128)S(1)}, u32[]{:S(2)}, u32[]{:S(2)}) collective-permute-start(f32[56,128]{1,0:T(8,128)S(1)} %get-tuple-element.44.stats_ref), channel_id=1, source_target_pairs={{0,1},{1,0},{2,3},{3,2},{4,5},{5,4},{6,7},{7,6},{8,9},{9,8},{10,11... | collective-permute-start | bytes 86024 | tf_op jit(solution)/shard_map/ppermute | solution.py:599
  16.6 10.2 %slice-start = ((s8[16777216]{0:T(1024)(128)(4,1)}), s8[4194304]{0:T(1024)(128)(4,1)S(1)}, s32[]{:S(2)}) async-start(s8[16777216]{0:T(1024)(128)(4,1)} %bitcast.5), calls=%async_computation | async-start | bytes 8388608
  16.6 10.2 %slice-start.1 = ((s8[16777216]{0:T(1024)(128)(4,1)}), s8[4194304]{0:T(1024)(128)(4,1)S(1)}, s32[]{:S(2)}) async-start(s8[16777216]{0:T(1024)(128)(4,1)} %bitcast.5), calls=%async_computation.1 | async-start | bytes 8388608
  18.0 8.8 %slice-start.2 = ((s8[16777216]{0:T(1024)(128)(4,1)}), s8[4194304]{0:T(1024)(128)(4,1)S(1)}, s32[]{:S(2)}) async-start(s8[16777216]{0:T(1024)(128)(4,1)} %bitcast.5), calls=%async_computation.2 | async-start | bytes 8388608
  18.0 8.8 %slice-start.3 = ((s8[16777216]{0:T(1024)(128)(4,1)}), s8[4194304]{0:T(1024)(128)(4,1)S(1)}, s32[]{:S(2)}) async-start(s8[16777216]{0:T(1024)(128)(4,1)} %bitcast.5), calls=%async_computation.3 | async-start | bytes 8388608
  18.0 8.3 %collective-permute-start.6 = (bf16[48,2304]{1,0:T(8,128)(2,1)S(1)}, bf16[48,2304]{1,0:T(8,128)(2,1)S(1)}, u32[]{:S(2)}, u32[]{:S(2)}) collective-permute-start(bf16[48,2304]{1,0:T(8,128)(2,1)S(1)} %get-tuple-element.46), channel_id=1, source_target_pairs={{0,2},{1,3},{2,0},{3,1},{4,6},{5,7},{6,4},{7,5},{8,10},{9,11},{10,... | collective-permute-start | bytes 663560 | tf_op jit(solution)/shard_map/ppermute | solution.py:599
  20.7 9.3 %collective-permute-start.8 = (bf16[48,2176]{1,0:T(8,128)(2,1)S(1)}, bf16[48,2176]{1,0:T(8,128)(2,1)S(1)}, u32[]{:S(2)}, u32[]{:S(2)}) collective-permute-start(bf16[48,2176]{1,0:T(8,128)(2,1)S(1)} %get-tuple-element.51), channel_id=1, source_target_pairs={{0,2},{1,3},{2,0},{3,1},{4,6},{5,7},{6,4},{7,5},{8,10},{9,11},{10,... | collective-permute-start | bytes 626696 | tf_op jit(solution)/shard_map/ppermute | solution.py:599
  26.7 1.5 %collective-permute-start.7 = (bf16[48,2048]{1,0:T(8,128)(2,1)S(1)}, bf16[48,2048]{1,0:T(8,128)(2,1)S(1)}, u32[]{:S(2)}, u32[]{:S(2)}) collective-permute-start(bf16[48,2048]{1,0:T(8,128)(2,1)S(1)} %hidden.4.hidden_ref), channel_id=1, source_target_pairs={{0,1},{1,0},{2,3},{3,2},{4,5},{5,4},{6,7},{7,6},{8,9},{9,8},{10,11... | collective-permute-start | bytes 589832 | tf_op jit(solution)/shard_map/ppermute | solution.py:599
  30.5 1.5 %collective-permute-start.9 = (bf16[48,2048]{1,0:T(8,128)(2,1)S(1)}, bf16[48,2048]{1,0:T(8,128)(2,1)S(1)}, u32[]{:S(2)}, u32[]{:S(2)}) collective-permute-start(bf16[48,2048]{1,0:T(8,128)(2,1)S(1)} %hidden.5.hidden_ref), channel_id=1, source_target_pairs={{0,1},{1,0},{2,3},{3,2},{4,5},{5,4},{6,7},{7,6},{8,9},{9,8},{10,11... | collective-permute-start | bytes 589832 | tf_op jit(solution)/shard_map/ppermute | solution.py:599
  32.8 10.4 %collective-permute-start.12 = (bf16[48,1152]{1,0:T(8,128)(2,1)S(1)}, bf16[48,1152]{1,0:T(8,128)(2,1)S(1)}, u32[]{:S(2)}, u32[]{:S(2)}) collective-permute-start(bf16[48,1152]{1,0:T(8,128)(2,1)S(1)} %down_last.2.after_ref.h0), channel_id=1, source_target_pairs={{0,12},{4,8},{8,4},{12,0},{1,13},{5,9},{9,5},{13,1},{2,14},{6,10},... | collective-permute-start | bytes 331784 | tf_op jit(solution)/shard_map/ppermute | solution.py:599
  36.7 8.7 %collective-permute-start.11 = (bf16[48,1152]{1,0:T(8,128)(2,1)S(1)}, bf16[48,1152]{1,0:T(8,128)(2,1)S(1)}, u32[]{:S(2)}, u32[]{:S(2)}) collective-permute-start(bf16[48,1152]{1,0:T(8,128)(2,1)S(1)} %down_last.2.after_ref.h0), channel_id=1, source_target_pairs={{0,8},{4,12},{8,0},{12,4},{1,9},{5,13},{9,1},{13,5},{2,10},{6,14},... | collective-permute-start | bytes 331784 | tf_op jit(solution)/shard_map/ppermute | solution.py:599
  36.7 8.7 %collective-permute-start.10 = (bf16[48,1152]{1,0:T(8,128)(2,1)S(1)}, bf16[48,1152]{1,0:T(8,128)(2,1)S(1)}, u32[]{:S(2)}, u32[]{:S(2)}) collective-permute-start(bf16[48,1152]{1,0:T(8,128)(2,1)S(1)} %down_last.2.after_ref.h0), channel_id=1, source_target_pairs={{0,4},{4,0},{8,12},{12,8},{1,5},{5,1},{9,13},{13,9},{2,6},{6,2},{1... | collective-permute-start | bytes 331784 | tf_op jit(solution)/shard_map/ppermute | solution.py:599
  47.5 1.9 %collective-permute-start.13 = (bf16[56,2048]{1,0:T(8,128)(2,1)S(1)}, bf16[56,2048]{1,0:T(8,128)(2,1)S(1)}, u32[]{:S(2)}, u32[]{:S(2)}) collective-permute-start(bf16[56,2048]{1,0:T(8,128)(2,1)S(1)} %get-tuple-element.57), channel_id=1, source_target_pairs={{0,1},{1,0},{2,3},{3,2},{4,5},{5,4},{6,7},{7,6},{8,9},{9,8},{10,11... | collective-permute-start | bytes 688136 | tf_op jit(solution)/shard_map/ppermute | solution.py:599
  47.6 3.6 %collective-permute-start.15 = (bf16[56,2048]{1,0:T(8,128)(2,1)S(1)}, bf16[56,2048]{1,0:T(8,128)(2,1)S(1)}, u32[]{:S(2)}, u32[]{:S(2)}) collective-permute-start(bf16[56,2048]{1,0:T(8,128)(2,1)S(1)} %get-tuple-element.60), channel_id=1, source_target_pairs={{0,1},{1,0},{2,3},{3,2},{4,5},{5,4},{6,7},{7,6},{8,9},{9,8},{10,11... | collective-permute-start | bytes 688136 | tf_op jit(solution)/shard_map/ppermute | solution.py:599
  48.1 1.3 %collective-permute-start.14 = (f32[56,128]{1,0:T(8,128)S(1)}, f32[56,128]{1,0:T(8,128)S(1)}, u32[]{:S(2)}, u32[]{:S(2)}) collective-permute-start(f32[56,128]{1,0:T(8,128)S(1)} %get-tuple-element.56.stats_ref), channel_id=1, source_target_pairs={{0,1},{1,0},{2,3},{3,2},{4,5},{5,4},{6,7},{7,6},{8,9},{9,8},{10,11... | collective-permute-start | bytes 86024 | tf_op jit(solution)/shard_map/ppermute | solution.py:599
  48.2 10.2 %slice-start.4 = ((s8[16777216]{0:T(1024)(128)(4,1)}), s8[4194304]{0:T(1024)(128)(4,1)S(1)}, s32[]{:S(2)}) async-start(s8[16777216]{0:T(1024)(128)(4,1)} %bitcast.7), calls=%async_computation.4 | async-start | bytes 8388608
  48.2 10.2 %slice-start.5 = ((s8[16777216]{0:T(1024)(128)(4,1)}), s8[4194304]{0:T(1024)(128)(4,1)S(1)}, s32[]{:S(2)}) async-start(s8[16777216]{0:T(1024)(128)(4,1)} %bitcast.7), calls=%async_computation.5 | async-start | bytes 8388608
  49.6 8.8 %slice-start.6 = ((s8[16777216]{0:T(1024)(128)(4,1)}), s8[4194304]{0:T(1024)(128)(4,1)S(1)}, s32[]{:S(2)}) async-start(s8[16777216]{0:T(1024)(128)(4,1)} %bitcast.7), calls=%async_computation.6 | async-start | bytes 8388608
  49.6 8.8 %slice-start.7 = ((s8[16777216]{0:T(1024)(128)(4,1)}), s8[4194304]{0:T(1024)(128)(4,1)S(1)}, s32[]{:S(2)}) async-start(s8[16777216]{0:T(1024)(128)(4,1)} %bitcast.7), calls=%async_computation.7 | async-start | bytes 8388608
  49.6 8.3 %collective-permute-start.16 = (bf16[48,2304]{1,0:T(8,128)(2,1)S(1)}, bf16[48,2304]{1,0:T(8,128)(2,1)S(1)}, u32[]{:S(2)}, u32[]{:S(2)}) collective-permute-start(bf16[48,2304]{1,0:T(8,128)(2,1)S(1)} %get-tuple-element.58), channel_id=1, source_target_pairs={{0,2},{1,3},{2,0},{3,1},{4,6},{5,7},{6,4},{7,5},{8,10},{9,11},{10,... | collective-permute-start | bytes 663560 | tf_op jit(solution)/shard_map/ppermute | solution.py:599
  52.1 9.6 %collective-permute-start.18 = (bf16[48,2176]{1,0:T(8,128)(2,1)S(1)}, bf16[48,2176]{1,0:T(8,128)(2,1)S(1)}, u32[]{:S(2)}, u32[]{:S(2)}) collective-permute-start(bf16[48,2176]{1,0:T(8,128)(2,1)S(1)} %get-tuple-element.63), channel_id=1, source_target_pairs={{0,2},{1,3},{2,0},{3,1},{4,6},{5,7},{6,4},{7,5},{8,10},{9,11},{10,... | collective-permute-start | bytes 626696 | tf_op jit(solution)/shard_map/ppermute | solution.py:599
  58.3 1.5 %collective-permute-start.17 = (bf16[48,2048]{1,0:T(8,128)(2,1)S(1)}, bf16[48,2048]{1,0:T(8,128)(2,1)S(1)}, u32[]{:S(2)}, u32[]{:S(2)}) collective-permute-start(bf16[48,2048]{1,0:T(8,128)(2,1)S(1)} %hidden.6.hidden_ref), channel_id=1, source_target_pairs={{0,1},{1,0},{2,3},{3,2},{4,5},{5,4},{6,7},{7,6},{8,9},{9,8},{10,11... | collective-permute-start | bytes 589832 | tf_op jit(solution)/shard_map/ppermute | solution.py:599
  62.0 1.5 %collective-permute-start.19 = (bf16[48,2048]{1,0:T(8,128)(2,1)S(1)}, bf16[48,2048]{1,0:T(8,128)(2,1)S(1)}, u32[]{:S(2)}, u32[]{:S(2)}) collective-permute-start(bf16[48,2048]{1,0:T(8,128)(2,1)S(1)} %hidden.7.hidden_ref), channel_id=1, source_target_pairs={{0,1},{1,0},{2,3},{3,2},{4,5},{5,4},{6,7},{7,6},{8,9},{9,8},{10,11... | collective-permute-start | bytes 589832 | tf_op jit(solution)/shard_map/ppermute | solution.py:599
  64.5 4.5 %collective-permute-start.20 = (bf16[16,1024]{1,0:T(8,128)(2,1)S(1)}, bf16[16,1024]{1,0:T(8,128)(2,1)S(1)}, u32[]{:S(2)}, u32[]{:S(2)}) collective-permute-start(bf16[16,1024]{1,0:T(8,128)(2,1)S(1)} %get-tuple-element.68), channel_id=1, source_target_pairs={{0,4},{4,0},{8,12},{12,8},{1,5},{5,1},{9,13},{13,9},{2,6},{6,2},{1... | collective-permute-start | bytes 98312 | tf_op jit(solution)/shard_map/ppermute | solution.py:599
  65.7 4.8 %collective-permute-start.21 = (bf16[16,1024]{1,0:T(8,128)(2,1)S(1)}, bf16[16,1024]{1,0:T(8,128)(2,1)S(1)}, u32[]{:S(2)}, u32[]{:S(2)}) collective-permute-start(bf16[16,1024]{1,0:T(8,128)(2,1)S(1)} %get-tuple-element.69), channel_id=1, source_target_pairs={{0,8},{4,12},{8,0},{12,4},{1,9},{5,13},{9,1},{13,5},{2,10},{6,14},... | collective-permute-start | bytes 98312 | tf_op jit(solution)/shard_map/ppermute | solution.py:599
  67.6 5.7 %collective-permute-start.22 = (bf16[16,1024]{1,0:T(8,128)(2,1)S(1)}, bf16[16,1024]{1,0:T(8,128)(2,1)S(1)}, u32[]{:S(2)}, u32[]{:S(2)}) collective-permute-start(bf16[16,1024]{1,0:T(8,128)(2,1)S(1)} %get-tuple-element.70), channel_id=1, source_target_pairs={{0,12},{4,8},{8,4},{12,0},{1,13},{5,9},{9,5},{13,1},{2,14},{6,10},... | collective-permute-start | bytes 98312 | tf_op jit(solution)/shard_map/ppermute | solution.py:599

commit v4 on v3

--- a/solution.py
+++ b/solution.py
@@ -123,7 +123,7 @@
 META = 128
 MIB = 1 << 20
 STEP = 1024
-FIRST_SHARE = 0.5
+FIRST_SHARE = 0.5625
 F32 = jnp.float32
 BF16 = jnp.bfloat16
 
@@ -230,26 +230,37 @@
     deep = deep_ref[...]
     shallow_column = to_column(shallow, rows)
     deep_column = to_column(deep, rows)
-    place = (shallow_column ^ here) * PAD + ranks(shallow, shallow_column, rows)
+    shallow_rank = ranks(shallow, shallow_column, rows)
+    deep_rank = ranks(deep, deep_column, rows)
+    place = (shallow_column ^ here) * PAD + shallow_rank
+    home_ref[...] = jnp.broadcast_to((deep_column ^ here) * PAD + deep_rank, (rows, META))
+    choose = (iota((EXPERTS * PAD, rows), 0) == to_row(place, rows)).astype(BF16)
+    sent = dot(choose, states)
     lane = iota((rows, META), 1)
-    notes = jnp.where(lane == 0, deep_column.astype(F32), 0.0)
-    deep_rank = ranks(deep, deep_column, rows)
-    home_ref[...] = jnp.broadcast_to((deep_column ^ here) * PAD + deep_rank, (rows, META))
-    notes = jnp.where(lane == 1, deep_rank.astype(F32), notes)
-    for start, gate_ref in ((2, sgate_ref), (5, dgate_ref)):
-        for at, piece in enumerate(split3(to_column(gate_ref[...], rows))):
-            notes = jnp.where(lane == start + at, piece, notes)
-    notes = jnp.where(lane == 8, 1.0, notes)
-    full = jnp.concatenate([states, notes.astype(BF16)], axis=1)
-    choose = (iota((EXPERTS * PAD, rows), 0) == to_row(place, rows)).astype(BF16)
-    sent = dot(choose, full)
+    shallow_gates = split3(to_column(sgate_ref[...], rows))
+    deep_gates = split3(to_column(dgate_ref[...], rows))
+    row = iota((PAD, META), 0)
     for at, out in enumerate((out0, out1, out2, out3)):
-        out[...] = sent[at * PAD : (at + 1) * PAD].astype(BF16)
+        to_shallow = (shallow_column == here ^ at) & (lane == shallow_rank)
+        to_deep = (deep_column == here ^ at) & (lane == deep_rank)
+        line = lambda kept, value: jnp.sum(jnp.where(kept, value, 0.0), axis=0, keepdims=True)
+        apart = shallow_column ^ deep_column
+        source = (apart * SLOTS + (shallow_column ^ here) * CAP + shallow_rank + 1).astype(F32)
+        block = sent[at * PAD : (at + 1) * PAD]
+        pieces = []
+        for part in range(3):
+            note = jnp.where(row == CAP, line(to_shallow, shallow_gates[part]), block[:, part * META : (part + 1) * META])
+            note = jnp.where(row == CAP + 1, line(to_deep, deep_gates[part]), note)
+            if part == 0:
+                note = jnp.where(row == CAP + 2, line(to_deep, source), note)
+            pieces.append(note)
+        block = jnp.concatenate(pieces + [block[:, 3 * META :]], axis=1)
+        out[...] = block.astype(BF16)
 
 
 def attend(arrays):
     rows, features = arrays[0].shape
-    shape = jax.ShapeDtypeStruct((PAD, features + META), BF16)
+    shape = jax.ShapeDtypeStruct((PAD, features), BF16)
     return pl.pallas_call(
         attend_kernel,
         in_specs=[HB] * len(arrays),
@@ -296,15 +307,22 @@
     return (kept == iota((TALL, EXPERTS * PAD), 0)).astype(BF16)
 
 
-def choose_deep(here, held, features):
-    notes = held[:, features:].astype(F32)
-    count = held.shape[0]
-    number = iota((count, 1), 0)
-    apart = (number // SLOTS) ^ (number % SLOTS // CAP)
-    place = apart * CAP + notes[:, 1:2].astype(jnp.int32)
-    mine = (notes[:, 0:1].astype(jnp.int32) == here) & (notes[:, 8:9] > 0.5)
-    place = jnp.where(mine, place, -1)
-    return (iota((TALL, count), 0) == to_row(place, count)).astype(BF16)
+def notes_of(held):
+    slot, lane = iota((TALL, META), 0), iota((TALL, META), 1)
+    columns = []
+    for row in range(CAP, CAP + 3):
+        column = jnp.zeros((TALL, 1), F32)
+        for at in range(EXPERTS):
+            line = held[at * PAD + row : at * PAD + row + 1]
+            value = line[:, :META]
+            if row < CAP + 2:
+                value = value + line[:, META : 2 * META] + line[:, 2 * META : 3 * META]
+            kept = (slot - at * CAP == lane) & (lane < CAP)
+            column = column + jnp.sum(jnp.where(kept, value, 0.0), axis=1, keepdims=True)
+        columns.append(column)
+    notes = jnp.where(lane == 0, columns[0], 0.0)
+    notes = jnp.where(lane == 1, columns[1], notes)
+    return jnp.where(lane == 2, columns[2], notes)
 
 
 def up_block(rows, means, weights):
@@ -316,7 +334,7 @@
 
 
 def cuts_of(half):
-    unit = 4 * META
+    unit = 2 * META
     first = max(unit, int(half * FIRST_SHARE) // unit * unit)
     return (0, first), (first, half - first)
 
@@ -331,44 +349,77 @@
     return [(at, min(STEP, width - at)) for at in range(0, width, STEP)]
 
 
-def up_first_kernel(deep, cuts, h0, h1, h2, h3, weight_ref, rows_ref, stats_ref, *sent):
-    features = weight_ref.shape[0]
+def send_block(rows_ref, means, weight_ref, start, sent_ref):
+    for at, step in steps_of(sent_ref.shape[1]):
+        weights = columns_at(weight_ref, False, start + at, step)
+        row, centred, columns = up_block(rows_ref[...], means, weights)
+        high = columns.astype(BF16).astype(F32)
+        tail = jnp.where(row == SLOTS, high, jnp.where(row == SLOTS + 1, columns - high, 0.0))
+        sent_ref[:, at : at + step] = jnp.where(row < SLOTS, centred, tail).astype(BF16)
+
+
+def up_first_kernel(deep, start, *refs):
+    if deep:
+        notes_ref, h0, h1, h2, h3, weight_ref, rows_ref, stats_ref, sent_ref = refs
+    else:
+        h0, h1, h2, h3, weight_ref, rows_ref, stats_ref, sent_ref, notes_ref = refs
     held = jnp.concatenate([h0[...], h1[...], h2[...], h3[...]], axis=0)
-    choose = choose_deep(lax.axis_index("ep"), held, features) if deep else choose_shallow()
-    picked = dot(choose, held)
-    ones = (iota(picked.shape, 0) == SLOTS) & (iota(picked.shape, 1) < features)
-    rows_ref[...] = jnp.where(ones, 1.0, picked).astype(BF16)
-    wide = picked[:, :features]
+    if deep:
+        place = notes_ref[:, 2:3].astype(jnp.int32) - 1
+        choose = (iota((TALL, held.shape[0]), 1) == place).astype(BF16)
+    else:
+        choose = choose_shallow()
+        notes_ref[...] = notes_of(held.astype(F32))
+    wide = dot(choose, held)
+    rows_ref[...] = jnp.where(iota(wide.shape, 0) == SLOTS, 1.0, wide).astype(BF16)
+    features = wide.shape[1]
     lane = iota((TALL, META), 1)
     total = jnp.sum(wide, axis=1, keepdims=True)
     square = jnp.sum(wide * wide, axis=1, keepdims=True)
     stats_ref[...] = jnp.where(lane == 0, total, jnp.where(lane == 1, square, 0.0))
-    means = total / features
-    for (start, width), sent_ref in zip(cuts, sent):
-        for at, step in steps_of(width):
-            weights = columns_at(weight_ref, False, start + at, step)
-            row, centred, columns = up_block(rows_ref[:, :features], means, weights)
-            high = columns.astype(BF16).astype(F32)
-            tail = jnp.where(row == SLOTS, high, jnp.where(row == SLOTS + 1, columns - high, 0.0))
-            sent_ref[:, at : at + step] = jnp.where(row < SLOTS, centred, tail).astype(BF16)
-
-
-def up_first(deep, cuts, held, weights):
-    features, width = weights.shape
-    half = width // 2
-    return pl.pallas_call(
-        functools.partial(up_first_kernel, deep, cuts),
-        in_specs=[VM] * 5,
-        out_specs=[VM] * 4,
+    send_block(rows_ref, total / features, weight_ref, start, sent_ref)
+
+
+def up_first(deep, cut, notes, held, weights):
+    features = weights.shape[0]
+    start, width = cut
+    operands = ([notes] if deep else []) + list(held)
+    note = jax.ShapeDtypeStruct((TALL, META), F32)
+    out = pl.pallas_call(
+        functools.partial(up_first_kernel, deep, start),
+        in_specs=[VM] * (len(operands) + 1),
+        out_specs=[VM] * (3 if deep else 4),
         out_shape=[
-            jax.ShapeDtypeStruct((TALL, features + META), BF16),
-            jax.ShapeDtypeStruct((TALL, META), F32),
+            jax.ShapeDtypeStruct((TALL, features), BF16),
+            note,
+            jax.ShapeDtypeStruct((TALL, width), BF16),
         ]
-        + [jax.ShapeDtypeStruct((TALL, cut[1]), BF16) for cut in cuts],
-        compiler_params=params(8),
-        cost_estimate=cost(2 * TALL * features * half, 2 * features * half),
+        + ([] if deep else [note]),
+        compiler_params=params(8),
+        cost_estimate=cost(2 * TALL * features * width, 2 * features * width),
         name="up_first",
-    )(*held, weights)
+    )(*operands, weights)
+    return out if not deep else [*out, notes]
+
+
+def up_other_kernel(start, rows_ref, stats_ref, weight_ref, *sent):
+    for sent_ref in sent:
+        send_block(rows_ref, stats_ref[:, 0:1] / rows_ref.shape[1], weight_ref, start, sent_ref)
+        start += sent_ref.shape[1]
+
+
+def up_other(rows, stats, weights, cut):
+    start, width = cut
+    features = weights.shape[0]
+    return pl.pallas_call(
+        functools.partial(up_other_kernel, start),
+        in_specs=[VM] * 3,
+        out_specs=[VM] * 2,
+        out_shape=[jax.ShapeDtypeStruct((TALL, width // 2), BF16)] * 2,
+        compiler_params=params(8),
+        cost_estimate=cost(2 * TALL * features * width, 2 * features * width),
+        name="up_other",
+    )(rows, stats, weights)
 
 
 def up_second_kernel(start, rows_ref, stats_ref, weight_ref, kept_ref):
@@ -376,7 +427,7 @@
     means = stats_ref[:, 0:1] / features
     for at, step in steps_of(kept_ref.shape[1]):
         weights = columns_at(weight_ref, True, start + at, step)
-        row, centred, columns = up_block(rows_ref[:, :features], means, weights)
+        row, centred, columns = up_block(rows_ref[...], means, weights)
         kept_ref[:, at : at + step] = jnp.where(
             row < SLOTS, centred, jnp.where(row == SLOTS, columns, 0.0)
         )
@@ -396,13 +447,16 @@
     )(rows, stats, weights)
 
 
-def merge_into(features, source, width, got_ref, stats, other, sum_ref, sent_ref):
+def merge_into(features, source, width, got_refs, stats, other, sum_ref, sent_ref):
     apart = (stats[:, 0:1] - other[:, 0:1]) * (0.5 / features)
     held = jnp.zeros((SLOTS, META), F32)
     slot = iota((SLOTS, META), 0)
-    for at, step in steps_of(width):
+    span = width // len(got_refs)
+    pieces = [(ref, i * span, at, step) for i, ref in enumerate(got_refs) for at, step in steps_of(span)]
+    for got_ref, base, start, step in pieces:
+        at = base + start
         kept = source(at, step)
-        got = got_ref[:, at : at + step].astype(F32)
+        got = got_ref[:, start : start + step].astype(F32)
         mine = kept[SLOTS : SLOTS + 1]
         theirs = got[SLOTS : SLOTS + 1] + got[SLOTS + 1 : SLOTS + 2]
         row = iota(kept.shape, 0)
@@ -421,7 +475,7 @@
     sums = stats + other
     sums_ref[...] = sums
     source = lambda at, step: kept_ref[:, at : at + step]
-    merge_into(features, source, width, got_ref, stats, other, sum_ref, sent_ref)
+    merge_into(features, source, width, [got_ref], stats, other, sum_ref, sent_ref)
     lane = iota((SLOTS, META), 1)
     packed = jnp.zeros((SLOTS, META), F32)
     for which in range(2):
@@ -447,7 +501,7 @@
 
 
 def up_merge_kernel(
-    start, rows_ref, stats_ref, got_stats_ref, weight_ref, got_ref, sent_ref, sum_ref
+    start, rows_ref, stats_ref, got_stats_ref, weight_ref, got0, got1, sent_ref, sum_ref
 ):
     features = weight_ref.shape[0]
     stats = stats_ref[...]
@@ -455,10 +509,11 @@
 
     def source(at, step):
         weights = columns_at(weight_ref, True, start + at, step)
-        row, centred, columns = up_block(rows_ref[:, :features], means, weights)
+        row, centred, columns = up_block(rows_ref[...], means, weights)
         return jnp.where(row < SLOTS, centred, jnp.where(row == SLOTS, columns, 0.0))
 
-    merge_into(features, source, sum_ref.shape[1], got_ref, stats, got_stats_ref[...], sum_ref, sent_ref)
+    got = [got0, got1]
+    merge_into(features, source, sum_ref.shape[1], got, stats, got_stats_ref[...], sum_ref, sent_ref)
 
 
 def up_merge(rows, stats, got_stats, weights, got, cut):
@@ -466,7 +521,7 @@
     features = weights.shape[0]
     return pl.pallas_call(
         functools.partial(up_merge_kernel, start),
-        in_specs=[VM] * 5,
+        in_specs=[VM] * 6,
         out_specs=[VM] * 2,
         out_shape=[
             jax.ShapeDtypeStruct((SLOTS, width + META), BF16),
@@ -475,10 +530,10 @@
         compiler_params=params(8),
         cost_estimate=cost(2 * TALL * features * width, 2 * features * width),
         name="up_merge",
-    )(rows, stats, got_stats, weights, got)
-
-
-def hidden_kernel(features, sum_ref, sums_ref, got_ref, packed_ref, hidden_ref):
+    )(rows, stats, got_stats, weights, *got)
+
+
+def hidden_kernel(features, sum_ref, sums_ref, got_ref, packed_ref, *hidden):
     width = sum_ref.shape[1]
     packed = packed_ref[:, packed_ref.shape[1] - META :].astype(F32)
     held = got_ref[:, width : width + META].astype(F32)
@@ -489,23 +544,25 @@
     center = (total + theirs_total) / D
     spread = (square + theirs_square) / D - center * center
     scale = lax.rsqrt(spread + epsilon)
-    step = 4 * META
-    for at in range(0, width, step):
+    span = width // len(hidden)
+    pieces = [(ref, i * span, at, step) for i, ref in enumerate(hidden) for at, step in steps_of(span)]
+    for hidden_ref, base, start, step in pieces:
+        at = base + start
         mine = sum_ref[:, at : at + step]
         got = got_ref[:, at : at + step].astype(F32)
         first = at // META
         theirs = jnp.concatenate([held[i : i + 1] for i in range(first, first + step // META)], axis=1)
         columns = mine[SLOTS : SLOTS + 1] - theirs
         pre = (mine[:SLOTS] + got + apart * columns) * scale
-        hidden_ref[:, at : at + step] = jax.nn.gelu(pre, approximate=True).astype(BF16)
-
-
-def hidden_units(features, total, sums, got, packed):
+        hidden_ref[:, start : start + step] = jax.nn.gelu(pre, approximate=True).astype(BF16)
+
+
+def hidden_units(features, total, sums, got, packed, count):
     return pl.pallas_call(
         functools.partial(hidden_kernel, features),
         in_specs=[VM] * 4,
-        out_specs=VM,
-        out_shape=jax.ShapeDtypeStruct((SLOTS, total.shape[1]), BF16),
+        out_specs=[VM] * count,
+        out_shape=[jax.ShapeDtypeStruct((SLOTS, total.shape[1] // count), BF16)] * count,
         compiler_params=params(8),
         cost_estimate=cost(1, 1),
         name="hidden",
@@ -518,40 +575,41 @@
     return weight_ref[pl.ds(pl.multiple_of(which * half + start, 128), width), :]
 
 
-def down_part_kernel(own, start, hidden_ref, weight_ref, *rest):
-    *earlier, out_ref = rest
-    product = dot(hidden_ref[...], rows_at(weight_ref, own, start, hidden_ref.shape[1]))
+def down_part_kernel(own, start, count, weight_ref, *refs):
+    hidden, earlier, out_ref = refs[:count], refs[count:-1], refs[-1]
+    product = None
+    for part in hidden:
+        width = part.shape[1]
+        term = dot(part[...], rows_at(weight_ref, own, start, width))
+        product = term if product is None else product + term
+        start += width
     for part in earlier:
         product = product + part[...]
     out_ref[...] = product
 
 
 def down_part(hidden, weights, own, cut, *earlier):
-    start, width = cut
     features = weights.shape[1]
     return pl.pallas_call(
-        functools.partial(down_part_kernel, own, start),
-        in_specs=[VM] * (2 + len(earlier)),
+        functools.partial(down_part_kernel, own, cut[0], len(hidden)),
+        in_specs=[VM] * (1 + len(hidden) + len(earlier)),
         out_specs=VM,
         out_shape=jax.ShapeDtypeStruct((SLOTS, features), F32),
         compiler_params=params(8),
         cost_estimate=cost(1, 1),
         name="down_part",
-    )(hidden, weights, *earlier)
-
-
-def down_last_kernel(deep, start, part_ref, rows_ref, hidden_ref, weight_ref, *outs):
+    )(weights, *hidden, *earlier)
+
+
+def down_last_kernel(deep, start, part_ref, rows_ref, notes_ref, hidden_ref, weight_ref, *outs):
     features = weight_ref.shape[1]
     weights = rows_at(weight_ref, False, start, hidden_ref.shape[1])
     total = part_ref[...] + dot(hidden_ref[...], weights)
-    rows = rows_ref[...].astype(F32)[:SLOTS]
-    notes = rows[:, features:]
-    first = 5 if deep else 2
-    gate = notes[:, first : first + 1] + notes[:, first + 1 : first + 2]
-    gate = gate + notes[:, first + 2 : first + 3]
-    result = rows[:, :features] + gate * total
+    which = 1 if deep else 0
+    gate = notes_ref[:SLOTS, which : which + 1]
+    result = rows_ref[...].astype(F32)[:SLOTS] + gate * total
     if not deep:
-        outs[0][...] = jnp.concatenate([result, notes], axis=1).astype(BF16)
+        outs[0][...] = result.astype(BF16)
     else:
         target = iota((EXPERTS * PAD, SLOTS), 0)
         kept = jnp.where(target % PAD < CAP, target // PAD * CAP + target % PAD, -1)
@@ -561,19 +619,19 @@
             out[...] = placed[at * PAD : (at + 1) * PAD].astype(BF16)
 
 
-def down_last(deep, part, rows, hidden, weights, cut):
+def down_last(deep, part, rows, notes, hidden, weights, cut):
     start, width = cut
     features = weights.shape[1]
-    shapes = [(PAD, features)] * EXPERTS if deep else [(SLOTS, features + META)]
+    shapes = [(PAD, features)] * EXPERTS if deep else [(SLOTS, features)]
     return pl.pallas_call(
         functools.partial(down_last_kernel, deep, start),
-        in_specs=[VM] * 4,
+        in_specs=[VM] * 5,
         out_specs=[VM] * len(shapes),
         out_shape=[jax.ShapeDtypeStruct(shape, BF16) for shape in shapes],
         compiler_params=params(8),
         cost_estimate=cost(2 * SLOTS * features * width, 2 * features * width),
         name="down_last",
-    )(part, rows, hidden, weights)
+    )(part, rows, notes, hidden, weights)
 
 
 def finish_kernel(home_ref, g0, g1, g2, g3, out_ref):
@@ -607,26 +665,26 @@
     return lax.optimization_barrier((value, earlier))[0]
 
 
-def expert_block(deep, held, up, down):
+def expert_block(deep, notes, held, up, down):
     features, width = up.shape
-    first, second = cuts = cuts_of(width // 2)
-    rows, stats, sent_a, sent_b = up_first(deep, cuts, held, up)
+    first, second = cuts_of(width // 2)
+    rows, stats, sent_a, notes = up_first(deep, first, notes, held, up)
     got_a, got_stats = swap(sent_a, "tp", 1), swap(stats, "tp", 1)
-    got_b = swap(sent_b, "tp", 1)
     kept = up_second(rows, stats, up, first)
     sent_a, total_a, sums = merge(features, kept, got_a, stats, got_stats)
     over_a = swap(sent_a, "tp", 2)
     later = after(rows, sent_a)
+    got_b = [swap(sent, "tp", 1) for sent in up_other(later, stats, up, second)]
     sent_b, total_b = up_merge(later, stats, got_stats, up, got_b, second)
     over_b = swap(sent_b, "tp", 2)
-    hidden_a = hidden_units(features, after(total_a, sent_b), sums, over_a, over_a)
-    other_a = swap(hidden_a, "tp", 1)
+    hidden_a = hidden_units(features, after(total_a, sent_b), sums, over_a, over_a, 2)
+    other_a = [swap(hidden, "tp", 1) for hidden in hidden_a]
     part = down_part(hidden_a, down, True, first)
     part = down_part(other_a, down, False, first, part)
-    hidden_b = hidden_units(features, after(total_b, part), sums, over_b, over_a)
+    (hidden_b,) = hidden_units(features, after(total_b, part), sums, over_b, over_a, 1)
     other_b = swap(hidden_b, "tp", 1)
-    part = down_part(hidden_b, down, True, second, part)
-    return down_last(deep, part, rows, other_b, down, second)
+    part = down_part([hidden_b], down, True, second, part)
+    return notes, down_last(deep, part, rows, notes, other_b, down, second)
 
 
 def fast_body(
@@ -663,8 +721,8 @@
         ),
     )
     weights = load(shallow_up, blocks[0])
-    (between,) = expert_block(False, swap_all(blocks), weights, shallow_down)
-    blocks = expert_block(True, swap_all([between] * EXPERTS), load(deep_up, between), deep_down)
+    notes, (between,) = expert_block(False, None, swap_all(blocks), weights, shallow_down)
+    _, blocks = expert_block(True, notes, swap_all([between] * EXPERTS), load(deep_up, between), deep_down)
     return finish(home, swap_all(blocks))
 
 

time: 74.3 us -> 70.6 us (0.950)
  waiting for transfers between devices: 22 us -> 16.6 us
  starting transfers between devices: 20.6 us -> 22.5 us
    ppermute x23 -> x27, waiting for transfers between devices: 22 us -> 16.6 us  [swap(): return lax.ppermute(value, axis, [(i, i ^ apart) for i in range(count)])]
    ppermute x23 -> x27, starting transfers between devices: 20.6 us -> 22.5 us  [swap(): return lax.ppermute(value, axis, [(i, i ^ apart) for i in range(count)])]
    pallas_call x8 -> x10, Pallas kernels: 8.86 us -> 8.94 us  [the longest x6 5.43 us: down_part(): pl.pallas_call(functools.partial(down_part_kernel, own, cut[0], len(hidde...]
  transfers between devices with their start and end apart: 23 -> 27, of which waited for: 13 -> 15; matrix products, arithmetic and copies ran while one was open for 0% -> 0% of each run, Pallas kernels for 29% -> 33%
where the time goes in v4:
time: 70.6 us; the launch traced here: 70.5 us
  Pallas kernels  31 us (44%)
  starting transfers between devices  22.5 us (32%)
  waiting for transfers between devices  16.6 us (24%)
    ppermute x27, starting transfers between devices, swap(): return lax.ppermute(value, axis, [(i, i ^ apart) for i in range(count)])  22.5 us
    ppermute x27, waiting for transfers between devices, swap(): return lax.ppermute(value, axis, [(i, i ^ apart) for i in range(count)])  16.6 us
    pallas_call x2, Pallas kernels, load(): pl.pallas_call(load_kernel, in_specs=[HB, pl.BlockSpec(memory_space=pl.AN...  11.8 us
    pallas_call x6, Pallas kernels, down_part(): pl.pallas_call(functools.partial(down_part_kernel, own, cut[0], len(hidde...  5.43 us
    pallas_call x1, Pallas kernels, attend(): pl.pallas_call(attend_kernel, in_specs=[HB] * len(arrays), out_specs=[VM]...  2.54 us
    pallas_call x2, Pallas kernels, up_first(): pl.pallas_call(functools.partial(up_first_kernel, deep, start), in_specs=...  1.99 us
    pallas_call x2, Pallas kernels, up_second(): pl.pallas_call(functools.partial(up_second_kernel, start), in_specs=[VM]...  1.93 us
    pallas_call x2, Pallas kernels, down_last(): pl.pallas_call(functools.partial(down_last_kernel, deep, start), in_specs...  1.66 us
  transfers between devices with their start and end apart: 27, of which 15 were waited for; matrix products, arithmetic and copies ran while one was open for 0% of the time, Pallas kernels for 33%

profile of v4, /device:TPU:0, one launch (start us, length us, event | category | flops | bytes accessed | tf_op | source)
XLA Modules:
  0.0 70.5 jit_solution(277306759925643002)
XLA Ops:
  0.0 2.5 %attend.1 = (bf16[16,1024]{1,0:T(8,128)(2,1)S(1)}, bf16[16,1024]{1,0:T(8,128)(2,1)S(1)}, bf16[16,1024]{1,0:T(8,128)(2,1)S(1)}, bf16[16,1024]{1,0:T(8,128)(2,1)S(1)}, s32[32,128]{1,0:T(8,128)S(1)}) custom-call(bf16[32,1024]{1,0:T(8,128)(2,1)} %resid_in.1, bf16[32,1024]{1,0:T(8,128)(2,1)} %query_in.1, bf16[32,1024]{1,0:T(8,128)(2,1)} %key_in.1, ...), custom_call_target="tpu_custom_call" | custom-call | tf_op jit(solution)/shard_map/attend/pallas_call | solution.py:264
  2.6 3.1 %collective-permute-start = (bf16[16,1024]{1,0:T(8,128)(2,1)S(1)}, bf16[16,1024]{1,0:T(8,128)(2,1)S(1)}, u32[]{:S(2)}, u32[]{:S(2)}) collective-permute-start(bf16[16,1024]{1,0:T(8,128)(2,1)S(1)} %get-tuple-element.47), channel_id=1, source_target_pairs={{0,4},{4,0},{8,12},{12,8},{1,5},{5,1},{9,13},{13,9},{2,6},{6,2},{1... | collective-permute-start | bytes 98312 | tf_op jit(solution)/shard_map/ppermute | solution.py:657
  5.6 2.6 %collective-permute-start.1 = (bf16[16,1024]{1,0:T(8,128)(2,1)S(1)}, bf16[16,1024]{1,0:T(8,128)(2,1)S(1)}, u32[]{:S(2)}, u32[]{:S(2)}) collective-permute-start(bf16[16,1024]{1,0:T(8,128)(2,1)S(1)} %get-tuple-element.48), channel_id=1, source_target_pairs={{0,8},{4,12},{8,0},{12,4},{1,9},{5,13},{9,1},{13,5},{2,10},{6,14},... | collective-permute-start | bytes 98312 | tf_op jit(solution)/shard_map/ppermute | solution.py:657
  8.2 5.9 %load.2.refs_4_.weight_ref = bf16[1024,8192]{1,0:T(8,128)(2,1)S(1)} custom-call(bf16[1024,8192]{1,0:T(8,128)(2,1)} %weight_ref.10, bf16[16,1024]{1,0:T(8,128)(2,1)S(1)} %get-tuple-element.46.after_ref.refs_0_), custom_call_target="tpu_custom_call" | custom-call | bytes 16777216 | tf_op jit(solution)/shard_map/load/pallas_call | solution.py:292
  14.2 0.9 %up_first.2 = (bf16[56,1024]{1,0:T(8,128)(2,1)S(1)}, f32[56,128]{1,0:T(8,128)S(1)}, bf16[56,2304]{1,0:T(8,128)(2,1)S(1)}, f32[56,128]{1,0:T(8,128)S(1)}) custom-call(bf16[16,1024]{1,0:T(8,128)(2,1)S(1)} %get-tuple-element.46.after_ref.refs_0_, bf16[16,1024]{1,0:T(8,128)(2,1)S(1)} %collective-permute-done.refs_1_, ...), custom_call_target="tpu_custom_call" | custom-call | flops 264241152 | bytes 4718592 | tf_op jit(solution)/shard_map/up_first/pallas_call | solution.py:388
  15.7 1.0 %up_second.2.kept_ref = f32[56,2304]{1,0:T(8,128)S(1)} custom-call(bf16[56,1024]{1,0:T(8,128)(2,1)S(1)} %get-tuple-element.55.rows_ref, f32[56,128]{1,0:T(8,128)S(1)} %get-tuple-element.52.stats_ref, bf16[1024,8192]{1,0:T(8,128)(2,1)S(1)} %load.2.refs_4_.weight_ref), custom_call_target="tpu_custom_call" | custom-call | flops 264241152 | bytes 4718592 | tf_op jit(solution)/shard_map/up_second/pallas_call | solution.py:439
  16.9 1.8 %collective-permute-start.7 = (bf16[48,2560]{1,0:T(8,128)(2,1)S(1)}, bf16[48,2560]{1,0:T(8,128)(2,1)S(1)}, u32[]{:S(2)}, u32[]{:S(2)}) collective-permute-start(bf16[48,2560]{1,0:T(8,128)(2,1)S(1)} %get-tuple-element.54), channel_id=1, source_target_pairs={{0,2},{1,3},{2,0},{3,1},{4,6},{5,7},{6,4},{7,5},{8,10},{9,11},{10,... | collective-permute-start | bytes 737288 | tf_op jit(solution)/shard_map/ppermute | solution.py:657
  18.7 0.8 %up_other.2 = (bf16[56,896]{1,0:T(8,128)(2,1)S(1)}, bf16[56,896]{1,0:T(8,128)(2,1)S(1)}) custom-call(bf16[56,1024]{1,0:T(8,128)(2,1)S(1)} %get-tuple-element.55.rows_ref, f32[56,128]{1,0:T(8,128)S(1)} %get-tuple-element.52.stats_ref, bf16[1024,8192]{1,0:T(8,128)(2,1)S(1)} %load.2.refs_4_.weight_ref), custom_call_target="tpu_custom_call" | custom-call | flops 205520896 | bytes 3670016 | tf_op jit(solution)/shard_map/up_other/pallas_call | solution.py:414
  20.0 0.8 %collective-permute-done.5.got0 = bf16[56,896]{1,0:T(8,128)(2,1)S(1)} collective-permute-done((bf16[56,896]{1,0:T(8,128)(2,1)S(1)}, bf16[56,896]{1,0:T(8,128)(2,1)S(1)}, u32[]{:S(2)}, u32[]{:S(2)}) %collective-permute-start.5) | collective-permute-done | bytes 100384 | tf_op jit(solution)/shard_map/ppermute | solution.py:657
  21.0 0.8 %up_merge.2 = (bf16[48,1920]{1,0:T(8,128)(2,1)S(1)}, f32[56,1792]{1,0:T(8,128)S(1)}) custom-call(bf16[56,1024]{1,0:T(8,128)(2,1)S(1)} %get-tuple-element.55.rows_ref, f32[56,128]{1,0:T(8,128)S(1)} %get-tuple-element.52.stats_ref, f32[56,128]{1,0:T(8,128)S(1)} %collective-permute-done.4.got_stats_ref, bf16[1024,8192]{1,0:T(8,128)(2,1)S(1)} %load.2.refs_4_.weight_ref, ...), custom_call_target="tpu_custom_call" | custom-call | flops 205520896 | bytes 3670016 | tf_op jit(solution)/shard_map/up_merge/pallas_call | solution.py:522
  22.1 2.9 %collective-permute-done.7.got_ref.packed_ref = bf16[48,2560]{1,0:T(8,128)(2,1)S(1)} collective-permute-done((bf16[48,2560]{1,0:T(8,128)(2,1)S(1)}, bf16[48,2560]{1,0:T(8,128)(2,1)S(1)}, u32[]{:S(2)}, u32[]{:S(2)}) %collective-permute-start.7) | collective-permute-done | bytes 245792 | tf_op jit(solution)/shard_map/ppermute | solution.py:657
  26.0 0.9 %down_part.6.refs_2_ = f32[48,1024]{1,0:T(8,128)S(1)} custom-call(bf16[8192,1024]{1,0:T(8,128)(2,1)S(1)} %bitcast.6, bf16[48,1152]{1,0:T(8,128)(2,1)S(1)} %get-tuple-element.63.refs_0_, bf16[48,1152]{1,0:T(8,128)(2,1)S(1)} %get-tuple-element.64.refs_1_), custom_call_target="tpu_custom_call" | custom-call | flops 1 | bytes 1 | tf_op jit(solution)/shard_map/down_part/pallas_call | solution.py:593
  27.0 0.9 %down_part.7.refs_1_ = f32[48,1024]{1,0:T(8,128)S(1)} custom-call(bf16[8192,1024]{1,0:T(8,128)(2,1)S(1)} %bitcast.6, bf16[48,1152]{1,0:T(8,128)(2,1)S(1)} %collective-permute-done.8.refs_0_, bf16[48,1152]{1,0:T(8,128)(2,1)S(1)} %collective-permute-done.9.refs_1_, f32[48,1024]{1,0:T(8,128)S(1)} %down_part.6.refs_2_), custom_call_target="tpu_custom_call" | custom-call | flops 1 | bytes 1 | tf_op jit(solution)/shard_map/down_part/pallas_call | solution.py:593
  28.0 0.9 %collective-permute-done.10.got_ref = bf16[48,1920]{1,0:T(8,128)(2,1)S(1)} collective-permute-done((bf16[48,1920]{1,0:T(8,128)(2,1)S(1)}, bf16[48,1920]{1,0:T(8,128)(2,1)S(1)}, u32[]{:S(2)}, u32[]{:S(2)}) %collective-permute-start.10) | collective-permute-done | bytes 184352 | tf_op jit(solution)/shard_map/ppermute | solution.py:657
  31.5 3.9 %collective-permute-start.14 = (bf16[48,1024]{1,0:T(8,128)(2,1)S(1)}, bf16[48,1024]{1,0:T(8,128)(2,1)S(1)}, u32[]{:S(2)}, u32[]{:S(2)}) collective-permute-start(bf16[48,1024]{1,0:T(8,128)(2,1)S(1)} %down_last.2.after_ref.refs_1_), channel_id=1, source_target_pairs={{0,12},{4,8},{8,4},{12,0},{1,13},{5,9},{9,5},{13,1},{2,14},{6,10},... | collective-permute-start | bytes 294920 | tf_op jit(solution)/shard_map/ppermute | solution.py:657
  36.0 5.9 %load.3.refs_5_.weight_ref = bf16[1024,8192]{1,0:T(8,128)(2,1)S(1)} custom-call(bf16[1024,8192]{1,0:T(8,128)(2,1)} %weight_ref.15, bf16[48,1024]{1,0:T(8,128)(2,1)S(1)} %down_last.2.after_ref.refs_1_), custom_call_target="tpu_custom_call" | custom-call | bytes 16777216 | tf_op jit(solution)/shard_map/load/pallas_call | solution.py:292
  41.9 1.1 %collective-permute-done.13.refs_3_ = bf16[48,1024]{1,0:T(8,128)(2,1)S(1)} collective-permute-done((bf16[48,1024]{1,0:T(8,128)(2,1)S(1)}, bf16[48,1024]{1,0:T(8,128)(2,1)S(1)}, u32[]{:S(2)}, u32[]{:S(2)}) %collective-permute-start.13) | collective-permute-done | bytes 98336 | tf_op jit(solution)/shard_map/ppermute | solution.py:657
  43.0 1.1 %up_first.3 = (bf16[56,1024]{1,0:T(8,128)(2,1)S(1)}, f32[56,128]{1,0:T(8,128)S(1)}, bf16[56,2304]{1,0:T(8,128)(2,1)S(1)}) custom-call(f32[56,128]{1,0:T(8,128)S(1)} %get-tuple-element.50.notes_ref.refs_0_, bf16[48,1024]{1,0:T(8,128)(2,1)S(1)} %down_last.2.after_ref.refs_1_, bf16[48,1024]{1,0:T(8,128)(2,1)S(1)} %collective-permute-done.12.refs_2_, ...), custom_call_target="tpu_custom_call" | custom-call | flops 264241152 | bytes 4718592 | tf_op jit(solution)/shard_map/up_first/pallas_call | solution.py:388
  44.7 1.0 %up_second.3.kept_ref = f32[56,2304]{1,0:T(8,128)S(1)} custom-call(bf16[56,1024]{1,0:T(8,128)(2,1)S(1)} %get-tuple-element.70.rows_ref, f32[56,128]{1,0:T(8,128)S(1)} %get-tuple-element.67.stats_ref, bf16[1024,8192]{1,0:T(8,128)(2,1)S(1)} %load.3.refs_5_.weight_ref), custom_call_target="tpu_custom_call" | custom-call | flops 264241152 | bytes 4718592 | tf_op jit(solution)/shard_map/up_second/pallas_call | solution.py:439
  45.9 1.6 %collective-permute-start.19 = (bf16[48,2560]{1,0:T(8,128)(2,1)S(1)}, bf16[48,2560]{1,0:T(8,128)(2,1)S(1)}, u32[]{:S(2)}, u32[]{:S(2)}) collective-permute-start(bf16[48,2560]{1,0:T(8,128)(2,1)S(1)} %get-tuple-element.69), channel_id=1, source_target_pairs={{0,2},{1,3},{2,0},{3,1},{4,6},{5,7},{6,4},{7,5},{8,10},{9,11},{10,... | collective-permute-start | bytes 737288 | tf_op jit(solution)/shard_map/ppermute | solution.py:657
  48.8 0.8 %collective-permute-done.17.got0 = bf16[56,896]{1,0:T(8,128)(2,1)S(1)} collective-permute-done((bf16[56,896]{1,0:T(8,128)(2,1)S(1)}, bf16[56,896]{1,0:T(8,128)(2,1)S(1)}, u32[]{:S(2)}, u32[]{:S(2)}) %collective-permute-start.17) | collective-permute-done | bytes 100384 | tf_op jit(solution)/shard_map/ppermute | solution.py:657
  49.8 0.8 %up_merge.3 = (bf16[48,1920]{1,0:T(8,128)(2,1)S(1)}, f32[56,1792]{1,0:T(8,128)S(1)}) custom-call(bf16[56,1024]{1,0:T(8,128)(2,1)S(1)} %get-tuple-element.70.rows_ref, f32[56,128]{1,0:T(8,128)S(1)} %get-tuple-element.67.stats_ref, f32[56,128]{1,0:T(8,128)S(1)} %collective-permute-done.16.got_stats_ref, bf16[1024,8192]{1,0:T(8,128)(2,1)S(1)} %load.3.refs_5_.weight_ref, ...), custom_call_target="tpu_custom_call" | custom-call | flops 205520896 | bytes 3670016 | tf_op jit(solution)/shard_map/up_merge/pallas_call | solution.py:522
  51.2 3.1 %collective-permute-done.19.got_ref.packed_ref = bf16[48,2560]{1,0:T(8,128)(2,1)S(1)} collective-permute-done((bf16[48,2560]{1,0:T(8,128)(2,1)S(1)}, bf16[48,2560]{1,0:T(8,128)(2,1)S(1)}, u32[]{:S(2)}, u32[]{:S(2)}) %collective-permute-start.19) | collective-permute-done | bytes 245792 | tf_op jit(solution)/shard_map/ppermute | solution.py:657
  55.3 1.1 %down_part.9.refs_2_ = f32[48,1024]{1,0:T(8,128)S(1)} custom-call(bf16[8192,1024]{1,0:T(8,128)(2,1)S(1)} %bitcast.8, bf16[48,1152]{1,0:T(8,128)(2,1)S(1)} %get-tuple-element.78.refs_0_, bf16[48,1152]{1,0:T(8,128)(2,1)S(1)} %get-tuple-element.79.refs_1_), custom_call_target="tpu_custom_call" | custom-call | flops 1 | bytes 1 | tf_op jit(solution)/shard_map/down_part/pallas_call | solution.py:593
  56.5 0.9 %down_part.10.refs_1_ = f32[48,1024]{1,0:T(8,128)S(1)} custom-call(bf16[8192,1024]{1,0:T(8,128)(2,1)S(1)} %bitcast.8, bf16[48,1152]{1,0:T(8,128)(2,1)S(1)} %collective-permute-done.20.refs_0_, bf16[48,1152]{1,0:T(8,128)(2,1)S(1)} %collective-permute-done.21.refs_1_, f32[48,1024]{1,0:T(8,128)S(1)} %down_part.9.refs_2_), custom_call_target="tpu_custom_call" | custom-call | flops 1 | bytes 1 | tf_op jit(solution)/shard_map/down_part/pallas_call | solution.py:593
  59.8 0.9 %down_last.3 = (bf16[16,1024]{1,0:T(8,128)(2,1)S(1)}, bf16[16,1024]{1,0:T(8,128)(2,1)S(1)}, bf16[16,1024]{1,0:T(8,128)(2,1)S(1)}, bf16[16,1024]{1,0:T(8,128)(2,1)S(1)}) custom-call(f32[48,1024]{1,0:T(8,128)S(1)} %down_part.11.part_ref, bf16[56,1024]{1,0:T(8,128)(2,1)S(1)} %get-tuple-element.70.rows_ref, f32[56,128]{1,0:T(8,128)S(1)} %get-tuple-element.50.notes_ref.refs_0_, ...), custom_call_target="tpu_custom_call" | custom-call | flops 176160768 | bytes 3670016 | tf_op jit(solution)/shard_map/down_last/pallas_call | solution.py:626
  60.7 1.5 %collective-permute-start.24 = (bf16[16,1024]{1,0:T(8,128)(2,1)S(1)}, bf16[16,1024]{1,0:T(8,128)(2,1)S(1)}, u32[]{:S(2)}, u32[]{:S(2)}) collective-permute-start(bf16[16,1024]{1,0:T(8,128)(2,1)S(1)} %get-tuple-element.82), channel_id=1, source_target_pairs={{0,4},{4,0},{8,12},{12,8},{1,5},{5,1},{9,13},{13,9},{2,6},{6,2},{1... | collective-permute-start | bytes 98312 | tf_op jit(solution)/shard_map/ppermute | solution.py:657
  62.2 1.8 %collective-permute-start.25 = (bf16[16,1024]{1,0:T(8,128)(2,1)S(1)}, bf16[16,1024]{1,0:T(8,128)(2,1)S(1)}, u32[]{:S(2)}, u32[]{:S(2)}) collective-permute-start(bf16[16,1024]{1,0:T(8,128)(2,1)S(1)} %get-tuple-element.83), channel_id=1, source_target_pairs={{0,8},{4,12},{8,0},{12,4},{1,9},{5,13},{9,1},{13,5},{2,10},{6,14},... | collective-permute-start | bytes 98312 | tf_op jit(solution)/shard_map/ppermute | solution.py:657
  63.9 1.2 %collective-permute-start.26 = (bf16[16,1024]{1,0:T(8,128)(2,1)S(1)}, bf16[16,1024]{1,0:T(8,128)(2,1)S(1)}, u32[]{:S(2)}, u32[]{:S(2)}) collective-permute-start(bf16[16,1024]{1,0:T(8,128)(2,1)S(1)} %get-tuple-element.84), channel_id=1, source_target_pairs={{0,12},{4,8},{8,4},{12,0},{1,13},{5,9},{9,5},{13,1},{2,14},{6,10},... | collective-permute-start | bytes 98312 | tf_op jit(solution)/shard_map/ppermute | solution.py:657
  65.1 2.2 %collective-permute-done.25.g2 = bf16[16,1024]{1,0:T(8,128)(2,1)S(1)} collective-permute-done((bf16[16,1024]{1,0:T(8,128)(2,1)S(1)}, bf16[16,1024]{1,0:T(8,128)(2,1)S(1)}, u32[]{:S(2)}, u32[]{:S(2)}) %collective-permute-start.25) | collective-permute-done | bytes 32800 | tf_op jit(solution)/shard_map/ppermute | solution.py:657
  67.3 2.3 %collective-permute-done.26.g3 = bf16[16,1024]{1,0:T(8,128)(2,1)S(1)} collective-permute-done((bf16[16,1024]{1,0:T(8,128)(2,1)S(1)}, bf16[16,1024]{1,0:T(8,128)(2,1)S(1)}, u32[]{:S(2)}, u32[]{:S(2)}) %collective-permute-start.26) | collective-permute-done | bytes 32800 | tf_op jit(solution)/shard_map/ppermute | solution.py:657
  69.6 0.8 %finish.1 = bf16[32,1024]{1,0:T(8,128)(2,1)} custom-call(s32[32,128]{1,0:T(8,128)S(1)} %get-tuple-element.45.home_ref, bf16[16,1024]{1,0:T(8,128)(2,1)S(1)} %get-tuple-element.81.g0, bf16[16,1024]{1,0:T(8,128)(2,1)S(1)} %collective-permute-done.24.g1, bf16[16,1024]{1,0:T(8,128)(2,1)S(1)} %collective-permute-done.25.g2, ...), custom_call_target="tpu_custom_call" | custom-call | tf_op jit(solution)/shard_map/finish/pallas_call | solution.py:645
  (66 shorter events, 12.3 us)
Async XLA Ops:
  2.6 11.6 %collective-permute-start = (bf16[16,1024]{1,0:T(8,128)(2,1)S(1)}, bf16[16,1024]{1,0:T(8,128)(2,1)S(1)}, u32[]{:S(2)}, u32[]{:S(2)}) collective-permute-start(bf16[16,1024]{1,0:T(8,128)(2,1)S(1)} %get-tuple-element.47), channel_id=1, source_target_pairs={{0,4},{4,0},{8,12},{12,8},{1,5},{5,1},{9,13},{13,9},{2,6},{6,2},{1... | collective-permute-start | bytes 98312 | tf_op jit(solution)/shard_map/ppermute | solution.py:657
  5.6 8.5 %collective-permute-start.1 = (bf16[16,1024]{1,0:T(8,128)(2,1)S(1)}, bf16[16,1024]{1,0:T(8,128)(2,1)S(1)}, u32[]{:S(2)}, u32[]{:S(2)}) collective-permute-start(bf16[16,1024]{1,0:T(8,128)(2,1)S(1)} %get-tuple-element.48), channel_id=1, source_target_pairs={{0,8},{4,12},{8,0},{12,4},{1,9},{5,13},{9,1},{13,5},{2,10},{6,14},... | collective-permute-start | bytes 98312 | tf_op jit(solution)/shard_map/ppermute | solution.py:657
  8.2 5.9 %collective-permute-start.2 = (bf16[16,1024]{1,0:T(8,128)(2,1)S(1)}, bf16[16,1024]{1,0:T(8,128)(2,1)S(1)}, u32[]{:S(2)}, u32[]{:S(2)}) collective-permute-start(bf16[16,1024]{1,0:T(8,128)(2,1)S(1)} %get-tuple-element.49), channel_id=1, source_target_pairs={{0,12},{4,8},{8,4},{12,0},{1,13},{5,9},{9,5},{13,1},{2,14},{6,10},... | collective-permute-start | bytes 98312 | tf_op jit(solution)/shard_map/ppermute | solution.py:657
  15.1 1.6 %collective-permute-start.3 = (bf16[56,2304]{1,0:T(8,128)(2,1)S(1)}, bf16[56,2304]{1,0:T(8,128)(2,1)S(1)}, u32[]{:S(2)}, u32[]{:S(2)}) collective-permute-start(bf16[56,2304]{1,0:T(8,128)(2,1)S(1)} %get-tuple-element.53), channel_id=1, source_target_pairs={{0,1},{1,0},{2,3},{3,2},{4,5},{5,4},{6,7},{7,6},{8,9},{9,8},{10,11... | collective-permute-start | bytes 774152 | tf_op jit(solution)/shard_map/ppermute | solution.py:657
  15.2 1.6 %collective-permute-start.4 = (f32[56,128]{1,0:T(8,128)S(1)}, f32[56,128]{1,0:T(8,128)S(1)}, u32[]{:S(2)}, u32[]{:S(2)}) collective-permute-start(f32[56,128]{1,0:T(8,128)S(1)} %get-tuple-element.52.stats_ref), channel_id=1, source_target_pairs={{0,1},{1,0},{2,3},{3,2},{4,5},{5,4},{6,7},{7,6},{8,9},{9,8},{10,11... | collective-permute-start | bytes 86024 | tf_op jit(solution)/shard_map/ppermute | solution.py:657
  16.8 9.2 %slice-start = ((s8[16777216]{0:T(1024)(128)(4,1)}), s8[4194304]{0:T(1024)(128)(4,1)S(1)}, s32[]{:S(2)}) async-start(s8[16777216]{0:T(1024)(128)(4,1)} %bitcast.5), calls=%async_computation | async-start | bytes 8388608
  16.9 9.2 %slice-start.1 = ((s8[16777216]{0:T(1024)(128)(4,1)}), s8[4194304]{0:T(1024)(128)(4,1)S(1)}, s32[]{:S(2)}) async-start(s8[16777216]{0:T(1024)(128)(4,1)} %bitcast.5), calls=%async_computation.1 | async-start | bytes 8388608
  16.9 8.2 %collective-permute-start.7 = (bf16[48,2560]{1,0:T(8,128)(2,1)S(1)}, bf16[48,2560]{1,0:T(8,128)(2,1)S(1)}, u32[]{:S(2)}, u32[]{:S(2)}) collective-permute-start(bf16[48,2560]{1,0:T(8,128)(2,1)S(1)} %get-tuple-element.54), channel_id=1, source_target_pairs={{0,2},{1,3},{2,0},{3,1},{4,6},{5,7},{6,4},{7,5},{8,10},{9,11},{10,... | collective-permute-start | bytes 737288 | tf_op jit(solution)/shard_map/ppermute | solution.py:657
  19.4 1.4 %collective-permute-start.5 = (bf16[56,896]{1,0:T(8,128)(2,1)S(1)}, bf16[56,896]{1,0:T(8,128)(2,1)S(1)}, u32[]{:S(2)}, u32[]{:S(2)}) collective-permute-start(bf16[56,896]{1,0:T(8,128)(2,1)S(1)} %get-tuple-element.56), channel_id=1, source_target_pairs={{0,1},{1,0},{2,3},{3,2},{4,5},{5,4},{6,7},{7,6},{8,9},{9,8},{10,11... | collective-permute-start | bytes 301064 | tf_op jit(solution)/shard_map/ppermute | solution.py:657
  19.5 1.4 %collective-permute-start.6 = (bf16[56,896]{1,0:T(8,128)(2,1)S(1)}, bf16[56,896]{1,0:T(8,128)(2,1)S(1)}, u32[]{:S(2)}, u32[]{:S(2)}) collective-permute-start(bf16[56,896]{1,0:T(8,128)(2,1)S(1)} %get-tuple-element.57), channel_id=1, source_target_pairs={{0,1},{1,0},{2,3},{3,2},{4,5},{5,4},{6,7},{7,6},{8,9},{9,8},{10,11... | collective-permute-start | bytes 301064 | tf_op jit(solution)/shard_map/ppermute | solution.py:657
  21.7 7.1 %collective-permute-start.10 = (bf16[48,1920]{1,0:T(8,128)(2,1)S(1)}, bf16[48,1920]{1,0:T(8,128)(2,1)S(1)}, u32[]{:S(2)}, u32[]{:S(2)}) collective-permute-start(bf16[48,1920]{1,0:T(8,128)(2,1)S(1)} %get-tuple-element.60), channel_id=1, source_target_pairs={{0,2},{1,3},{2,0},{3,1},{4,6},{5,7},{6,4},{7,5},{8,10},{9,11},{10,... | collective-permute-start | bytes 552968 | tf_op jit(solution)/shard_map/ppermute | solution.py:657
  25.4 1.5 %collective-permute-start.8 = (bf16[48,1152]{1,0:T(8,128)(2,1)S(1)}, bf16[48,1152]{1,0:T(8,128)(2,1)S(1)}, u32[]{:S(2)}, u32[]{:S(2)}) collective-permute-start(bf16[48,1152]{1,0:T(8,128)(2,1)S(1)} %get-tuple-element.63.refs_0_), channel_id=1, source_target_pairs={{0,1},{1,0},{2,3},{3,2},{4,5},{5,4},{6,7},{7,6},{8,9},{9,8},{10,11... | collective-permute-start | bytes 331784 | tf_op jit(solution)/shard_map/ppermute | solution.py:657
  25.5 1.5 %collective-permute-start.9 = (bf16[48,1152]{1,0:T(8,128)(2,1)S(1)}, bf16[48,1152]{1,0:T(8,128)(2,1)S(1)}, u32[]{:S(2)}, u32[]{:S(2)}) collective-permute-start(bf16[48,1152]{1,0:T(8,128)(2,1)S(1)} %get-tuple-element.64.refs_1_), channel_id=1, source_target_pairs={{0,1},{1,0},{2,3},{3,2},{4,5},{5,4},{6,7},{7,6},{8,9},{9,8},{10,11... | collective-permute-start | bytes 331784 | tf_op jit(solution)/shard_map/ppermute | solution.py:657
  29.2 1.5 %collective-permute-start.11 = (bf16[48,1792]{1,0:T(8,128)(2,1)S(1)}, bf16[48,1792]{1,0:T(8,128)(2,1)S(1)}, u32[]{:S(2)}, u32[]{:S(2)}) collective-permute-start(bf16[48,1792]{1,0:T(8,128)(2,1)S(1)} %hidden.5.refs_0_), channel_id=1, source_target_pairs={{0,1},{1,0},{2,3},{3,2},{4,5},{5,4},{6,7},{7,6},{8,9},{9,8},{10,11... | collective-permute-start | bytes 516104 | tf_op jit(solution)/shard_map/ppermute | solution.py:657
  31.5 10.4 %collective-permute-start.14 = (bf16[48,1024]{1,0:T(8,128)(2,1)S(1)}, bf16[48,1024]{1,0:T(8,128)(2,1)S(1)}, u32[]{:S(2)}, u32[]{:S(2)}) collective-permute-start(bf16[48,1024]{1,0:T(8,128)(2,1)S(1)} %down_last.2.after_ref.refs_1_), channel_id=1, source_target_pairs={{0,12},{4,8},{8,4},{12,0},{1,13},{5,9},{9,5},{13,1},{2,14},{6,10},... | collective-permute-start | bytes 294920 | tf_op jit(solution)/shard_map/ppermute | solution.py:657
  35.4 7.7 %collective-permute-start.13 = (bf16[48,1024]{1,0:T(8,128)(2,1)S(1)}, bf16[48,1024]{1,0:T(8,128)(2,1)S(1)}, u32[]{:S(2)}, u32[]{:S(2)}) collective-permute-start(bf16[48,1024]{1,0:T(8,128)(2,1)S(1)} %down_last.2.after_ref.refs_1_), channel_id=1, source_target_pairs={{0,8},{4,12},{8,0},{12,4},{1,9},{5,13},{9,1},{13,5},{2,10},{6,14},... | collective-permute-start | bytes 294920 | tf_op jit(solution)/shard_map/ppermute | solution.py:657
  35.4 7.7 %collective-permute-start.12 = (bf16[48,1024]{1,0:T(8,128)(2,1)S(1)}, bf16[48,1024]{1,0:T(8,128)(2,1)S(1)}, u32[]{:S(2)}, u32[]{:S(2)}) collective-permute-start(bf16[48,1024]{1,0:T(8,128)(2,1)S(1)} %down_last.2.after_ref.refs_1_), channel_id=1, source_target_pairs={{0,4},{4,0},{8,12},{12,8},{1,5},{5,1},{9,13},{13,9},{2,6},{6,2},{1... | collective-permute-start | bytes 294920 | tf_op jit(solution)/shard_map/ppermute | solution.py:657
  44.1 1.6 %collective-permute-start.15 = (bf16[56,2304]{1,0:T(8,128)(2,1)S(1)}, bf16[56,2304]{1,0:T(8,128)(2,1)S(1)}, u32[]{:S(2)}, u32[]{:S(2)}) collective-permute-start(bf16[56,2304]{1,0:T(8,128)(2,1)S(1)} %get-tuple-element.68), channel_id=1, source_target_pairs={{0,1},{1,0},{2,3},{3,2},{4,5},{5,4},{6,7},{7,6},{8,9},{9,8},{10,11... | collective-permute-start | bytes 774152 | tf_op jit(solution)/shard_map/ppermute | solution.py:657
  44.2 1.6 %collective-permute-start.16 = (f32[56,128]{1,0:T(8,128)S(1)}, f32[56,128]{1,0:T(8,128)S(1)}, u32[]{:S(2)}, u32[]{:S(2)}) collective-permute-start(f32[56,128]{1,0:T(8,128)S(1)} %get-tuple-element.67.stats_ref), channel_id=1, source_target_pairs={{0,1},{1,0},{2,3},{3,2},{4,5},{5,4},{6,7},{7,6},{8,9},{9,8},{10,11... | collective-permute-start | bytes 86024 | tf_op jit(solution)/shard_map/ppermute | solution.py:657
  45.9 9.4 %slice-start.4 = ((s8[16777216]{0:T(1024)(128)(4,1)}), s8[4194304]{0:T(1024)(128)(4,1)S(1)}, s32[]{:S(2)}) async-start(s8[16777216]{0:T(1024)(128)(4,1)} %bitcast.7), calls=%async_computation.4 | async-start | bytes 8388608
  45.9 9.4 %slice-start.5 = ((s8[16777216]{0:T(1024)(128)(4,1)}), s8[4194304]{0:T(1024)(128)(4,1)S(1)}, s32[]{:S(2)}) async-start(s8[16777216]{0:T(1024)(128)(4,1)} %bitcast.7), calls=%async_computation.5 | async-start | bytes 8388608
  45.9 8.4 %collective-permute-start.19 = (bf16[48,2560]{1,0:T(8,128)(2,1)S(1)}, bf16[48,2560]{1,0:T(8,128)(2,1)S(1)}, u32[]{:S(2)}, u32[]{:S(2)}) collective-permute-start(bf16[48,2560]{1,0:T(8,128)(2,1)S(1)} %get-tuple-element.69), channel_id=1, source_target_pairs={{0,2},{1,3},{2,0},{3,1},{4,6},{5,7},{6,4},{7,5},{8,10},{9,11},{10,... | collective-permute-start | bytes 737288 | tf_op jit(solution)/shard_map/ppermute | solution.py:657
  48.3 1.4 %collective-permute-start.17 = (bf16[56,896]{1,0:T(8,128)(2,1)S(1)}, bf16[56,896]{1,0:T(8,128)(2,1)S(1)}, u32[]{:S(2)}, u32[]{:S(2)}) collective-permute-start(bf16[56,896]{1,0:T(8,128)(2,1)S(1)} %get-tuple-element.71), channel_id=1, source_target_pairs={{0,1},{1,0},{2,3},{3,2},{4,5},{5,4},{6,7},{7,6},{8,9},{9,8},{10,11... | collective-permute-start | bytes 301064 | tf_op jit(solution)/shard_map/ppermute | solution.py:657
  48.3 7.0 %slice-start.6 = ((s8[16777216]{0:T(1024)(128)(4,1)}), s8[4194304]{0:T(1024)(128)(4,1)S(1)}, s32[]{:S(2)}) async-start(s8[16777216]{0:T(1024)(128)(4,1)} %bitcast.7), calls=%async_computation.6 | async-start | bytes 8388608
  48.4 1.4 %collective-permute-start.18 = (bf16[56,896]{1,0:T(8,128)(2,1)S(1)}, bf16[56,896]{1,0:T(8,128)(2,1)S(1)}, u32[]{:S(2)}, u32[]{:S(2)}) collective-permute-start(bf16[56,896]{1,0:T(8,128)(2,1)S(1)} %get-tuple-element.72), channel_id=1, source_target_pairs={{0,1},{1,0},{2,3},{3,2},{4,5},{5,4},{6,7},{7,6},{8,9},{9,8},{10,11... | collective-permute-start | bytes 301064 | tf_op jit(solution)/shard_map/ppermute | solution.py:657
  50.6 7.4 %collective-permute-start.22 = (bf16[48,1920]{1,0:T(8,128)(2,1)S(1)}, bf16[48,1920]{1,0:T(8,128)(2,1)S(1)}, u32[]{:S(2)}, u32[]{:S(2)}) collective-permute-start(bf16[48,1920]{1,0:T(8,128)(2,1)S(1)} %get-tuple-element.75), channel_id=1, source_target_pairs={{0,2},{1,3},{2,0},{3,1},{4,6},{5,7},{6,4},{7,5},{8,10},{9,11},{10,... | collective-permute-start | bytes 552968 | tf_op jit(solution)/shard_map/ppermute | solution.py:657
  54.7 1.7 %collective-permute-start.20 = (bf16[48,1152]{1,0:T(8,128)(2,1)S(1)}, bf16[48,1152]{1,0:T(8,128)(2,1)S(1)}, u32[]{:S(2)}, u32[]{:S(2)}) collective-permute-start(bf16[48,1152]{1,0:T(8,128)(2,1)S(1)} %get-tuple-element.78.refs_0_), channel_id=1, source_target_pairs={{0,1},{1,0},{2,3},{3,2},{4,5},{5,4},{6,7},{7,6},{8,9},{9,8},{10,11... | collective-permute-start | bytes 331784 | tf_op jit(solution)/shard_map/ppermute | solution.py:657
  54.8 1.6 %collective-permute-start.21 = (bf16[48,1152]{1,0:T(8,128)(2,1)S(1)}, bf16[48,1152]{1,0:T(8,128)(2,1)S(1)}, u32[]{:S(2)}, u32[]{:S(2)}) collective-permute-start(bf16[48,1152]{1,0:T(8,128)(2,1)S(1)} %get-tuple-element.79.refs_1_), channel_id=1, source_target_pairs={{0,1},{1,0},{2,3},{3,2},{4,5},{5,4},{6,7},{7,6},{8,9},{9,8},{10,11... | collective-permute-start | bytes 331784 | tf_op jit(solution)/shard_map/ppermute | solution.py:657
  58.3 1.5 %collective-permute-start.23 = (bf16[48,1792]{1,0:T(8,128)(2,1)S(1)}, bf16[48,1792]{1,0:T(8,128)(2,1)S(1)}, u32[]{:S(2)}, u32[]{:S(2)}) collective-permute-start(bf16[48,1792]{1,0:T(8,128)(2,1)S(1)} %hidden.7.refs_0_), channel_id=1, source_target_pairs={{0,1},{1,0},{2,3},{3,2},{4,5},{5,4},{6,7},{7,6},{8,9},{9,8},{10,11... | collective-permute-start | bytes 516104 | tf_op jit(solution)/shard_map/ppermute | solution.py:657
  60.7 4.5 %collective-permute-start.24 = (bf16[16,1024]{1,0:T(8,128)(2,1)S(1)}, bf16[16,1024]{1,0:T(8,128)(2,1)S(1)}, u32[]{:S(2)}, u32[]{:S(2)}) collective-permute-start(bf16[16,1024]{1,0:T(8,128)(2,1)S(1)} %get-tuple-element.82), channel_id=1, source_target_pairs={{0,4},{4,0},{8,12},{12,8},{1,5},{5,1},{9,13},{13,9},{2,6},{6,2},{1... | collective-permute-start | bytes 98312 | tf_op jit(solution)/shard_map/ppermute | solution.py:657
  62.2 5.2 %collective-permute-start.25 = (bf16[16,1024]{1,0:T(8,128)(2,1)S(1)}, bf16[16,1024]{1,0:T(8,128)(2,1)S(1)}, u32[]{:S(2)}, u32[]{:S(2)}) collective-permute-start(bf16[16,1024]{1,0:T(8,128)(2,1)S(1)} %get-tuple-element.83), channel_id=1, source_target_pairs={{0,8},{4,12},{8,0},{12,4},{1,9},{5,13},{9,1},{13,5},{2,10},{6,14},... | collective-permute-start | bytes 98312 | tf_op jit(solution)/shard_map/ppermute | solution.py:657
  63.9 5.7 %collective-permute-start.26 = (bf16[16,1024]{1,0:T(8,128)(2,1)S(1)}, bf16[16,1024]{1,0:T(8,128)(2,1)S(1)}, u32[]{:S(2)}, u32[]{:S(2)}) collective-permute-start(bf16[16,1024]{1,0:T(8,128)(2,1)S(1)} %get-tuple-element.84), channel_id=1, source_target_pairs={{0,12},{4,8},{8,4},{12,0},{1,13},{5,9},{9,5},{13,1},{2,14},{6,10},... | collective-permute-start | bytes 98312 | tf_op jit(solution)/shard_map/ppermute | solution.py:657
  (3 other events, 20.0 us)

commit v5 on v4

--- a/solution.py
+++ b/solution.py
@@ -177,7 +177,8 @@
 
 def attend_kernel(
     resid_in, query_in, key_in, value_in, keys_in, values_in, length_in,
-    shallow_in, sgate_in, deep_in, dgate_in, out0, out1, out2, out3, home_ref,
+    shallow_in, sgate_in, deep_in, dgate_in, up_in, out0, out1, out2, out3, home_ref,
+    piece_ref,
     resid_ref, query_ref, key_ref, value_ref, keys_ref, values_ref, length_ref,
     shallow_ref, sgate_ref, deep_ref, dgate_ref, sems,
 ):
@@ -193,6 +194,10 @@
     copies = [pltpu.make_async_copy(a, b, sems.at[i]) for i, (a, b) in enumerate(order)]
     for copy in copies:
         copy.start()
+    width = piece_ref.shape[1]
+    others = pl.ds(pl.multiple_of((1 - core_here()) * (up_in.shape[1] // 2), 128), width)
+    ahead = pltpu.make_async_copy(up_in.at[:, others], piece_ref, sems.at[len(order)])
+    ahead.start()
     spread = (iota((features, META), 0) // HD == iota((features, META), 1)).astype(BF16)
     gather = (iota((META, features), 1) // HD == iota((META, features), 0)).astype(BF16)
 
@@ -256,21 +261,25 @@
             pieces.append(note)
         block = jnp.concatenate(pieces + [block[:, 3 * META :]], axis=1)
         out[...] = block.astype(BF16)
-
-
-def attend(arrays):
+    ahead.wait()
+
+
+def attend(arrays, up, width):
     rows, features = arrays[0].shape
     shape = jax.ShapeDtypeStruct((PAD, features), BF16)
     return pl.pallas_call(
         attend_kernel,
-        in_specs=[HB] * len(arrays),
-        out_specs=[VM] * 5,
-        out_shape=[shape] * 4 + [jax.ShapeDtypeStruct((rows, META), jnp.int32)],
+        in_specs=[HB] * (len(arrays) + 1),
+        out_specs=[VM] * 6,
+        out_shape=[shape] * 4 + [
+            jax.ShapeDtypeStruct((rows, META), jnp.int32),
+            jax.ShapeDtypeStruct((up.shape[0], width), BF16),
+        ],
         scratch_shapes=[pltpu.VMEM(a.shape, a.dtype) for a in arrays]
-        + [pltpu.SemaphoreType.DMA((len(arrays),))],
+        + [pltpu.SemaphoreType.DMA((len(arrays) + 1,))],
         compiler_params=params(16),
         name="attend",
-    )(*[pltpu.with_memory_space_constraint(a, pltpu.HBM) for a in arrays])
+    )(*[pltpu.with_memory_space_constraint(a, pltpu.HBM) for a in (*arrays, up)])
 
 
 def load_kernel(weight_ref, after_ref, out_ref, sems):
@@ -298,6 +307,44 @@
         compiler_params=params(4),
         cost_estimate=cost(0, 2 * weights.size),
         name="load",
+    )(pltpu.with_memory_space_constraint(weights, pltpu.HBM), after)
+
+
+def load_rest_kernel(first, weight_ref, after_ref, others_ref, own_ref, sems):
+    half = own_ref.shape[1]
+    rows = own_ref.shape[0] // 2
+    ours = core_here() * half
+    copies = []
+    for base, ref in ((half - ours + first, others_ref), (ours, own_ref)):
+        columns = pl.ds(pl.multiple_of(base, 128), ref.shape[1])
+        for at in (0, rows):
+            copies.append(
+                pltpu.make_async_copy(
+                    weight_ref.at[pl.ds(at, rows), columns],
+                    ref.at[pl.ds(at, rows)],
+                    sems.at[len(copies)],
+                )
+            )
+    for copy in copies:
+        copy.start()
+    for copy in copies:
+        copy.wait()
+
+
+def load_rest(weights, after, first):
+    rows, half = weights.shape[0], weights.shape[1] // 2
+    return pl.pallas_call(
+        functools.partial(load_rest_kernel, first),
+        in_specs=[HB, pl.BlockSpec(memory_space=pl.ANY)],
+        out_specs=[VM] * 2,
+        out_shape=[
+            jax.ShapeDtypeStruct((rows, half - first), weights.dtype),
+            jax.ShapeDtypeStruct((rows, half), weights.dtype),
+        ],
+        scratch_shapes=[pltpu.SemaphoreType.DMA((4,))],
+        compiler_params=params(4),
+        cost_estimate=cost(0, 2 * weights.size),
+        name="load_rest",
     )(pltpu.with_memory_space_constraint(weights, pltpu.HBM), after)
 
 
@@ -339,7 +386,9 @@
     return (0, first), (first, half - first)
 
 
-def columns_at(weight_ref, own, at, step):
+def columns_at(weight_ref, own, at, low, step):
+    if low is not None:
+        return weight_ref[:, at - low : at - low + step]
     half = weight_ref.shape[1] // 2
     which = core_here() if own else 1 - core_here()
     return weight_ref[:, pl.ds(pl.multiple_of(which * half + at, 128), step)]
@@ -349,18 +398,18 @@
     return [(at, min(STEP, width - at)) for at in range(0, width, STEP)]
 
 
-def send_block(rows_ref, means, weight_ref, start, sent_ref):
+def send_block(rows_ref, means, weight_ref, start, low, sent_ref):
     for at, step in steps_of(sent_ref.shape[1]):
-        weights = columns_at(weight_ref, False, start + at, step)
+        weights = columns_at(weight_ref, False, start + at, low, step)
         row, centred, columns = up_block(rows_ref[...], means, weights)
         high = columns.astype(BF16).astype(F32)
         tail = jnp.where(row == SLOTS, high, jnp.where(row == SLOTS + 1, columns - high, 0.0))
         sent_ref[:, at : at + step] = jnp.where(row < SLOTS, centred, tail).astype(BF16)
 
 
-def up_first_kernel(deep, start, *refs):
+def up_first_kernel(deep, start, low, *refs):
     if deep:
-        notes_ref, h0, h1, h2, h3, weight_ref, rows_ref, stats_ref, sent_ref = refs
+        notes_ref, h0, h1, h3, h2, weight_ref, rows_ref, stats_ref, sent_ref = refs
     else:
         h0, h1, h2, h3, weight_ref, rows_ref, stats_ref, sent_ref, notes_ref = refs
     held = jnp.concatenate([h0[...], h1[...], h2[...], h3[...]], axis=0)
@@ -377,16 +426,17 @@
     total = jnp.sum(wide, axis=1, keepdims=True)
     square = jnp.sum(wide * wide, axis=1, keepdims=True)
     stats_ref[...] = jnp.where(lane == 0, total, jnp.where(lane == 1, square, 0.0))
-    send_block(rows_ref, total / features, weight_ref, start, sent_ref)
-
-
-def up_first(deep, cut, notes, held, weights):
+    send_block(rows_ref, total / features, weight_ref, start, low, sent_ref)
+
+
+def up_first(deep, cut, low, notes, held, weights):
     features = weights.shape[0]
     start, width = cut
-    operands = ([notes] if deep else []) + list(held)
+    turn = (0, 1, 3, 2) if deep else (0, 1, 2, 3)
+    operands = ([notes] if deep else []) + [held[k] for k in turn]
     note = jax.ShapeDtypeStruct((TALL, META), F32)
     out = pl.pallas_call(
-        functools.partial(up_first_kernel, deep, start),
+        functools.partial(up_first_kernel, deep, start, low),
         in_specs=[VM] * (len(operands) + 1),
         out_specs=[VM] * (3 if deep else 4),
         out_shape=[
@@ -402,17 +452,17 @@
     return out if not deep else [*out, notes]
 
 
-def up_other_kernel(start, rows_ref, stats_ref, weight_ref, *sent):
+def up_other_kernel(start, low, rows_ref, stats_ref, weight_ref, *sent):
     for sent_ref in sent:
-        send_block(rows_ref, stats_ref[:, 0:1] / rows_ref.shape[1], weight_ref, start, sent_ref)
+        send_block(rows_ref, stats_ref[:, 0:1] / rows_ref.shape[1], weight_ref, start, low, sent_ref)
         start += sent_ref.shape[1]
 
 
-def up_other(rows, stats, weights, cut):
+def up_other(rows, stats, weights, cut, low):
     start, width = cut
     features = weights.shape[0]
     return pl.pallas_call(
-        functools.partial(up_other_kernel, start),
+        functools.partial(up_other_kernel, start, low),
         in_specs=[VM] * 3,
         out_specs=[VM] * 2,
         out_shape=[jax.ShapeDtypeStruct((TALL, width // 2), BF16)] * 2,
@@ -422,22 +472,22 @@
     )(rows, stats, weights)
 
 
-def up_second_kernel(start, rows_ref, stats_ref, weight_ref, kept_ref):
+def up_second_kernel(start, low, rows_ref, stats_ref, weight_ref, kept_ref):
     features = weight_ref.shape[0]
     means = stats_ref[:, 0:1] / features
     for at, step in steps_of(kept_ref.shape[1]):
-        weights = columns_at(weight_ref, True, start + at, step)
+        weights = columns_at(weight_ref, True, start + at, low, step)
         row, centred, columns = up_block(rows_ref[...], means, weights)
         kept_ref[:, at : at + step] = jnp.where(
             row < SLOTS, centred, jnp.where(row == SLOTS, columns, 0.0)
         )
 
 
-def up_second(rows, stats, weights, cut):
+def up_second(rows, stats, weights, cut, low):
     start, width = cut
     features = weights.shape[0]
     return pl.pallas_call(
-        functools.partial(up_second_kernel, start),
+        functools.partial(up_second_kernel, start, low),
         in_specs=[VM] * 3,
         out_specs=VM,
         out_shape=jax.ShapeDtypeStruct((TALL, width), F32),
@@ -501,14 +551,14 @@
 
 
 def up_merge_kernel(
-    start, rows_ref, stats_ref, got_stats_ref, weight_ref, got0, got1, sent_ref, sum_ref
+    start, low, rows_ref, stats_ref, got_stats_ref, weight_ref, got0, got1, sent_ref, sum_ref
 ):
     features = weight_ref.shape[0]
     stats = stats_ref[...]
     means = stats[:, 0:1] / features
 
     def source(at, step):
-        weights = columns_at(weight_ref, True, start + at, step)
+        weights = columns_at(weight_ref, True, start + at, low, step)
         row, centred, columns = up_block(rows_ref[...], means, weights)
         return jnp.where(row < SLOTS, centred, jnp.where(row == SLOTS, columns, 0.0))
 
@@ -516,11 +566,11 @@
     merge_into(features, source, sum_ref.shape[1], got, stats, got_stats_ref[...], sum_ref, sent_ref)
 
 
-def up_merge(rows, stats, got_stats, weights, got, cut):
+def up_merge(rows, stats, got_stats, weights, got, cut, low):
     start, width = cut
     features = weights.shape[0]
     return pl.pallas_call(
-        functools.partial(up_merge_kernel, start),
+        functools.partial(up_merge_kernel, start, low),
         in_specs=[VM] * 6,
         out_specs=[VM] * 2,
         out_shape=[
@@ -657,8 +707,9 @@
     return lax.ppermute(value, axis, [(i, i ^ apart) for i in range(count)])
 
 
-def swap_all(blocks):
-    return [blocks[0]] + [swap(blocks[k], "ep", k) for k in (1, 2, 3)]
+def swap_all(blocks, order=(1, 2, 3)):
+    got = {k: swap(blocks[k], "ep", k) for k in order}
+    return [blocks[0]] + [got[k] for k in (1, 2, 3)]
 
 
 def after(value, earlier):
@@ -666,16 +717,18 @@
 
 
 def expert_block(deep, notes, held, up, down):
-    features, width = up.shape
-    first, second = cuts_of(width // 2)
-    rows, stats, sent_a, notes = up_first(deep, first, notes, held, up)
+    up_first_piece, up_other_piece, up_own = up
+    features = up_own.shape[0]
+    first, second = cuts_of(down.shape[0] // 2)
+    low = (None, None) if deep else (0, second[0])
+    rows, stats, sent_a, notes = up_first(deep, first, low[0], notes, held, up_first_piece)
     got_a, got_stats = swap(sent_a, "tp", 1), swap(stats, "tp", 1)
-    kept = up_second(rows, stats, up, first)
+    kept = up_second(rows, stats, up_own, first, low[0])
     sent_a, total_a, sums = merge(features, kept, got_a, stats, got_stats)
     over_a = swap(sent_a, "tp", 2)
     later = after(rows, sent_a)
-    got_b = [swap(sent, "tp", 1) for sent in up_other(later, stats, up, second)]
-    sent_b, total_b = up_merge(later, stats, got_stats, up, got_b, second)
+    got_b = [swap(sent, "tp", 1) for sent in up_other(later, stats, up_other_piece, second, low[1])]
+    sent_b, total_b = up_merge(later, stats, got_stats, up_own, got_b, second, low[0])
     over_b = swap(sent_b, "tp", 2)
     hidden_a = hidden_units(features, after(total_a, sent_b), sums, over_a, over_a, 2)
     other_a = [swap(hidden, "tp", 1) for hidden in hidden_a]
@@ -705,7 +758,8 @@
     deep_down,
 ):
     rows = resid.shape[0]
-    *blocks, home = attend(
+    width = cuts_of(shallow_down.shape[0] // 2)[0][1]
+    *blocks, home, piece = attend(
         (
             resid,
             query,
@@ -719,10 +773,16 @@
             deep_expert.reshape(1, rows),
             deep_gate.reshape(1, rows),
         ),
-    )
-    weights = load(shallow_up, blocks[0])
+        shallow_up,
+        width,
+    )
+    others, own = load_rest(shallow_up, blocks[0], width)
+    piece = after(piece, own)
+    weights = (piece, others, own)
     notes, (between,) = expert_block(False, None, swap_all(blocks), weights, shallow_down)
-    _, blocks = expert_block(True, notes, swap_all([between] * EXPERTS), load(deep_up, between), deep_down)
+    weights = (load(deep_up, between),) * 3
+    held = swap_all([between] * EXPERTS, (1, 3, 2))
+    _, blocks = expert_block(True, notes, held, weights, deep_down)
     return finish(home, swap_all(blocks))
 
 

time: 70.6 us -> 69.8 us (0.989)
  starting transfers between devices: 22.5 us -> 21.5 us
  waiting for transfers between devices: 16.6 us -> 17.6 us
  Pallas kernels: 31 us -> 30.2 us
    pallas_call x2 -> x1, Pallas kernels: 11.8 us -> 5.89 us  [load(): pl.pallas_call(load_kernel, in_specs=[HB, pl.BlockSpec(memory_space=pl.AN...]
    pallas_call x9 -> x10, Pallas kernels: 9.56 us -> 14.6 us  [the longest x1 4.68 us: load_rest(): pl.pallas_call(functools.partial(load_rest_kernel, first), in_specs=[HB,...]
    ppermute x27, waiting for transfers between devices: 16.6 us -> 17.6 us  [swap(): return lax.ppermute(value, axis, [(i, i ^ apart) for i in range(count)])]
    ppermute x27, starting transfers between devices: 22.5 us -> 21.5 us  [swap(): return lax.ppermute(value, axis, [(i, i ^ apart) for i in range(count)])]
  transfers between devices with their start and end apart: 27 -> 27, of which waited for: 15 -> 17; matrix products, arithmetic and copies ran while one was open for 0% -> 0% of each run, Pallas kernels for 33% -> 31%
where the time goes in v5:
time: 69.8 us; the launch traced here: 69.7 us
  Pallas kernels  30.2 us (43%)
  starting transfers between devices  21.5 us (31%)
  waiting for transfers between devices  17.6 us (25%)
    ppermute x27, starting transfers between devices, swap(): return lax.ppermute(value, axis, [(i, i ^ apart) for i in range(count)])  21.5 us
    ppermute x27, waiting for transfers between devices, swap(): return lax.ppermute(value, axis, [(i, i ^ apart) for i in range(count)])  17.6 us
    pallas_call x1, Pallas kernels, load(): pl.pallas_call(load_kernel, in_specs=[HB, pl.BlockSpec(memory_space=pl.AN...  5.89 us
    pallas_call x6, Pallas kernels, down_part(): pl.pallas_call(functools.partial(down_part_kernel, own, cut[0], len(hidde...  5.4 us
    pallas_call x1, Pallas kernels, load_rest(): pl.pallas_call(functools.partial(load_rest_kernel, first), in_specs=[HB,...  4.68 us
    pallas_call x1, Pallas kernels, attend(): pl.pallas_call(attend_kernel, in_specs=[HB] * (len(arrays) + 1), out_spec...  2.92 us
    pallas_call x2, Pallas kernels, up_first(): pl.pallas_call(functools.partial(up_first_kernel, deep, start, low), in_s...  1.98 us
    pallas_call x2, Pallas kernels, up_second(): pl.pallas_call(functools.partial(up_second_kernel, start, low), in_specs=...  1.94 us
  transfers between devices with their start and end apart: 27, of which 17 were waited for; matrix products, arithmetic and copies ran while one was open for 0% of the time, Pallas kernels for 31%

profile of v5, /device:TPU:0, one launch (start us, length us, event | category | flops | bytes accessed | tf_op | source)
XLA Modules:
  0.0 69.7 jit_solution(8098989876452053571)
XLA Ops:
  0.0 2.9 %attend.1 = (bf16[16,1024]{1,0:T(8,128)(2,1)S(1)}, bf16[16,1024]{1,0:T(8,128)(2,1)S(1)}, bf16[16,1024]{1,0:T(8,128)(2,1)S(1)}, bf16[16,1024]{1,0:T(8,128)(2,1)S(...) custom-call(bf16[32,1024]{1,0:T(8,128)(2,1)} %resid_in.1, bf16[32,1024]{1,0:T(8,128)(2,1)} %query_in.1, ...), custom_call_target="tpu_custom_call" | custom-call | tf_op jit(solution)/shard_map/attend/pallas_call | solution.py:270
  2.9 3.1 %collective-permute-start = (bf16[16,1024]{1,0:T(8,128)(2,1)S(1)}, bf16[16,1024]{1,0:T(8,128)(2,1)S(1)}, u32[]{:S(2)}, u32[]{:S(2)}) collective-permute-start(bf16[16,1024]{1,0:T(8,128)(2,1)S(1)} %get-tuple-element.51), channel_id=1, source_target_pairs={{0,4},{4,0},{8,12},{12,8},{1,5},{5,1},{9,13},{13,9},{2,6},{6,2},{1... | collective-permute-start | bytes 98312 | tf_op jit(solution)/shard_map/ppermute | solution.py:707
  6.0 2.6 %collective-permute-start.1 = (bf16[16,1024]{1,0:T(8,128)(2,1)S(1)}, bf16[16,1024]{1,0:T(8,128)(2,1)S(1)}, u32[]{:S(2)}, u32[]{:S(2)}) collective-permute-start(bf16[16,1024]{1,0:T(8,128)(2,1)S(1)} %get-tuple-element.52), channel_id=1, source_target_pairs={{0,8},{4,12},{8,0},{12,4},{1,9},{5,13},{9,1},{13,5},{2,10},{6,14},... | collective-permute-start | bytes 98312 | tf_op jit(solution)/shard_map/ppermute | solution.py:707
  8.6 4.7 %load_rest.1 = (bf16[1024,1792]{1,0:T(8,128)(2,1)S(1)}, bf16[1024,4096]{1,0:T(8,128)(2,1)S(1)}) custom-call(bf16[1024,8192]{1,0:T(8,128)(2,1)} %weight_ref.10, bf16[16,1024]{1,0:T(8,128)(2,1)S(1)} %get-tuple-element.50.after_ref.refs_0_), custom_call_target="tpu_custom_call" | custom-call | bytes 16777216 | tf_op jit(solution)/shard_map/load_rest/pallas_call | solution.py:336
  13.3 1.0 %collective-permute-done.2.refs_3_ = bf16[16,1024]{1,0:T(8,128)(2,1)S(1)} collective-permute-done((bf16[16,1024]{1,0:T(8,128)(2,1)S(1)}, bf16[16,1024]{1,0:T(8,128)(2,1)S(1)}, u32[]{:S(2)}, u32[]{:S(2)}) %collective-permute-start.2) | collective-permute-done | bytes 32800 | tf_op jit(solution)/shard_map/ppermute | solution.py:707
  14.3 0.9 %up_first.2 = (bf16[56,1024]{1,0:T(8,128)(2,1)S(1)}, f32[56,128]{1,0:T(8,128)S(1)}, bf16[56,2304]{1,0:T(8,128)(2,1)S(1)}, f32[56,128]{1,0:T(8,128)S(1)}) custom-call(bf16[16,1024]{1,0:T(8,128)(2,1)S(1)} %get-tuple-element.50.after_ref.refs_0_, bf16[16,1024]{1,0:T(8,128)(2,1)S(1)} %collective-permute-done.refs_1_, ...), custom_call_target="tpu_custom_call" | custom-call | flops 264241152 | bytes 4718592 | tf_op jit(solution)/shard_map/up_first/pallas_call | solution.py:438
  15.8 1.0 %up_second.2.kept_ref = f32[56,2304]{1,0:T(8,128)S(1)} custom-call(bf16[56,1024]{1,0:T(8,128)(2,1)S(1)} %get-tuple-element.62.rows_ref, f32[56,128]{1,0:T(8,128)S(1)} %get-tuple-element.59.stats_ref, bf16[1024,4096]{1,0:T(8,128)(2,1)S(1)} %get-tuple-element.55.weight_ref), custom_call_target="tpu_custom_call" | custom-call | flops 264241152 | bytes 4718592 | tf_op jit(solution)/shard_map/up_second/pallas_call | solution.py:489
  17.0 1.6 %collective-permute-start.7 = (bf16[48,2560]{1,0:T(8,128)(2,1)S(1)}, bf16[48,2560]{1,0:T(8,128)(2,1)S(1)}, u32[]{:S(2)}, u32[]{:S(2)}) collective-permute-start(bf16[48,2560]{1,0:T(8,128)(2,1)S(1)} %get-tuple-element.61), channel_id=1, source_target_pairs={{0,2},{1,3},{2,0},{3,1},{4,6},{5,7},{6,4},{7,5},{8,10},{9,11},{10,... | collective-permute-start | bytes 737288 | tf_op jit(solution)/shard_map/ppermute | solution.py:707
  19.9 0.8 %collective-permute-done.5.got0 = bf16[56,896]{1,0:T(8,128)(2,1)S(1)} collective-permute-done((bf16[56,896]{1,0:T(8,128)(2,1)S(1)}, bf16[56,896]{1,0:T(8,128)(2,1)S(1)}, u32[]{:S(2)}, u32[]{:S(2)}) %collective-permute-start.5) | collective-permute-done | bytes 100384 | tf_op jit(solution)/shard_map/ppermute | solution.py:707
  20.9 0.8 %up_merge.2 = (bf16[48,1920]{1,0:T(8,128)(2,1)S(1)}, f32[56,1792]{1,0:T(8,128)S(1)}) custom-call(bf16[56,1024]{1,0:T(8,128)(2,1)S(1)} %get-tuple-element.62.rows_ref, f32[56,128]{1,0:T(8,128)S(1)} %get-tuple-element.59.stats_ref, f32[56,128]{1,0:T(8,128)S(1)} %collective-permute-done.4.got_stats_ref, bf16[1024,4096]{1,0:T(8,128)(2,1)S(1)} %get-tuple-element.55.weight_ref, ...), custom_call_target="tpu_custom_call" | custom-call | flops 205520896 | bytes 3670016 | tf_op jit(solution)/shard_map/up_merge/pallas_call | solution.py:572
  22.3 3.2 %collective-permute-done.7.got_ref.packed_ref = bf16[48,2560]{1,0:T(8,128)(2,1)S(1)} collective-permute-done((bf16[48,2560]{1,0:T(8,128)(2,1)S(1)}, bf16[48,2560]{1,0:T(8,128)(2,1)S(1)}, u32[]{:S(2)}, u32[]{:S(2)}) %collective-permute-start.7) | collective-permute-done | bytes 245792 | tf_op jit(solution)/shard_map/ppermute | solution.py:707
  26.4 0.9 %down_part.6.refs_2_ = f32[48,1024]{1,0:T(8,128)S(1)} custom-call(bf16[8192,1024]{1,0:T(8,128)(2,1)S(1)} %bitcast.6, bf16[48,1152]{1,0:T(8,128)(2,1)S(1)} %get-tuple-element.71.refs_0_, bf16[48,1152]{1,0:T(8,128)(2,1)S(1)} %get-tuple-element.72.refs_1_), custom_call_target="tpu_custom_call" | custom-call | flops 1 | bytes 1 | tf_op jit(solution)/shard_map/down_part/pallas_call | solution.py:643
  27.4 1.0 %down_part.7.refs_1_ = f32[48,1024]{1,0:T(8,128)S(1)} custom-call(bf16[8192,1024]{1,0:T(8,128)(2,1)S(1)} %bitcast.6, bf16[48,1152]{1,0:T(8,128)(2,1)S(1)} %collective-permute-done.8.refs_0_, bf16[48,1152]{1,0:T(8,128)(2,1)S(1)} %collective-permute-done.9.refs_1_, f32[48,1024]{1,0:T(8,128)S(1)} %down_part.6.refs_2_), custom_call_target="tpu_custom_call" | custom-call | flops 1 | bytes 1 | tf_op jit(solution)/shard_map/down_part/pallas_call | solution.py:643
  31.6 1.0 %collective-permute-start.14 = (bf16[48,1024]{1,0:T(8,128)(2,1)S(1)}, bf16[48,1024]{1,0:T(8,128)(2,1)S(1)}, u32[]{:S(2)}, u32[]{:S(2)}) collective-permute-start(bf16[48,1024]{1,0:T(8,128)(2,1)S(1)} %down_last.2.after_ref.refs_1_), channel_id=1, source_target_pairs={{0,8},{4,12},{8,0},{12,4},{1,9},{5,13},{9,1},{13,5},{2,10},{6,14},... | collective-permute-start | bytes 294920 | tf_op jit(solution)/shard_map/ppermute | solution.py:707
  32.6 2.0 %collective-permute-start.13 = (bf16[48,1024]{1,0:T(8,128)(2,1)S(1)}, bf16[48,1024]{1,0:T(8,128)(2,1)S(1)}, u32[]{:S(2)}, u32[]{:S(2)}) collective-permute-start(bf16[48,1024]{1,0:T(8,128)(2,1)S(1)} %down_last.2.after_ref.refs_1_), channel_id=1, source_target_pairs={{0,12},{4,8},{8,4},{12,0},{1,13},{5,9},{9,5},{13,1},{2,14},{6,10},... | collective-permute-start | bytes 294920 | tf_op jit(solution)/shard_map/ppermute | solution.py:707
  35.2 5.9 %load.1.refs_5_.weight_ref = bf16[1024,8192]{1,0:T(8,128)(2,1)S(1)} custom-call(bf16[1024,8192]{1,0:T(8,128)(2,1)} %weight_ref.15, bf16[48,1024]{1,0:T(8,128)(2,1)S(1)} %down_last.2.after_ref.refs_1_), custom_call_target="tpu_custom_call" | custom-call | bytes 16777216 | tf_op jit(solution)/shard_map/load/pallas_call | solution.py:301
  41.1 0.9 %collective-permute-done.14.refs_4_ = bf16[48,1024]{1,0:T(8,128)(2,1)S(1)} collective-permute-done((bf16[48,1024]{1,0:T(8,128)(2,1)S(1)}, bf16[48,1024]{1,0:T(8,128)(2,1)S(1)}, u32[]{:S(2)}, u32[]{:S(2)}) %collective-permute-start.14) | collective-permute-done | bytes 98336 | tf_op jit(solution)/shard_map/ppermute | solution.py:707
  42.0 1.1 %collective-permute-done.12.refs_2_ = bf16[48,1024]{1,0:T(8,128)(2,1)S(1)} collective-permute-done((bf16[48,1024]{1,0:T(8,128)(2,1)S(1)}, bf16[48,1024]{1,0:T(8,128)(2,1)S(1)}, u32[]{:S(2)}, u32[]{:S(2)}) %collective-permute-start.12) | collective-permute-done | bytes 98336 | tf_op jit(solution)/shard_map/ppermute | solution.py:707
  43.1 1.1 %up_first.3 = (bf16[56,1024]{1,0:T(8,128)(2,1)S(1)}, f32[56,128]{1,0:T(8,128)S(1)}, bf16[56,2304]{1,0:T(8,128)(2,1)S(1)}) custom-call(f32[56,128]{1,0:T(8,128)S(1)} %get-tuple-element.57.notes_ref.refs_0_, bf16[48,1024]{1,0:T(8,128)(2,1)S(1)} %down_last.2.after_ref.refs_1_, bf16[48,1024]{1,0:T(8,128)(2,1)S(1)} %collective-permute-done.12.refs_2_, ...), custom_call_target="tpu_custom_call" | custom-call | flops 264241152 | bytes 4718592 | tf_op jit(solution)/shard_map/up_first/pallas_call | solution.py:438
  44.7 1.0 %up_second.3.kept_ref = f32[56,2304]{1,0:T(8,128)S(1)} custom-call(bf16[56,1024]{1,0:T(8,128)(2,1)S(1)} %get-tuple-element.78.rows_ref, f32[56,128]{1,0:T(8,128)S(1)} %get-tuple-element.75.stats_ref, bf16[1024,8192]{1,0:T(8,128)(2,1)S(1)} %load.1.refs_5_.weight_ref), custom_call_target="tpu_custom_call" | custom-call | flops 264241152 | bytes 4718592 | tf_op jit(solution)/shard_map/up_second/pallas_call | solution.py:489
  46.0 1.6 %collective-permute-start.19 = (bf16[48,2560]{1,0:T(8,128)(2,1)S(1)}, bf16[48,2560]{1,0:T(8,128)(2,1)S(1)}, u32[]{:S(2)}, u32[]{:S(2)}) collective-permute-start(bf16[48,2560]{1,0:T(8,128)(2,1)S(1)} %get-tuple-element.77), channel_id=1, source_target_pairs={{0,2},{1,3},{2,0},{3,1},{4,6},{5,7},{6,4},{7,5},{8,10},{9,11},{10,... | collective-permute-start | bytes 737288 | tf_op jit(solution)/shard_map/ppermute | solution.py:707
  48.9 0.8 %collective-permute-done.17.got0 = bf16[56,896]{1,0:T(8,128)(2,1)S(1)} collective-permute-done((bf16[56,896]{1,0:T(8,128)(2,1)S(1)}, bf16[56,896]{1,0:T(8,128)(2,1)S(1)}, u32[]{:S(2)}, u32[]{:S(2)}) %collective-permute-start.17) | collective-permute-done | bytes 100384 | tf_op jit(solution)/shard_map/ppermute | solution.py:707
  51.2 3.1 %collective-permute-done.19.got_ref.packed_ref = bf16[48,2560]{1,0:T(8,128)(2,1)S(1)} collective-permute-done((bf16[48,2560]{1,0:T(8,128)(2,1)S(1)}, bf16[48,2560]{1,0:T(8,128)(2,1)S(1)}, u32[]{:S(2)}, u32[]{:S(2)}) %collective-permute-start.19) | collective-permute-done | bytes 245792 | tf_op jit(solution)/shard_map/ppermute | solution.py:707
  55.4 1.1 %down_part.9.refs_2_ = f32[48,1024]{1,0:T(8,128)S(1)} custom-call(bf16[8192,1024]{1,0:T(8,128)(2,1)S(1)} %bitcast.8, bf16[48,1152]{1,0:T(8,128)(2,1)S(1)} %get-tuple-element.86.refs_0_, bf16[48,1152]{1,0:T(8,128)(2,1)S(1)} %get-tuple-element.87.refs_1_), custom_call_target="tpu_custom_call" | custom-call | flops 1 | bytes 1 | tf_op jit(solution)/shard_map/down_part/pallas_call | solution.py:643
  56.5 0.9 %down_part.10.refs_1_ = f32[48,1024]{1,0:T(8,128)S(1)} custom-call(bf16[8192,1024]{1,0:T(8,128)(2,1)S(1)} %bitcast.8, bf16[48,1152]{1,0:T(8,128)(2,1)S(1)} %collective-permute-done.20.refs_0_, bf16[48,1152]{1,0:T(8,128)(2,1)S(1)} %collective-permute-done.21.refs_1_, f32[48,1024]{1,0:T(8,128)S(1)} %down_part.9.refs_2_), custom_call_target="tpu_custom_call" | custom-call | flops 1 | bytes 1 | tf_op jit(solution)/shard_map/down_part/pallas_call | solution.py:643
  59.8 0.9 %down_last.3 = (bf16[16,1024]{1,0:T(8,128)(2,1)S(1)}, bf16[16,1024]{1,0:T(8,128)(2,1)S(1)}, bf16[16,1024]{1,0:T(8,128)(2,1)S(1)}, bf16[16,1024]{1,0:T(8,128)(2,1)S(1)}) custom-call(f32[48,1024]{1,0:T(8,128)S(1)} %down_part.11.part_ref, bf16[56,1024]{1,0:T(8,128)(2,1)S(1)} %get-tuple-element.78.rows_ref, f32[56,128]{1,0:T(8,128)S(1)} %get-tuple-element.57.notes_ref.refs_0_, ...), custom_call_target="tpu_custom_call" | custom-call | flops 176160768 | bytes 3670016 | tf_op jit(solution)/shard_map/down_last/pallas_call | solution.py:676
  60.7 1.3 %collective-permute-start.24 = (bf16[16,1024]{1,0:T(8,128)(2,1)S(1)}, bf16[16,1024]{1,0:T(8,128)(2,1)S(1)}, u32[]{:S(2)}, u32[]{:S(2)}) collective-permute-start(bf16[16,1024]{1,0:T(8,128)(2,1)S(1)} %get-tuple-element.90), channel_id=1, source_target_pairs={{0,4},{4,0},{8,12},{12,8},{1,5},{5,1},{9,13},{13,9},{2,6},{6,2},{1... | collective-permute-start | bytes 98312 | tf_op jit(solution)/shard_map/ppermute | solution.py:707
  62.1 1.1 %collective-permute-start.25 = (bf16[16,1024]{1,0:T(8,128)(2,1)S(1)}, bf16[16,1024]{1,0:T(8,128)(2,1)S(1)}, u32[]{:S(2)}, u32[]{:S(2)}) collective-permute-start(bf16[16,1024]{1,0:T(8,128)(2,1)S(1)} %get-tuple-element.91), channel_id=1, source_target_pairs={{0,8},{4,12},{8,0},{12,4},{1,9},{5,13},{9,1},{13,5},{2,10},{6,14},... | collective-permute-start | bytes 98312 | tf_op jit(solution)/shard_map/ppermute | solution.py:707
  63.1 2.0 %collective-permute-start.26 = (bf16[16,1024]{1,0:T(8,128)(2,1)S(1)}, bf16[16,1024]{1,0:T(8,128)(2,1)S(1)}, u32[]{:S(2)}, u32[]{:S(2)}) collective-permute-start(bf16[16,1024]{1,0:T(8,128)(2,1)S(1)} %get-tuple-element.92), channel_id=1, source_target_pairs={{0,12},{4,8},{8,4},{12,0},{1,13},{5,9},{9,5},{13,1},{2,14},{6,10},... | collective-permute-start | bytes 98312 | tf_op jit(solution)/shard_map/ppermute | solution.py:707
  65.2 2.4 %collective-permute-done.25.g2 = bf16[16,1024]{1,0:T(8,128)(2,1)S(1)} collective-permute-done((bf16[16,1024]{1,0:T(8,128)(2,1)S(1)}, bf16[16,1024]{1,0:T(8,128)(2,1)S(1)}, u32[]{:S(2)}, u32[]{:S(2)}) %collective-permute-start.25) | collective-permute-done | bytes 32800 | tf_op jit(solution)/shard_map/ppermute | solution.py:707
  67.6 1.3 %collective-permute-done.26.g3 = bf16[16,1024]{1,0:T(8,128)(2,1)S(1)} collective-permute-done((bf16[16,1024]{1,0:T(8,128)(2,1)S(1)}, bf16[16,1024]{1,0:T(8,128)(2,1)S(1)}, u32[]{:S(2)}, u32[]{:S(2)}) %collective-permute-start.26) | collective-permute-done | bytes 32800 | tf_op jit(solution)/shard_map/ppermute | solution.py:707
  68.9 0.8 %finish.1 = bf16[32,1024]{1,0:T(8,128)(2,1)} custom-call(s32[32,128]{1,0:T(8,128)S(1)} %get-tuple-element.49.home_ref, bf16[16,1024]{1,0:T(8,128)(2,1)S(1)} %get-tuple-element.89.g0, bf16[16,1024]{1,0:T(8,128)(2,1)S(1)} %collective-permute-done.24.g1, bf16[16,1024]{1,0:T(8,128)(2,1)S(1)} %collective-permute-done.25.g2, ...), custom_call_target="tpu_custom_call" | custom-call | tf_op jit(solution)/shard_map/finish/pallas_call | solution.py:695
  (66 shorter events, 14.7 us)
Async XLA Ops:
  2.9 10.4 %collective-permute-start = (bf16[16,1024]{1,0:T(8,128)(2,1)S(1)}, bf16[16,1024]{1,0:T(8,128)(2,1)S(1)}, u32[]{:S(2)}, u32[]{:S(2)}) collective-permute-start(bf16[16,1024]{1,0:T(8,128)(2,1)S(1)} %get-tuple-element.51), channel_id=1, source_target_pairs={{0,4},{4,0},{8,12},{12,8},{1,5},{5,1},{9,13},{13,9},{2,6},{6,2},{1... | collective-permute-start | bytes 98312 | tf_op jit(solution)/shard_map/ppermute | solution.py:707
  6.0 7.3 %collective-permute-start.1 = (bf16[16,1024]{1,0:T(8,128)(2,1)S(1)}, bf16[16,1024]{1,0:T(8,128)(2,1)S(1)}, u32[]{:S(2)}, u32[]{:S(2)}) collective-permute-start(bf16[16,1024]{1,0:T(8,128)(2,1)S(1)} %get-tuple-element.52), channel_id=1, source_target_pairs={{0,8},{4,12},{8,0},{12,4},{1,9},{5,13},{9,1},{13,5},{2,10},{6,14},... | collective-permute-start | bytes 98312 | tf_op jit(solution)/shard_map/ppermute | solution.py:707
  8.6 5.7 %collective-permute-start.2 = (bf16[16,1024]{1,0:T(8,128)(2,1)S(1)}, bf16[16,1024]{1,0:T(8,128)(2,1)S(1)}, u32[]{:S(2)}, u32[]{:S(2)}) collective-permute-start(bf16[16,1024]{1,0:T(8,128)(2,1)S(1)} %get-tuple-element.53), channel_id=1, source_target_pairs={{0,12},{4,8},{8,4},{12,0},{1,13},{5,9},{9,5},{13,1},{2,14},{6,10},... | collective-permute-start | bytes 98312 | tf_op jit(solution)/shard_map/ppermute | solution.py:707
  8.6 17.8 %slice-start = ((s8[16777216]{0:T(1024)(128)(4,1)}), s8[4194304]{0:T(1024)(128)(4,1)S(1)}, s32[]{:S(2)}) async-start(s8[16777216]{0:T(1024)(128)(4,1)} %bitcast.5), calls=%async_computation | async-start | bytes 8388608
  8.6 17.8 %slice-start.1 = ((s8[16777216]{0:T(1024)(128)(4,1)}), s8[4194304]{0:T(1024)(128)(4,1)S(1)}, s32[]{:S(2)}) async-start(s8[16777216]{0:T(1024)(128)(4,1)} %bitcast.5), calls=%async_computation.1 | async-start | bytes 8388608
  15.2 1.6 %collective-permute-start.3 = (bf16[56,2304]{1,0:T(8,128)(2,1)S(1)}, bf16[56,2304]{1,0:T(8,128)(2,1)S(1)}, u32[]{:S(2)}, u32[]{:S(2)}) collective-permute-start(bf16[56,2304]{1,0:T(8,128)(2,1)S(1)} %get-tuple-element.60), channel_id=1, source_target_pairs={{0,1},{1,0},{2,3},{3,2},{4,5},{5,4},{6,7},{7,6},{8,9},{9,8},{10,11... | collective-permute-start | bytes 774152 | tf_op jit(solution)/shard_map/ppermute | solution.py:707
  15.3 1.6 %collective-permute-start.4 = (f32[56,128]{1,0:T(8,128)S(1)}, f32[56,128]{1,0:T(8,128)S(1)}, u32[]{:S(2)}, u32[]{:S(2)}) collective-permute-start(f32[56,128]{1,0:T(8,128)S(1)} %get-tuple-element.59.stats_ref), channel_id=1, source_target_pairs={{0,1},{1,0},{2,3},{3,2},{4,5},{5,4},{6,7},{7,6},{8,9},{9,8},{10,11... | collective-permute-start | bytes 86024 | tf_op jit(solution)/shard_map/ppermute | solution.py:707
  15.8 10.6 %slice-start.2 = ((s8[16777216]{0:T(1024)(128)(4,1)}), s8[4194304]{0:T(1024)(128)(4,1)S(1)}, s32[]{:S(2)}) async-start(s8[16777216]{0:T(1024)(128)(4,1)} %bitcast.5), calls=%async_computation.2 | async-start | bytes 8388608
  17.0 8.4 %collective-permute-start.7 = (bf16[48,2560]{1,0:T(8,128)(2,1)S(1)}, bf16[48,2560]{1,0:T(8,128)(2,1)S(1)}, u32[]{:S(2)}, u32[]{:S(2)}) collective-permute-start(bf16[48,2560]{1,0:T(8,128)(2,1)S(1)} %get-tuple-element.61), channel_id=1, source_target_pairs={{0,2},{1,3},{2,0},{3,1},{4,6},{5,7},{6,4},{7,5},{8,10},{9,11},{10,... | collective-permute-start | bytes 737288 | tf_op jit(solution)/shard_map/ppermute | solution.py:707
  19.3 1.4 %collective-permute-start.5 = (bf16[56,896]{1,0:T(8,128)(2,1)S(1)}, bf16[56,896]{1,0:T(8,128)(2,1)S(1)}, u32[]{:S(2)}, u32[]{:S(2)}) collective-permute-start(bf16[56,896]{1,0:T(8,128)(2,1)S(1)} %get-tuple-element.64), channel_id=1, source_target_pairs={{0,1},{1,0},{2,3},{3,2},{4,5},{5,4},{6,7},{7,6},{8,9},{9,8},{10,11... | collective-permute-start | bytes 301064 | tf_op jit(solution)/shard_map/ppermute | solution.py:707
  19.4 1.4 %collective-permute-start.6 = (bf16[56,896]{1,0:T(8,128)(2,1)S(1)}, bf16[56,896]{1,0:T(8,128)(2,1)S(1)}, u32[]{:S(2)}, u32[]{:S(2)}) collective-permute-start(bf16[56,896]{1,0:T(8,128)(2,1)S(1)} %get-tuple-element.65), channel_id=1, source_target_pairs={{0,1},{1,0},{2,3},{3,2},{4,5},{5,4},{6,7},{7,6},{8,9},{9,8},{10,11... | collective-permute-start | bytes 301064 | tf_op jit(solution)/shard_map/ppermute | solution.py:707
  21.7 7.4 %collective-permute-start.10 = (bf16[48,1920]{1,0:T(8,128)(2,1)S(1)}, bf16[48,1920]{1,0:T(8,128)(2,1)S(1)}, u32[]{:S(2)}, u32[]{:S(2)}) collective-permute-start(bf16[48,1920]{1,0:T(8,128)(2,1)S(1)} %get-tuple-element.68), channel_id=1, source_target_pairs={{0,2},{1,3},{2,0},{3,1},{4,6},{5,7},{6,4},{7,5},{8,10},{9,11},{10,... | collective-permute-start | bytes 552968 | tf_op jit(solution)/shard_map/ppermute | solution.py:707
  25.8 1.5 %collective-permute-start.8 = (bf16[48,1152]{1,0:T(8,128)(2,1)S(1)}, bf16[48,1152]{1,0:T(8,128)(2,1)S(1)}, u32[]{:S(2)}, u32[]{:S(2)}) collective-permute-start(bf16[48,1152]{1,0:T(8,128)(2,1)S(1)} %get-tuple-element.71.refs_0_), channel_id=1, source_target_pairs={{0,1},{1,0},{2,3},{3,2},{4,5},{5,4},{6,7},{7,6},{8,9},{9,8},{10,11... | collective-permute-start | bytes 331784 | tf_op jit(solution)/shard_map/ppermute | solution.py:707
  25.9 1.5 %collective-permute-start.9 = (bf16[48,1152]{1,0:T(8,128)(2,1)S(1)}, bf16[48,1152]{1,0:T(8,128)(2,1)S(1)}, u32[]{:S(2)}, u32[]{:S(2)}) collective-permute-start(bf16[48,1152]{1,0:T(8,128)(2,1)S(1)} %get-tuple-element.72.refs_1_), channel_id=1, source_target_pairs={{0,1},{1,0},{2,3},{3,2},{4,5},{5,4},{6,7},{7,6},{8,9},{9,8},{10,11... | collective-permute-start | bytes 331784 | tf_op jit(solution)/shard_map/ppermute | solution.py:707
  29.4 1.5 %collective-permute-start.11 = (bf16[48,1792]{1,0:T(8,128)(2,1)S(1)}, bf16[48,1792]{1,0:T(8,128)(2,1)S(1)}, u32[]{:S(2)}, u32[]{:S(2)}) collective-permute-start(bf16[48,1792]{1,0:T(8,128)(2,1)S(1)} %hidden.5.refs_0_), channel_id=1, source_target_pairs={{0,1},{1,0},{2,3},{3,2},{4,5},{5,4},{6,7},{7,6},{8,9},{9,8},{10,11... | collective-permute-start | bytes 516104 | tf_op jit(solution)/shard_map/ppermute | solution.py:707
  31.6 10.4 %collective-permute-start.14 = (bf16[48,1024]{1,0:T(8,128)(2,1)S(1)}, bf16[48,1024]{1,0:T(8,128)(2,1)S(1)}, u32[]{:S(2)}, u32[]{:S(2)}) collective-permute-start(bf16[48,1024]{1,0:T(8,128)(2,1)S(1)} %down_last.2.after_ref.refs_1_), channel_id=1, source_target_pairs={{0,8},{4,12},{8,0},{12,4},{1,9},{5,13},{9,1},{13,5},{2,10},{6,14},... | collective-permute-start | bytes 294920 | tf_op jit(solution)/shard_map/ppermute | solution.py:707
  32.6 9.4 %collective-permute-start.13 = (bf16[48,1024]{1,0:T(8,128)(2,1)S(1)}, bf16[48,1024]{1,0:T(8,128)(2,1)S(1)}, u32[]{:S(2)}, u32[]{:S(2)}) collective-permute-start(bf16[48,1024]{1,0:T(8,128)(2,1)S(1)} %down_last.2.after_ref.refs_1_), channel_id=1, source_target_pairs={{0,12},{4,8},{8,4},{12,0},{1,13},{5,9},{9,5},{13,1},{2,14},{6,10},... | collective-permute-start | bytes 294920 | tf_op jit(solution)/shard_map/ppermute | solution.py:707
  34.6 8.5 %collective-permute-start.12 = (bf16[48,1024]{1,0:T(8,128)(2,1)S(1)}, bf16[48,1024]{1,0:T(8,128)(2,1)S(1)}, u32[]{:S(2)}, u32[]{:S(2)}) collective-permute-start(bf16[48,1024]{1,0:T(8,128)(2,1)S(1)} %down_last.2.after_ref.refs_1_), channel_id=1, source_target_pairs={{0,4},{4,0},{8,12},{12,8},{1,5},{5,1},{9,13},{13,9},{2,6},{6,2},{1... | collective-permute-start | bytes 294920 | tf_op jit(solution)/shard_map/ppermute | solution.py:707
  44.2 1.6 %collective-permute-start.15 = (bf16[56,2304]{1,0:T(8,128)(2,1)S(1)}, bf16[56,2304]{1,0:T(8,128)(2,1)S(1)}, u32[]{:S(2)}, u32[]{:S(2)}) collective-permute-start(bf16[56,2304]{1,0:T(8,128)(2,1)S(1)} %get-tuple-element.76), channel_id=1, source_target_pairs={{0,1},{1,0},{2,3},{3,2},{4,5},{5,4},{6,7},{7,6},{8,9},{9,8},{10,11... | collective-permute-start | bytes 774152 | tf_op jit(solution)/shard_map/ppermute | solution.py:707
  44.2 1.6 %collective-permute-start.16 = (f32[56,128]{1,0:T(8,128)S(1)}, f32[56,128]{1,0:T(8,128)S(1)}, u32[]{:S(2)}, u32[]{:S(2)}) collective-permute-start(f32[56,128]{1,0:T(8,128)S(1)} %get-tuple-element.75.stats_ref), channel_id=1, source_target_pairs={{0,1},{1,0},{2,3},{3,2},{4,5},{5,4},{6,7},{7,6},{8,9},{9,8},{10,11... | collective-permute-start | bytes 86024 | tf_op jit(solution)/shard_map/ppermute | solution.py:707
  45.9 9.4 %slice-start.4 = ((s8[16777216]{0:T(1024)(128)(4,1)}), s8[4194304]{0:T(1024)(128)(4,1)S(1)}, s32[]{:S(2)}) async-start(s8[16777216]{0:T(1024)(128)(4,1)} %bitcast.7), calls=%async_computation.4 | async-start | bytes 8388608
  46.0 9.4 %slice-start.5 = ((s8[16777216]{0:T(1024)(128)(4,1)}), s8[4194304]{0:T(1024)(128)(4,1)S(1)}, s32[]{:S(2)}) async-start(s8[16777216]{0:T(1024)(128)(4,1)} %bitcast.7), calls=%async_computation.5 | async-start | bytes 8388608
  46.0 8.4 %collective-permute-start.19 = (bf16[48,2560]{1,0:T(8,128)(2,1)S(1)}, bf16[48,2560]{1,0:T(8,128)(2,1)S(1)}, u32[]{:S(2)}, u32[]{:S(2)}) collective-permute-start(bf16[48,2560]{1,0:T(8,128)(2,1)S(1)} %get-tuple-element.77), channel_id=1, source_target_pairs={{0,2},{1,3},{2,0},{3,1},{4,6},{5,7},{6,4},{7,5},{8,10},{9,11},{10,... | collective-permute-start | bytes 737288 | tf_op jit(solution)/shard_map/ppermute | solution.py:707
  48.3 1.4 %collective-permute-start.17 = (bf16[56,896]{1,0:T(8,128)(2,1)S(1)}, bf16[56,896]{1,0:T(8,128)(2,1)S(1)}, u32[]{:S(2)}, u32[]{:S(2)}) collective-permute-start(bf16[56,896]{1,0:T(8,128)(2,1)S(1)} %get-tuple-element.79), channel_id=1, source_target_pairs={{0,1},{1,0},{2,3},{3,2},{4,5},{5,4},{6,7},{7,6},{8,9},{9,8},{10,11... | collective-permute-start | bytes 301064 | tf_op jit(solution)/shard_map/ppermute | solution.py:707
  48.4 1.4 %collective-permute-start.18 = (bf16[56,896]{1,0:T(8,128)(2,1)S(1)}, bf16[56,896]{1,0:T(8,128)(2,1)S(1)}, u32[]{:S(2)}, u32[]{:S(2)}) collective-permute-start(bf16[56,896]{1,0:T(8,128)(2,1)S(1)} %get-tuple-element.80), channel_id=1, source_target_pairs={{0,1},{1,0},{2,3},{3,2},{4,5},{5,4},{6,7},{7,6},{8,9},{9,8},{10,11... | collective-permute-start | bytes 301064 | tf_op jit(solution)/shard_map/ppermute | solution.py:707
  50.6 7.4 %collective-permute-start.22 = (bf16[48,1920]{1,0:T(8,128)(2,1)S(1)}, bf16[48,1920]{1,0:T(8,128)(2,1)S(1)}, u32[]{:S(2)}, u32[]{:S(2)}) collective-permute-start(bf16[48,1920]{1,0:T(8,128)(2,1)S(1)} %get-tuple-element.83), channel_id=1, source_target_pairs={{0,2},{1,3},{2,0},{3,1},{4,6},{5,7},{6,4},{7,5},{8,10},{9,11},{10,... | collective-permute-start | bytes 552968 | tf_op jit(solution)/shard_map/ppermute | solution.py:707
  54.8 1.7 %collective-permute-start.20 = (bf16[48,1152]{1,0:T(8,128)(2,1)S(1)}, bf16[48,1152]{1,0:T(8,128)(2,1)S(1)}, u32[]{:S(2)}, u32[]{:S(2)}) collective-permute-start(bf16[48,1152]{1,0:T(8,128)(2,1)S(1)} %get-tuple-element.86.refs_0_), channel_id=1, source_target_pairs={{0,1},{1,0},{2,3},{3,2},{4,5},{5,4},{6,7},{7,6},{8,9},{9,8},{10,11... | collective-permute-start | bytes 331784 | tf_op jit(solution)/shard_map/ppermute | solution.py:707
  54.8 1.6 %collective-permute-start.21 = (bf16[48,1152]{1,0:T(8,128)(2,1)S(1)}, bf16[48,1152]{1,0:T(8,128)(2,1)S(1)}, u32[]{:S(2)}, u32[]{:S(2)}) collective-permute-start(bf16[48,1152]{1,0:T(8,128)(2,1)S(1)} %get-tuple-element.87.refs_1_), channel_id=1, source_target_pairs={{0,1},{1,0},{2,3},{3,2},{4,5},{5,4},{6,7},{7,6},{8,9},{9,8},{10,11... | collective-permute-start | bytes 331784 | tf_op jit(solution)/shard_map/ppermute | solution.py:707
  58.3 1.5 %collective-permute-start.23 = (bf16[48,1792]{1,0:T(8,128)(2,1)S(1)}, bf16[48,1792]{1,0:T(8,128)(2,1)S(1)}, u32[]{:S(2)}, u32[]{:S(2)}) collective-permute-start(bf16[48,1792]{1,0:T(8,128)(2,1)S(1)} %hidden.7.refs_0_), channel_id=1, source_target_pairs={{0,1},{1,0},{2,3},{3,2},{4,5},{5,4},{6,7},{7,6},{8,9},{9,8},{10,11... | collective-permute-start | bytes 516104 | tf_op jit(solution)/shard_map/ppermute | solution.py:707
  60.7 4.5 %collective-permute-start.24 = (bf16[16,1024]{1,0:T(8,128)(2,1)S(1)}, bf16[16,1024]{1,0:T(8,128)(2,1)S(1)}, u32[]{:S(2)}, u32[]{:S(2)}) collective-permute-start(bf16[16,1024]{1,0:T(8,128)(2,1)S(1)} %get-tuple-element.90), channel_id=1, source_target_pairs={{0,4},{4,0},{8,12},{12,8},{1,5},{5,1},{9,13},{13,9},{2,6},{6,2},{1... | collective-permute-start | bytes 98312 | tf_op jit(solution)/shard_map/ppermute | solution.py:707
  62.1 5.5 %collective-permute-start.25 = (bf16[16,1024]{1,0:T(8,128)(2,1)S(1)}, bf16[16,1024]{1,0:T(8,128)(2,1)S(1)}, u32[]{:S(2)}, u32[]{:S(2)}) collective-permute-start(bf16[16,1024]{1,0:T(8,128)(2,1)S(1)} %get-tuple-element.91), channel_id=1, source_target_pairs={{0,8},{4,12},{8,0},{12,4},{1,9},{5,13},{9,1},{13,5},{2,10},{6,14},... | collective-permute-start | bytes 98312 | tf_op jit(solution)/shard_map/ppermute | solution.py:707
  63.1 5.7 %collective-permute-start.26 = (bf16[16,1024]{1,0:T(8,128)(2,1)S(1)}, bf16[16,1024]{1,0:T(8,128)(2,1)S(1)}, u32[]{:S(2)}, u32[]{:S(2)}) collective-permute-start(bf16[16,1024]{1,0:T(8,128)(2,1)S(1)} %get-tuple-element.92), channel_id=1, source_target_pairs={{0,12},{4,8},{8,4},{12,0},{1,13},{5,9},{9,5},{13,1},{2,14},{6,10},... | collective-permute-start | bytes 98312 | tf_op jit(solution)/shard_map/ppermute | solution.py:707
  (3 other events, 21.8 us)
